TPU v7x, 32 devices: a whole 2x2x4 slice. The times are simulated.
32 devices in a mesh: rep: 2 (over x), adp: 16 (over z, y, core).
Axes of the slice: x: 2, y: 2, z: 4, core: 2. Of those that a mesh axis runs over, the one named last changes fastest.
Arguments:
- tokens: bfloat16 [768, 8192], P('rep', 'adp'), parts along dimension 0, may hold values from -6 to 6
- request_adapter: int32 [768, 1], P('rep'), parts along dimension 0, may hold values from 0 to 15
- adapter_storage_slot: int32 [16], replicated, may hold values from 0 to 15, each once
- cache_length: int32 [768], P(('rep', 'adp')), parts along dimension 0, may hold values from 2 to 128, as said below
- query_weight: bfloat16 [8192, 8192], P(None, 'adp'), may hold values from -0.0625 to 0.0625
- adapter_down_maps: bfloat16 [16, 8192, 64], P('adp'), may hold values from -0.0625 to 0.0625
- adapter_up_maps: bfloat16 [16, 8192, 64], P('adp'), may hold values from -0.75 to 0.75
- key_cache: bfloat16 [8, 768, 128, 128], P(None, ('rep', 'adp')), parts along dimension 1, may hold values from -250 to 250
- value_cache: bfloat16 [8, 768, 128, 128], P(None, ('rep', 'adp')), parts along dimension 1, may hold values from -6 to 6
- new_token_key: bfloat16 [768, 1024], P(('rep', 'adp')), parts along dimension 0, may hold values from -6 to 6
- new_token_value: bfloat16 [768, 1024], P(('rep', 'adp')), parts along dimension 0, may hold values from -6 to 6
- output_weight: bfloat16 [8192, 8192], P('adp'), may hold values from -0.09375 to 0.09375
Outputs:
- attn_out: bfloat16 [768, 8192], P('rep', 'adp'), parts along dimension 0
There are 2 independent parts, one for each index of `rep`. A program takes and returns all parts, laid end to end along the dimension named above; an argument that names none is the same for every part. Nothing has to cross between parts.
Inputs may be any that keep to these rules, and one draw needn't show every extreme that they name: `request_adapter`: every adapter is named by some request of a group. `adapter_storage_slot`: each adapter id has its own slot. `cache_length`: some request holds exactly 128 positions.
All inputs are finite; a program needn't handle non-finite values.
Results may differ from a plain program's by a relative error of at most 0.011.
Values may be sent and summed in bfloat16 or wider, within the bound.
No kernel may reach another device: no remote copies, remote signals or barrier semaphores. Data moves between devices by JAX's collectives and lax.ppermute only.
A program may use at most 128 MiB of HBM per device.

v0:
```python
import jax
import jax.numpy as jnp
from jax import lax
from jax.experimental import pallas as pl
from jax.experimental.pallas import tpu as pltpu
from jax.sharding import Mesh
from jax.sharding import PartitionSpec as P

HEADS = 64
HEAD_DIM = 128
ADP = ("z", "y", "core")
GATHERED = ((0, 0), (0, 1), (3, 0), (1, 0), (3, 1), (1, 1), (2, 0), (2, 1))
NT = (((1,), (1,)), ((), ()))
VMEM_LIMIT = 56 << 20
QUICK = pl.CostEstimate(flops=1, bytes_accessed=1, transcendentals=0)


def project_kernel(places, first, count, *refs):
    blocks, w_own, w_other, a_own, a_other = (refs[i * count : (i + 1) * count] for i in range(5))
    ins, outs = refs[5 * count : -3], refs[-3:]
    first_core = places[0] % 2 == 0
    sums = [ref[...] for ref in ins[:3]]
    for i in range(count):
        x = blocks[i][...]
        own, other = a_own[i][0], a_other[i][0]
        pair = jnp.concatenate(
            [jnp.where(first_core, own, other), jnp.where(first_core, other, own)], axis=0
        )
        parts = (
            jnp.dot(x, w_own[i][...], preferred_element_type=jnp.float32),
            jnp.dot(x, w_other[i][...], preferred_element_type=jnp.float32),
            lax.dot_general(x, pair, NT, preferred_element_type=jnp.float32),
        )
        sums = [total + part for total, part in zip(sums, parts)] if sums else parts
    outs[0][...], outs[1][...] = sums[:2]
    low = sums[2]
    if ins:
        slot = ins[3][...]
        rank = low.shape[1] // 2
        mine = places[0] - places[0] % 2
        low = jnp.where(slot == mine, low[:, :rank], 0.0) + jnp.where(
            slot == mine + 1, low[:, rank:], 0.0
        )
        half = low.shape[0] // 2
        low = jnp.concatenate([low[:half], low[half:]], axis=1)
    outs[2][...] = low


def project(places, first, blocks, weight, weight_other, down, down_other, rest):
    count = len(blocks)
    rows, width = blocks[0].shape
    cols, rank = weight.shape[1], down.shape[1]
    flat = lambda shape: pl.BlockSpec(shape, lambda j, p: (0, 0))
    low_rows = rows // 2 if rest else rows
    shapes = [(rows, cols), (rows, cols), (low_rows, 2 * rank)]
    weights = [pl.BlockSpec((width, cols), lambda j, p, i=i: (p[first + i], 0)) for i in range(count)]
    maps = [
        pl.BlockSpec((1, rank, width), lambda j, p, i=i: (0, 0, p[first + i])) for i in range(count)
    ]

    def kernel(places, *refs):
        project_kernel(places, first, count, *refs)

    return pl.pallas_call(
        kernel,
        grid_spec=pltpu.PrefetchScalarGridSpec(
            num_scalar_prefetch=1,
            grid=(1,),
            in_specs=[flat((rows, width))] * count
            + weights * 2
            + maps * 2
            + [flat(array.shape) for array in rest],
            out_specs=[flat(shape) for shape in shapes],
        ),
        out_shape=[jax.ShapeDtypeStruct(shape, jnp.float32) for shape in shapes],
        compiler_params=pltpu.CompilerParams(vmem_limit_bytes=VMEM_LIMIT),
        cost_estimate=pl.CostEstimate(
            flops=4 * count * rows * width * (cols + rank),
            bytes_accessed=2 * count * width * (rows + 2 * cols) + 8 * rows * cols,
            transcendentals=0,
        ),
    )(
        places,
        *blocks,
        *[weight] * count,
        *[weight_other] * count,
        *[down] * count,
        *[down_other] * count,
        *rest,
    )


def query_kernel(half, own, received, low, slot, up_own, up_other, out):
    step = pl.program_id(0)
    lanes = low.shape[1]
    rank = lanes // 2
    part = rank // 2
    depth = up_own.shape[0]
    shape = (lanes, depth)
    lane = lax.broadcasted_iota(jnp.int32, shape, 1) % part
    row = lax.broadcasted_iota(jnp.int32, shape, 0)
    owner = lax.broadcasted_iota(jnp.int32, (own.shape[0], depth), 1) // part
    live = slot[...] == owner
    total = own[...] + received[...]
    for h, up in ((half[0], up_own), (1 - half[0], up_other)):
        copies = (row == lane + rank * step + part * h).astype(jnp.bfloat16)
        spread = jnp.dot(low[...], copies, preferred_element_type=jnp.float32)
        spread = jnp.where(live, spread, 0.0).astype(jnp.bfloat16)
        total += jnp.dot(spread, up[...], preferred_element_type=jnp.float32)
    out[...] = (total * HEAD_DIM ** (-0.5)).astype(out.dtype)


def make_query(half, own, received, low, slot, up_own, up_other):
    rows, cols = own.shape
    tile = rows // 2
    depth = up_own.shape[0]
    by_rows = lambda width: pl.BlockSpec((tile, width), lambda j, h: (j, 0))
    whole = lambda array: pl.BlockSpec(array.shape, lambda j, h: (0, 0))
    return pl.pallas_call(
        query_kernel,
        grid_spec=pltpu.PrefetchScalarGridSpec(
            num_scalar_prefetch=1,
            grid=(2,),
            in_specs=[
                by_rows(cols),
                by_rows(received.shape[1]),
                whole(low),
                by_rows(1),
                whole(up_own),
                whole(up_other),
            ],
            out_specs=by_rows(cols),
        ),
        out_shape=jax.ShapeDtypeStruct((rows, cols), jnp.bfloat16),
        compiler_params=pltpu.CompilerParams(vmem_limit_bytes=VMEM_LIMIT),
        cost_estimate=QUICK,
    )(half, own, received, low, slot, up_own, up_other)


def output_kernel(places, count, own, other, *refs):
    for w_own, w_other, out in zip(refs[:count], refs[count : 2 * count], refs[2 * count :]):
        total = jnp.dot(own[...], w_own[...], preferred_element_type=jnp.float32)
        total += jnp.dot(other[...], w_other[...], preferred_element_type=jnp.float32)
        out[...] = total.astype(out.dtype)


def output_partial(places, first, count, own, other, weight, weight_other, width):
    rows, depth = own.shape
    tile = width // 2 if width % 256 == 0 else width
    steps = width // tile
    whole = pl.BlockSpec((rows, depth), lambda j, p: (0, 0))
    weights = [
        pl.BlockSpec((depth, tile), lambda j, p, i=i: (0, p[first + i] * steps + j))
        for i in range(count)
    ]

    def kernel(places, *refs):
        output_kernel(places, count, *refs)

    return pl.pallas_call(
        kernel,
        grid_spec=pltpu.PrefetchScalarGridSpec(
            num_scalar_prefetch=1,
            grid=(steps,),
            in_specs=[whole, whole] + weights * 2,
            out_specs=[pl.BlockSpec((rows, tile), lambda j, p: (0, j))] * count,
        ),
        out_shape=[jax.ShapeDtypeStruct((rows, width), jnp.bfloat16)] * count,
        compiler_params=pltpu.CompilerParams(vmem_limit_bytes=VMEM_LIMIT),
        cost_estimate=QUICK,
    )(places, own, other, *[weight] * count, *[weight_other] * count)


def attention(query, cache_length, key_cache, value_cache, k_new, v_new):
    local_reqs = query.shape[0]
    kv_count, _, span, dim = key_cache.shape
    group = HEADS // kv_count
    query = query.reshape(local_reqs, kv_count, group, dim)
    k_new = k_new.reshape(local_reqs, kv_count, dim)
    v_new = v_new.reshape(local_reqs, kv_count, dim)
    live = (jnp.arange(span)[None, :] < cache_length[:, None])[None, :, None, :]
    scores = jnp.einsum("rkge,krje->krgj", query, key_cache, preferred_element_type=jnp.float32)
    fresh = jnp.einsum("rkge,rke->krg", query, k_new, preferred_element_type=jnp.float32)
    scores = jnp.where(live, scores, -jnp.inf)
    top = jnp.maximum(jnp.max(scores, axis=3), fresh)
    expd = jnp.where(live, jnp.exp(scores - top[:, :, :, None]), 0.0)
    expf = jnp.exp(fresh - top)
    total = jnp.sum(expd, axis=3) + expf
    probs = (expd / total[:, :, :, None]).astype(jnp.bfloat16)
    probf = (expf / total).astype(jnp.bfloat16)
    context = jnp.einsum("krgj,krje->rkge", probs, value_cache, preferred_element_type=jnp.float32)
    fresh_part = jnp.einsum("krg,rke->rkge", probf.astype(jnp.float32), v_new.astype(jnp.float32))
    return (context + fresh_part).astype(jnp.bfloat16).reshape(local_reqs, HEADS * dim)


def shift(value, axis, by):
    size = lax.axis_size(axis)
    return lax.ppermute(value, axis, [(i, (i + by) % size) for i in range(size)])


def after(value, *others):
    return lax.optimization_barrier((value, *others))[0]


def gathered_chips():
    layers, sides = lax.axis_size("z"), lax.axis_size("y")
    z, y = lax.axis_index("z"), lax.axis_index("y")
    steps = GATHERED
    if layers != 4 or sides != 2:
        steps = [(-k, side) for k in range(layers) for side in range(sides)]
    return [((z + k) % layers) * sides + (y + side) % sides for k, side in steps]


def gather_features(tokens, down_other, up, begin):
    layers, sides = lax.axis_size("z"), lax.axis_size("y")
    z = lax.axis_index("z")
    if layers != 4 or sides != 2:
        blocks = [shift(tokens, "z", k) if k else tokens for k in range(layers)]
        blocks = [[block, shift(block, "y", 1)][:sides] for block in blocks]
        blocks = [block for pair in blocks for block in pair]
        return begin(blocks[:-1]), blocks[-1:], up
    side = shift(tokens, "y", 1)
    below, above = shift(tokens, "z", 1), shift(tokens, "z", 3)
    below, side, _ = lax.optimization_barrier((below, side, down_other))
    below_side = shift(below, "y", 1)
    from_below = lax.ppermute(below, "z", [(1, 2), (2, 3)])
    above_side = shift(above, "y", 1)
    from_above = lax.ppermute(above, "z", [(2, 1), (1, 0)])
    sums = begin([tokens, side, below, above])
    two = jnp.where(z >= 2, from_below, from_above)
    two, _, up = lax.optimization_barrier((two, below_side, up))
    return sums, [below_side, above_side, two, shift(two, "y", 1)], up


def scatter_layers(parts):
    layers = lax.axis_size("z")
    wide = lambda value: value.astype(jnp.float32)
    narrow = lambda value: value.astype(jnp.bfloat16)
    if layers != 4:
        return sum([wide(shift(narrow(parts[k]), "z", k)) for k in range(1, layers)], parts[0])
    two = narrow(parts[2])
    up = lax.ppermute(two, "z", [(0, 1), (1, 2)])
    down = lax.ppermute(two, "z", [(3, 2), (2, 1)])
    above = shift(narrow(parts[1] + wide(up)), "z", 1)
    below = shift(narrow(parts[3] + wide(down)), "z", 3)
    return parts[0] + wide(above) + wide(below)


def shards(
    tokens,
    request_adapter,
    adapter_storage_slot,
    cache_length,
    query_weight,
    adapter_down_maps,
    adapter_up_maps,
    key_cache,
    value_cache,
    new_token_key,
    new_token_value,
    output_weight,
):
    layers, sides = lax.axis_size("z"), lax.axis_size("y")
    z, y, core = lax.axis_index("z"), lax.axis_index("y"), lax.axis_index("core")
    rows, width = tokens.shape
    total_adapters = adapter_storage_slot.shape[0]
    rank = adapter_down_maps.shape[2]
    depth = output_weight.shape[0]
    chips_of = lambda layer: [
        (layer % layers) * sides + (y + side) % sides for side in range(sides)
    ]

    down = jnp.swapaxes(adapter_down_maps, 1, 2)
    down_other = shift(down, "core", 1)
    query_weight_other = shift(query_weight, "core", 1)

    ids = request_adapter[:, 0]
    numbers = jnp.arange(total_adapters, dtype=jnp.int32)
    slot = jnp.sum(
        jnp.where(ids[:, None] == numbers[None, :], adapter_storage_slot[None, :], 0), axis=1
    )[:, None]

    out_order = [2, 1, 3, 0] if layers == 4 else list(range(1, layers)) + [0]
    out_keys = [(k, side) for k in out_order for side in reversed(range(sides))]
    chips = gathered_chips()
    out_first = len(chips)
    chips += [chips_of(z + k)[side] for k, side in out_keys]
    places = jnp.stack([2 * chip + core for chip in chips]).astype(jnp.int32)

    weights = query_weight, query_weight_other, down, down_other
    half = lax.axis_index("rep") % 2
    up = jnp.swapaxes(adapter_up_maps, 1, 2)[0]
    up = lax.dynamic_slice_in_dim(up, half * (rank // 2), rank // 2, 0)
    up = lax.all_to_all(up, ADP, split_axis=1, concat_axis=0, tiled=True)
    sums, blocks, up = gather_features(
        tokens, down_other, up, lambda blocks: project(places, 0, blocks, *weights, ())
    )
    up_other = lax.ppermute(up, "rep", [(i, i ^ 1) for i in range(lax.axis_size("rep"))])

    own, sent, low = project(
        after(places, up_other), out_first - len(blocks), blocks, *weights, (*sums, slot)
    )

    low = (low + shift(low, "core", 1)).astype(jnp.bfloat16)
    received = shift(sent, "core", 1)
    if sides == 2:
        low = low + shift(low, "y", 1)
    low, received = lax.optimization_barrier((low, received))
    low = sum([shift(low, "z", k) for k in range(1, layers)], low)

    query = make_query(half.astype(jnp.int32).reshape(1), own, received, low, slot, up, up_other)
    output_weight_other = shift(after(output_weight, query), "core", 1)
    query_local = lax.all_to_all(query, ADP, split_axis=0, concat_axis=1, tiled=True)

    context = attention(
        query_local, cache_length, key_cache, value_cache, new_token_key, new_token_value
    )
    context = jnp.swapaxes(context.reshape(context.shape[0], -1, depth), 0, 1)
    context = lax.all_to_all(context, ADP, split_axis=0, concat_axis=0, tiled=True)
    context = context.reshape(rows, depth)
    context_other = shift(context, "core", 1)

    made = {}
    for first, count in ((0, 1), (1, len(out_keys) - 1)):
        outs = output_partial(
            places,
            out_first + first,
            count,
            context,
            context_other,
            output_weight,
            output_weight_other,
            width,
        )
        made.update(zip(out_keys[first : first + count], outs))
    other_side = {k: shift(made[k, 1], "y", 1) for k in out_order if sides == 2}
    parts = [None] * layers
    for k in out_order:
        parts[k] = after(made[k, 0], made[out_keys[-1]]).astype(jnp.float32)
        if sides == 2:
            parts[k] = parts[k] + other_side[k].astype(jnp.float32)
    return scatter_layers(parts).astype(jnp.bfloat16)


def solution(mesh):
    reps, adp = mesh.shape["rep"], mesh.shape["adp"]
    sides = 2 if adp == 16 else 1
    mesh = Mesh(mesh.devices.reshape(reps, adp // (2 * sides), sides, 2), ("rep",) + ADP)
    in_specs = (
        P("rep", ADP),
        P("rep", None),
        P(),
        P(("rep",) + ADP),
        P(None, ADP),
        P(ADP, None, None),
        P(ADP, None, None),
        P(None, ("rep",) + ADP, None, None),
        P(None, ("rep",) + ADP, None, None),
        P(("rep",) + ADP, None),
        P(("rep",) + ADP, None),
        P(ADP, None),
    )
    return jax.shard_map(
        shards, mesh=mesh, in_specs=in_specs, out_specs=P("rep", ADP), check_vma=False
    )
```

profile of v0, /device:TPU:0, one launch (start us, length us, event | category | flops | bytes accessed | tf_op | source)
XLA Modules:
  0.0 188.9 jit_solution(11780743151058753898)
XLA Ops:
  0.0 0.5 collective-permute-start.10
  0.5 2.6 %collective-permute-start = (bf16[384,512]{1,0:T(8,128)(2,1)}, bf16[384,512]{1,0:T(8,128)(2,1)S(1)}, u32[]{:S(2)}, u32[]{:S(2)}) collective-permute-start(bf16[384,512]{1,0:T(8,128)(2,1)} %refs_0_.1), channel_id=1, source_target_pairs={{0,4},{4,8},{8,12},{12,0},{1,5},{5,9},{9,13},{13,1},{2,6},{6,10},{... | collective-permute-start | bytes 1179656 | tf_op jit(solution)/shard_map/ppermute | solution.py:198
  3.1 1.5 collective-permute-start.1
  4.6 2.2 %collective-permute-start.4 = (bf16[384,512]{1,0:T(8,128)(2,1)}, bf16[384,512]{1,0:T(8,128)(2,1)S(1)}, u32[]{:S(2)}, u32[]{:S(2)}) collective-permute-start(bf16[384,512]{1,0:T(8,128)(2,1)} %refs_0_.1), channel_id=1, source_target_pairs={{0,12},{4,0},{8,4},{12,8},{1,13},{5,1},{9,5},{13,9},{2,14},{6,2},{... | collective-permute-start | bytes 1179656 | tf_op jit(solution)/shard_map/ppermute | solution.py:198
  7.1 1.1 copy.36
  8.2 3.6 %all-to-all-start = ((bf16[32,16,512]{2,0,1:T(8,128)(2,1)}), bf16[32,16,512]{2,0,1:T(8,128)(2,1)S(1)}, u32[]{:S(2)}, u32[]{:S(2)}) async-start(bf16[32,16,512]{2,0,1:T(8,128)(2,1)} %copy.36), calls=%async_computation | async-start | bytes 1048576 | tf_op jit(solution)/shard_map/all_to_all | solution.py:294
  11.7 13.2 %collective-permute-done.4.refs_3_ = bf16[384,512]{1,0:T(8,128)(2,1)S(1)} collective-permute-done((bf16[384,512]{1,0:T(8,128)(2,1)}, bf16[384,512]{1,0:T(8,128)(2,1)S(1)}, u32[]{:S(2)}, u32[]{:S(2)}) %collective-permute-start.4) | collective-permute-done | bytes 393248 | tf_op jit(solution)/shard_map/ppermute | solution.py:198
  25.0 1.3 collective-permute-start.5
  26.3 1.4 collective-permute-start.3
  27.8 0.7 collective-permute-start.6
  28.5 11.9 %collective-permute-done.5 = bf16[384,512]{1,0:T(8,128)(2,1)S(1)} collective-permute-done((bf16[384,512]{1,0:T(8,128)(2,1)S(1)}, bf16[384,512]{1,0:T(8,128)(2,1)S(1)}, u32[]{:S(2)}, u32[]{:S(2)}) %collective-permute-start.5) | collective-permute-done | bytes 393248 | tf_op jit(solution)/shard_map/ppermute | solution.py:228
  40.3 0.7 copy-done.12
  41.1 1.0 broadcast_select_fusion.refs_2_
  42.2 1.6 collective-permute-start.7
  43.7 1.2 collective-permute-start.8
  44.9 0.8 collective-permute-start.9
  45.8 0.7 reduce
  46.5 0.7 select_reduce_fusion
  47.2 0.8 broadcast_in_dim.46.refs_23_.slot
  48.0 0.6 stack.43.places
  48.6 7.5 %collective-permute-done.7.up_other = bf16[512,512]{1,0:T(8,128)(2,1)S(1)} collective-permute-done((bf16[512,512]{1,0:T(8,128)(2,1)S(1)}, bf16[512,512]{1,0:T(8,128)(2,1)S(1)}, u32[]{:S(2)}, u32[]{:S(2)}) %collective-permute-start.7) | collective-permute-done | bytes 524320 | tf_op jit(solution)/shard_map/ppermute | solution.py:298
  56.1 6.6 %shard_map.118 = (f32[384,512]{1,0:T(8,128)}, f32[384,512]{1,0:T(8,128)}, f32[384,128]{1,0:T(8,128)}) custom-call(s32[16]{0:T(128)} %stack.43.places, bf16[384,512]{1,0:T(8,128)(2,1)} %refs_0_.1, bf16[384,512]{1,0:T(8,128)(2,1)} %copy-done.10, bf16[384,512]{1,0:T(8,128)(2,1)} %copy-done.9, bf16[384,512]{1,0:T(8,128)(2,1)} %copy-done.11, ...), custom_call_target="tpu_custom_call" | custom-call | flops 1811939328 | bytes 7340032 | tf_op jit(solution)/shard_map/pallas_call | solution.py:64
  62.7 0.5 collective-permute-done.9.refs_3_
  63.2 7.3 %shard_map.119 = (f32[384,512]{1,0:T(8,128)}, f32[384,512]{1,0:T(8,128)}, f32[192,128]{1,0:T(8,128)}) custom-call(s32[16]{0:T(128)} %stack.43.places, bf16[384,512]{1,0:T(8,128)(2,1)} %collective-permute-done.6.refs_0_, bf16[384,512]{1,0:T(8,128)(2,1)} %collective-permute-done.8.refs_1_, bf16[384,512]{1,0:T(8,128)(2,1)} %copy-done.5, ...), custom_call_target="tpu_custom_call" | custom-call | flops 1811939328 | bytes 7340032 | tf_op jit(solution)/shard_map/pallas_call | solution.py:64
  70.5 0.5 collective-permute-start.11
  71.0 2.1 %collective-permute-done.11 = f32[192,128]{1,0:T(8,128)S(1)} collective-permute-done((f32[192,128]{1,0:T(8,128)}, f32[192,128]{1,0:T(8,128)S(1)}, u32[]{:S(2)}, u32[]{:S(2)}) %collective-permute-start.11) | collective-permute-done | bytes 98336 | tf_op jit(solution)/shard_map/ppermute | solution.py:198
  73.2 0.9 add_convert_fusion.4
  74.1 0.9 collective-permute-start.12
  75.0 3.3 %collective-permute-done.12 = bf16[192,128]{1,0:T(8,128)(2,1)S(1)} collective-permute-done((bf16[192,128]{1,0:T(8,128)(2,1)S(1)}, bf16[192,128]{1,0:T(8,128)(2,1)S(1)}, u32[]{:S(2)}, u32[]{:S(2)}) %collective-permute-start.12) | collective-permute-done | bytes 49184 | tf_op jit(solution)/shard_map/ppermute | solution.py:198
  78.3 3.5 %collective-permute-start.14 = (bf16[192,128]{1,0:T(8,128)(2,1)S(1)}, bf16[192,128]{1,0:T(8,128)(2,1)S(1)}, u32[]{:S(2)}, u32[]{:S(2)}) collective-permute-start(bf16[192,128]{1,0:T(8,128)(2,1)S(1)} %add.217), channel_id=1, source_target_pairs={{0,4},{4,8},{8,12},{12,0},{1,5},{5,9},{9,13},{13,1},{2,6},{6,10},{... | collective-permute-start | bytes 147464 | tf_op jit(solution)/shard_map/ppermute | solution.py:198
  81.8 2.5 %collective-permute-start.16 = (bf16[192,128]{1,0:T(8,128)(2,1)S(1)}, bf16[192,128]{1,0:T(8,128)(2,1)S(1)}, u32[]{:S(2)}, u32[]{:S(2)}) collective-permute-start(bf16[192,128]{1,0:T(8,128)(2,1)S(1)} %add.217), channel_id=1, source_target_pairs={{0,12},{4,0},{8,4},{12,8},{1,13},{5,1},{9,5},{13,9},{2,14},{6,2},{... | collective-permute-start | bytes 147464 | tf_op jit(solution)/shard_map/ppermute | solution.py:198
  84.3 0.4 collective-permute-done.14
  84.7 2.2 %collective-permute-done.15 = bf16[192,128]{1,0:T(8,128)(2,1)S(1)} collective-permute-done((bf16[192,128]{1,0:T(8,128)(2,1)S(1)}, bf16[192,128]{1,0:T(8,128)(2,1)S(1)}, u32[]{:S(2)}, u32[]{:S(2)}) %collective-permute-start.15) | collective-permute-done | bytes 49184 | tf_op jit(solution)/shard_map/ppermute | solution.py:198
  86.9 0.6 add_add_fusion.low
  87.5 3.6 %shard_map.120 = bf16[384,512]{1,0:T(8,128)(2,1)} custom-call(s32[1]{0:T(128)} %bitcast.8.half, f32[384,512]{1,0:T(8,128)} %get-tuple-element.38.own, f32[384,512]{1,0:T(8,128)} %copy-done.7, bf16[192,128]{1,0:T(8,128)(2,1)} %add_add_fusion.low, s32[384,1]{1,0:T(8,128)} %broadcast_in_dim.46.refs_23_.slot, bf16[512,512]{1,0:T(8,128)(2,1)} %bitcast.52, ...), custom_call_target="tpu_custom_call" | custom-call | flops 1 | bytes 1 | tf_op jit(solution)/shard_map/pallas_call | solution.py:119
  91.1 5.8 %all-to-all-start.1 = ((bf16[16,24,512]{2,1,0:T(8,128)(2,1)}), bf16[16,24,512]{2,1,0:T(8,128)(2,1)S(1)}, u32[]{:S(2)}, u32[]{:S(2)}) async-start(bf16[16,24,512]{2,1,0:T(8,128)(2,1)} %bitcast.55), calls=%async_computation.1 | async-start | bytes 786432 | tf_op jit(solution)/shard_map/all_to_all | solution.py:313
  97.0 12.0 %all-to-all-done.1 = bf16[16,24,512]{2,1,0:T(8,128)(2,1)S(1)} async-done(((bf16[16,24,512]{2,1,0:T(8,128)(2,1)}), bf16[16,24,512]{2,1,0:T(8,128)(2,1)S(1)}, u32[]{:S(2)}, u32[]{:S(2)}) %all-to-all-start.1) | async-done | bytes 393248 | tf_op jit(solution)/shard_map/all_to_all | solution.py:313
  109.8 5.5 %fusion.15 = (f32[8,24,8]{2,1,0:T(8,128)S(1)}, f32[8,24,8,128]{3,2,1,0:T(8,128)S(1)}) fusion(bf16[8,24,128,128]{3,2,1,0:T(8,128)(2,1)} %param.19, bf16[24,8,8,128]{3,2,1,0:T(8,128)(2,1)S(1)} %reshape.48, pred[24,128]{1,0:T(8,128)(4,1)S(1)} %iota_compare_fusion.1), kind=kOutput, calls=%fused_computation.30 | convolution fusion | flops 50723328 | bytes 7480320 | tf_op jit(solution)/shard_map/rkge,krje->krgj/dot_general | solution.py:182
  115.3 0.5 fusion.8
  116.0 4.6 %fusion.5 = bf16[24,8,8,128]{3,2,1,0:T(8,128)(2,1)S(1)} fusion(bf16[8,24,128,128]{3,2,1,0:T(8,128)(2,1)} %param.20, f32[24,8,128]{2,1,0:T(8,128)S(1)} %bitcast.58, f32[24,8,8]{2,1,0:T(8,128)S(1)} %copy.43, f32[8,24,8,128]{3,2,1,0:T(8,128)S(1)} %get-tuple-element.58, f32[8,24,8]{2,1,0:T(8,128)S(1)} %get-tuple-element.56, f32[8,24,8]{2,1,0:T(8,128)S(1)} %max.3, ...), kind=kOutput, calls=%fused_computation.4 | convolution fusion | flops 51707904 | bytes 7590912 | tf_op jit(solution)/shard_map/krgj,krje->rkge/dot_general | solution.py:191
  121.0 15.5 %all_to_all.40 = bf16[16,24,512]{2,1,0:T(8,128)(2,1)S(1)} all-to-all(bf16[16,24,512]{2,1,0:T(8,128)(2,1)S(1)} %bitcast.54), channel_id=1, replica_groups=mesh['rep'=2,'z'=4,'y'=2,'core'=2] {'z','y','core'}, dimensions={0} | all-to-all | bytes 786432 | tf_op jit(solution)/shard_map/all_to_all | solution.py:319
  136.6 1.6 collective-permute-done.17.refs_1_
  138.3 0.8 copy-done.6
  139.1 3.4 %shard_map.122 = bf16[384,512]{1,0:T(8,128)(2,1)} custom-call(s32[16]{0:T(128)} %stack.43.places, bf16[384,512]{1,0:T(8,128)(2,1)} %bitcast.47, bf16[384,512]{1,0:T(8,128)(2,1)} %copy-done.6, bf16[512,8192]{1,0:T(8,128)(2,1)} %refs_2_.3, bf16[512,8192]{1,0:T(8,128)(2,1)} %collective-permute-done.18.refs_9_.refs_10_.refs_11_.refs_12_.refs_13_.refs_14_.refs_15_.refs_3_), custom_call_target="tpu_custom_call" | custom-call | flops 1 | bytes 1 | tf_op jit(solution)/shard_map/pallas_call | solution.py:160
  142.5 0.6 collective-permute-start.21
  143.1 7.5 %shard_map.121 = (bf16[384,512]{1,0:T(8,128)(2,1)}, bf16[384,512]{1,0:T(8,128)(2,1)}, bf16[384,512]{1,0:T(8,128)(2,1)}, bf16[384,512]{1,0:T(8,128)(2,1)}, bf16[3...) custom-call(s32[16]{0:T(128)} %stack.43.places, bf16[384,512]{1,0:T(8,128)(2,1)} %bitcast.48, ...), custom_call_target="tpu_custom_call" | custom-call | flops 1 | bytes 1 | tf_op jit(solution)/shard_map/pallas_call | solution.py:160
  150.6 1.5 collective-permute-start.20
  152.1 2.1 %collective-permute-done.21 = bf16[384,512]{1,0:T(8,128)(2,1)S(1)} collective-permute-done((bf16[384,512]{1,0:T(8,128)(2,1)}, bf16[384,512]{1,0:T(8,128)(2,1)S(1)}, u32[]{:S(2)}, u32[]{:S(2)}) %collective-permute-start.21) | collective-permute-done | bytes 393248 | tf_op jit(solution)/shard_map/ppermute | solution.py:198
  154.1 1.1 add_convert_fusion.3
  155.2 3.1 %collective-permute-start.22 = (bf16[384,512]{1,0:T(8,128)(2,1)S(1)}, bf16[384,512]{1,0:T(8,128)(2,1)S(1)}, u32[]{:S(2)}, u32[]{:S(2)}) collective-permute-start(bf16[384,512]{1,0:T(8,128)(2,1)S(1)} %add_convert_fusion.3), channel_id=1, source_target_pairs={{0,4},{4,8},{1,5},{5,9},{2,6},{6,10},{3,7},{7,11},{16,20},{20,24},... | collective-permute-start | bytes 1179656 | tf_op jit(solution)/shard_map/ppermute | solution.py:242
  158.3 0.6 collective-permute-start.24
  158.9 0.7 collective-permute-start.25
  159.6 1.5 collective-permute-start.19
  161.1 1.7 collective-permute-done.20
  162.8 3.3 %collective-permute-done.22 = bf16[384,512]{1,0:T(8,128)(2,1)S(1)} collective-permute-done((bf16[384,512]{1,0:T(8,128)(2,1)S(1)}, bf16[384,512]{1,0:T(8,128)(2,1)S(1)}, u32[]{:S(2)}, u32[]{:S(2)}) %collective-permute-start.22) | collective-permute-done | bytes 393248 | tf_op jit(solution)/shard_map/ppermute | solution.py:242
  166.1 1.1 add_convert_fusion.2
  167.2 2.5 %collective-permute-start.23 = (bf16[384,512]{1,0:T(8,128)(2,1)S(1)}, bf16[384,512]{1,0:T(8,128)(2,1)S(1)}, u32[]{:S(2)}, u32[]{:S(2)}) collective-permute-start(bf16[384,512]{1,0:T(8,128)(2,1)S(1)} %add_convert_fusion.2), channel_id=1, source_target_pairs={{0,4},{4,8},{8,12},{12,0},{1,5},{5,9},{9,13},{13,1},{2,6},{6,10},{... | collective-permute-start | bytes 1179656 | tf_op jit(solution)/shard_map/ppermute | solution.py:198
  169.8 1.5 collective-permute-done.24
  171.2 1.1 add_convert_fusion.1
  172.4 2.2 %collective-permute-start.26 = (bf16[384,512]{1,0:T(8,128)(2,1)S(1)}, bf16[384,512]{1,0:T(8,128)(2,1)S(1)}, u32[]{:S(2)}, u32[]{:S(2)}) collective-permute-start(bf16[384,512]{1,0:T(8,128)(2,1)S(1)} %add_convert_fusion.1), channel_id=1, source_target_pairs={{0,12},{4,0},{8,4},{12,8},{1,13},{5,1},{9,5},{13,9},{2,14},{6,2},{... | collective-permute-start | bytes 1179656 | tf_op jit(solution)/shard_map/ppermute | solution.py:198
  174.5 4.6 %collective-permute-done.19 = bf16[384,512]{1,0:T(8,128)(2,1)S(1)} collective-permute-done((bf16[384,512]{1,0:T(8,128)(2,1)}, bf16[384,512]{1,0:T(8,128)(2,1)S(1)}, u32[]{:S(2)}, u32[]{:S(2)}) %collective-permute-start.19) | collective-permute-done | bytes 393248 | tf_op jit(solution)/shard_map/ppermute | solution.py:198
  179.1 2.0 %collective-permute-done.23 = bf16[384,512]{1,0:T(8,128)(2,1)S(1)} collective-permute-done((bf16[384,512]{1,0:T(8,128)(2,1)S(1)}, bf16[384,512]{1,0:T(8,128)(2,1)S(1)}, u32[]{:S(2)}, u32[]{:S(2)}) %collective-permute-start.23) | collective-permute-done | bytes 393248 | tf_op jit(solution)/shard_map/ppermute | solution.py:198
  181.1 5.9 %collective-permute-done.26 = bf16[384,512]{1,0:T(8,128)(2,1)S(1)} collective-permute-done((bf16[384,512]{1,0:T(8,128)(2,1)S(1)}, bf16[384,512]{1,0:T(8,128)(2,1)S(1)}, u32[]{:S(2)}, u32[]{:S(2)}) %collective-permute-start.26) | collective-permute-done | bytes 393248 | tf_op jit(solution)/shard_map/ppermute | solution.py:198
  187.0 1.9 %add_convert_fusion = bf16[384,512]{1,0:T(8,128)(2,1)} fusion(bf16[384,512]{1,0:T(8,128)(2,1)S(1)} %collective-permute-done.26, bf16[384,512]{1,0:T(8,128)(2,1)S(1)} %collective-permute-done.23, bf16[384,512]{1,0:T(8,128)(2,1)S(1)} %collective-permute-done.19, bf16[384,512]{1,0:T(8,128)(2,1)} %get-tuple-element.45), kind=kLoop, calls=%fused_computation.5 | loop fusion | flops 1572864 | bytes 1966080 | tf_op jit(solution)/shard_map/convert_element_type | solution.py:342
  (62 shorter events, 1.8 us)
Async XLA Ops:
  0.0 6.9 %copy-start = (bf16[1,8192,64]{1,2,0:T(8,128)(2,1)S(1)}, bf16[1,8192,64]{1,2,0:T(8,128)(2,1)}, u32[]{:S(2)}) copy-start(bf16[1,8192,64]{1,2,0:T(8,128)(2,1)} %param.18) | copy-start | bytes 3145732
  0.0 56.1 %collective-permute-start.10 = (bf16[8192,512]{1,0:T(8,128)(2,1)}, bf16[8192,512]{1,0:T(8,128)(2,1)}, u32[]{:S(2)}, u32[]{:S(2)}) collective-permute-start(bf16[8192,512]{1,0:T(8,128)(2,1)} %refs_7_.4), channel_id=1, source_target_pairs={{0,1},{1,0},{2,3},{3,2},{4,5},{5,4},{6,7},{7,6},{8,9},{9,8},{10,11... | collective-permute-start | bytes 25165832 | tf_op jit(solution)/shard_map/ppermute | solution.py:198
  0.5 25.8 %collective-permute-start = (bf16[384,512]{1,0:T(8,128)(2,1)}, bf16[384,512]{1,0:T(8,128)(2,1)S(1)}, u32[]{:S(2)}, u32[]{:S(2)}) collective-permute-start(bf16[384,512]{1,0:T(8,128)(2,1)} %refs_0_.1), channel_id=1, source_target_pairs={{0,4},{4,8},{8,12},{12,0},{1,5},{5,9},{9,13},{13,1},{2,6},{6,10},{... | collective-permute-start | bytes 1179656 | tf_op jit(solution)/shard_map/ppermute | solution.py:198
  3.1 23.2 %collective-permute-start.1 = (bf16[384,512]{1,0:T(8,128)(2,1)}, bf16[384,512]{1,0:T(8,128)(2,1)S(1)}, u32[]{:S(2)}, u32[]{:S(2)}) collective-permute-start(bf16[384,512]{1,0:T(8,128)(2,1)} %refs_0_.1), channel_id=1, source_target_pairs={{0,2},{2,0},{1,3},{3,1},{4,6},{6,4},{5,7},{7,5},{8,10},{10,8},{9,1... | collective-permute-start | bytes 1179656 | tf_op jit(solution)/shard_map/ppermute | solution.py:198
  4.6 20.4 %collective-permute-start.4 = (bf16[384,512]{1,0:T(8,128)(2,1)}, bf16[384,512]{1,0:T(8,128)(2,1)S(1)}, u32[]{:S(2)}, u32[]{:S(2)}) collective-permute-start(bf16[384,512]{1,0:T(8,128)(2,1)} %refs_0_.1), channel_id=1, source_target_pairs={{0,12},{4,0},{8,4},{12,8},{1,13},{5,1},{9,5},{13,9},{2,14},{6,2},{... | collective-permute-start | bytes 1179656 | tf_op jit(solution)/shard_map/ppermute | solution.py:198
  6.9 19.4 %collective-permute-start.2 = (bf16[1,64,8192]{2,1,0:T(8,128)(2,1)}, bf16[1,64,8192]{2,1,0:T(8,128)(2,1)S(1)}, u32[]{:S(2)}, u32[]{:S(2)}) collective-permute-start(bf16[1,64,8192]{2,1,0:T(8,128)(2,1)} %bitcast.37), channel_id=1, source_target_pairs={{0,1},{1,0},{2,3},{3,2},{4,5},{5,4},{6,7},{7,6},{8,9},{9,8},{10,11... | collective-permute-start | bytes 3145736 | tf_op jit(solution)/shard_map/ppermute | solution.py:198
  8.2 34.0 %all-to-all-start = ((bf16[32,16,512]{2,0,1:T(8,128)(2,1)}), bf16[32,16,512]{2,0,1:T(8,128)(2,1)S(1)}, u32[]{:S(2)}, u32[]{:S(2)}) async-start(bf16[32,16,512]{2,0,1:T(8,128)(2,1)} %copy.36), calls=%async_computation | async-start | bytes 1048576 | tf_op jit(solution)/shard_map/all_to_all | solution.py:294
  25.0 17.2 %copy-start.11 = (bf16[384,512]{1,0:T(8,128)(2,1)}, bf16[384,512]{1,0:T(8,128)(2,1)S(1)}, u32[]{:S(2)}) copy-start(bf16[384,512]{1,0:T(8,128)(2,1)S(1)} %collective-permute-done.4.refs_3_) | copy-start | bytes 1179652
  25.0 15.4 %collective-permute-start.5 = (bf16[384,512]{1,0:T(8,128)(2,1)S(1)}, bf16[384,512]{1,0:T(8,128)(2,1)S(1)}, u32[]{:S(2)}, u32[]{:S(2)}) collective-permute-start(bf16[384,512]{1,0:T(8,128)(2,1)S(1)} %collective-permute-done.4.refs_3_), channel_id=1, source_target_pairs={{8,4},{4,0},{9,5},{5,1},{10,6},{6,2},{11,7},{7,3},{24,20},{20,16},... | collective-permute-start | bytes 1179656 | tf_op jit(solution)/shard_map/ppermute | solution.py:228
  26.3 29.8 %copy-start.9 = (bf16[384,512]{1,0:T(8,128)(2,1)}, bf16[384,512]{1,0:T(8,128)(2,1)S(1)}, u32[]{:S(2)}) copy-start(bf16[384,512]{1,0:T(8,128)(2,1)S(1)} %collective-permute-done.refs_2_) | copy-start | bytes 1179652
  26.3 29.8 %copy-start.10 = (bf16[384,512]{1,0:T(8,128)(2,1)}, bf16[384,512]{1,0:T(8,128)(2,1)S(1)}, u32[]{:S(2)}) copy-start(bf16[384,512]{1,0:T(8,128)(2,1)S(1)} %collective-permute-done.1.refs_1_) | copy-start | bytes 1179652
  26.3 29.8 %copy-start.2 = (bf16[1,64,8192]{2,1,0:T(8,128)(2,1)}, bf16[1,64,8192]{2,1,0:T(8,128)(2,1)S(1)}, u32[]{:S(2)}) copy-start(bf16[1,64,8192]{2,1,0:T(8,128)(2,1)S(1)} %collective-permute-done.2.refs_16_.refs_17_.refs_18_.refs_19_) | copy-start | bytes 3145732
  26.3 14.8 %collective-permute-start.3 = (bf16[384,512]{1,0:T(8,128)(2,1)S(1)}, bf16[384,512]{1,0:T(8,128)(2,1)}, u32[]{:S(2)}, u32[]{:S(2)}) collective-permute-start(bf16[384,512]{1,0:T(8,128)(2,1)S(1)} %collective-permute-done.refs_2_), channel_id=1, source_target_pairs={{4,8},{8,12},{5,9},{9,13},{6,10},{10,14},{7,11},{11,15},{20,24},{2... | collective-permute-start | bytes 1179656 | tf_op jit(solution)/shard_map/ppermute | solution.py:226
  27.8 14.4 %collective-permute-start.6 = (bf16[384,512]{1,0:T(8,128)(2,1)S(1)}, bf16[384,512]{1,0:T(8,128)(2,1)}, u32[]{:S(2)}, u32[]{:S(2)}) collective-permute-start(bf16[384,512]{1,0:T(8,128)(2,1)S(1)} %collective-permute-done.refs_2_), channel_id=1, source_target_pairs={{0,2},{2,0},{1,3},{3,1},{4,6},{6,4},{5,7},{7,5},{8,10},{10,8},{9,1... | collective-permute-start | bytes 1179656 | tf_op jit(solution)/shard_map/ppermute | solution.py:198
  40.3 0.7 copy-start.12
  42.1 20.6 %copy-start.5 = (bf16[384,512]{1,0:T(8,128)(2,1)}, bf16[384,512]{1,0:T(8,128)(2,1)S(1)}, u32[]{:S(2)}) copy-start(bf16[384,512]{1,0:T(8,128)(2,1)S(1)} %broadcast_select_fusion.refs_2_) | copy-start | bytes 1179652
  42.1 20.5 %copy-start.4 = (bf16[32,16,512]{2,0,1:T(8,128)(2,1)}, bf16[32,16,512]{2,0,1:T(8,128)(2,1)S(1)}, u32[]{:S(2)}) copy-start(bf16[32,16,512]{2,0,1:T(8,128)(2,1)S(1)} %all-to-all-done) | copy-start | bytes 1572868
  42.2 13.9 %collective-permute-start.7 = (bf16[512,512]{1,0:T(8,128)(2,1)S(1)}, bf16[512,512]{1,0:T(8,128)(2,1)S(1)}, u32[]{:S(2)}, u32[]{:S(2)}) collective-permute-start(bf16[512,512]{1,0:T(8,128)(2,1)S(1)} %bitcast.51), channel_id=1, source_target_pairs={{0,16},{16,0},{1,17},{17,1},{2,18},{18,2},{3,19},{19,3},{4,20},{20... | collective-permute-start | bytes 1572872 | tf_op jit(solution)/shard_map/ppermute | solution.py:298
  43.7 19.0 %collective-permute-start.8 = (bf16[384,512]{1,0:T(8,128)(2,1)}, bf16[384,512]{1,0:T(8,128)(2,1)}, u32[]{:S(2)}, u32[]{:S(2)}) collective-permute-start(bf16[384,512]{1,0:T(8,128)(2,1)} %copy-done.11), channel_id=1, source_target_pairs={{0,2},{2,0},{1,3},{3,1},{4,6},{6,4},{5,7},{7,5},{8,10},{10,8},{9,1... | collective-permute-start | bytes 1179656 | tf_op jit(solution)/shard_map/ppermute | solution.py:198
  44.9 18.3 %collective-permute-start.9 = (bf16[384,512]{1,0:T(8,128)(2,1)S(1)}, bf16[384,512]{1,0:T(8,128)(2,1)}, u32[]{:S(2)}, u32[]{:S(2)}) collective-permute-start(bf16[384,512]{1,0:T(8,128)(2,1)S(1)} %broadcast_select_fusion.refs_2_), channel_id=1, source_target_pairs={{0,2},{2,0},{1,3},{3,1},{4,6},{6,4},{5,7},{7,5},{8,10},{10,8},{9,1... | collective-permute-start | bytes 1179656 | tf_op jit(solution)/shard_map/ppermute | solution.py:198
  56.1 6.6 %copy-start.8 = (bf16[512,512]{1,0:T(8,128)(2,1)}, bf16[512,512]{1,0:T(8,128)(2,1)S(1)}, u32[]{:S(2)}) copy-start(bf16[512,512]{1,0:T(8,128)(2,1)S(1)} %collective-permute-done.7.up_other) | copy-start | bytes 1572868
  63.2 33.6 %copy-start.13 = (bf16[24,1024]{1,0:T(8,128)(2,1)S(1)}, bf16[24,1024]{1,0:T(8,128)(2,1)}, u32[]{:S(2)}) copy-start(bf16[24,1024]{1,0:T(8,128)(2,1)} %param.21) | copy-start | bytes 147460
  63.2 33.7 %copy-start.14 = (bf16[24,1024]{1,0:T(8,128)(2,1)S(1)}, bf16[24,1024]{1,0:T(8,128)(2,1)}, u32[]{:S(2)}) copy-start(bf16[24,1024]{1,0:T(8,128)(2,1)} %param.22) | copy-start | bytes 147460
  63.2 33.7 %copy-start.15 = (s32[24]{0:T(128)S(1)}, s32[24]{0:T(128)}, u32[]{:S(2)}) copy-start(s32[24]{0:T(128)} %param.15) | copy-start | bytes 292
  70.5 7.7 %collective-permute-start.13 = (f32[384,512]{1,0:T(8,128)}, f32[384,512]{1,0:T(8,128)S(1)}, u32[]{:S(2)}, u32[]{:S(2)}) collective-permute-start(f32[384,512]{1,0:T(8,128)} %get-tuple-element.40), channel_id=1, source_target_pairs={{0,1},{1,0},{2,3},{3,2},{4,5},{5,4},{6,7},{7,6},{8,9},{9,8},{10,11... | collective-permute-start | bytes 2359304 | tf_op jit(solution)/shard_map/ppermute | solution.py:198
  70.5 2.6 %collective-permute-start.11 = (f32[192,128]{1,0:T(8,128)}, f32[192,128]{1,0:T(8,128)S(1)}, u32[]{:S(2)}, u32[]{:S(2)}) collective-permute-start(f32[192,128]{1,0:T(8,128)} %get-tuple-element.39), channel_id=1, source_target_pairs={{0,1},{1,0},{2,3},{3,2},{4,5},{5,4},{6,7},{7,6},{8,9},{9,8},{10,11... | collective-permute-start | bytes 294920 | tf_op jit(solution)/shard_map/ppermute | solution.py:198
  74.1 4.2 %collective-permute-start.12 = (bf16[192,128]{1,0:T(8,128)(2,1)S(1)}, bf16[192,128]{1,0:T(8,128)(2,1)S(1)}, u32[]{:S(2)}, u32[]{:S(2)}) collective-permute-start(bf16[192,128]{1,0:T(8,128)(2,1)S(1)} %add_convert_fusion.4), channel_id=1, source_target_pairs={{0,2},{2,0},{1,3},{3,1},{4,6},{6,4},{5,7},{7,5},{8,10},{10,8},{9,1... | collective-permute-start | bytes 147464 | tf_op jit(solution)/shard_map/ppermute | solution.py:198
  78.3 9.2 %copy-start.7 = (f32[384,512]{1,0:T(8,128)}, f32[384,512]{1,0:T(8,128)S(1)}, u32[]{:S(2)}) copy-start(f32[384,512]{1,0:T(8,128)S(1)} %collective-permute-done.13.received) | copy-start | bytes 2359300
  78.3 6.4 %collective-permute-start.14 = (bf16[192,128]{1,0:T(8,128)(2,1)S(1)}, bf16[192,128]{1,0:T(8,128)(2,1)S(1)}, u32[]{:S(2)}, u32[]{:S(2)}) collective-permute-start(bf16[192,128]{1,0:T(8,128)(2,1)S(1)} %add.217), channel_id=1, source_target_pairs={{0,4},{4,8},{8,12},{12,0},{1,5},{5,9},{9,13},{13,1},{2,6},{6,10},{... | collective-permute-start | bytes 147464 | tf_op jit(solution)/shard_map/ppermute | solution.py:198
  81.8 5.1 %collective-permute-start.15 = (bf16[192,128]{1,0:T(8,128)(2,1)S(1)}, bf16[192,128]{1,0:T(8,128)(2,1)S(1)}, u32[]{:S(2)}, u32[]{:S(2)}) collective-permute-start(bf16[192,128]{1,0:T(8,128)(2,1)S(1)} %add.217), channel_id=1, source_target_pairs={{0,8},{4,12},{8,0},{12,4},{1,9},{5,13},{9,1},{13,5},{2,10},{6,14},... | collective-permute-start | bytes 147464 | tf_op jit(solution)/shard_map/ppermute | solution.py:198
  81.8 5.1 %collective-permute-start.16 = (bf16[192,128]{1,0:T(8,128)(2,1)S(1)}, bf16[192,128]{1,0:T(8,128)(2,1)S(1)}, u32[]{:S(2)}, u32[]{:S(2)}) collective-permute-start(bf16[192,128]{1,0:T(8,128)(2,1)S(1)} %add.217), channel_id=1, source_target_pairs={{0,12},{4,0},{8,4},{12,8},{1,13},{5,1},{9,5},{13,9},{2,14},{6,2},{... | collective-permute-start | bytes 147464 | tf_op jit(solution)/shard_map/ppermute | solution.py:198
  91.1 47.2 %collective-permute-start.18 = (bf16[512,8192]{1,0:T(8,128)(2,1)}, bf16[512,8192]{1,0:T(8,128)(2,1)}, u32[]{:S(2)}, u32[]{:S(2)}) collective-permute-start(bf16[512,8192]{1,0:T(8,128)(2,1)} %refs_2_.3), channel_id=1, source_target_pairs={{0,1},{1,0},{2,3},{3,2},{4,5},{5,4},{6,7},{7,6},{8,9},{9,8},{10,11... | collective-permute-start | bytes 25165832 | tf_op jit(solution)/shard_map/ppermute | solution.py:198
  91.1 18.0 %all-to-all-start.1 = ((bf16[16,24,512]{2,1,0:T(8,128)(2,1)}), bf16[16,24,512]{2,1,0:T(8,128)(2,1)S(1)}, u32[]{:S(2)}, u32[]{:S(2)}) async-start(bf16[16,24,512]{2,1,0:T(8,128)(2,1)} %bitcast.55), calls=%async_computation.1 | async-start | bytes 786432 | tf_op jit(solution)/shard_map/all_to_all | solution.py:313
  136.5 1.7 copy-start.3
  136.5 1.7 collective-permute-start.17
  138.3 0.8 copy-start.6
  142.5 11.6 %collective-permute-start.21 = (bf16[384,512]{1,0:T(8,128)(2,1)}, bf16[384,512]{1,0:T(8,128)(2,1)S(1)}, u32[]{:S(2)}, u32[]{:S(2)}) collective-permute-start(bf16[384,512]{1,0:T(8,128)(2,1)} %shard_map.122), channel_id=1, source_target_pairs={{0,2},{2,0},{1,3},{3,1},{4,6},{6,4},{5,7},{7,5},{8,10},{10,8},{9,1... | collective-permute-start | bytes 1179656 | tf_op jit(solution)/shard_map/ppermute | solution.py:198
  143.1 45.8 %copy-start.1 = (bf16[1,8192,64]{1,2,0:T(8,128)(2,1)S(1)}, bf16[1,8192,64]{1,2,0:T(8,128)(2,1)}, u32[]{:S(2)}) copy-start(bf16[1,8192,64]{1,2,0:T(8,128)(2,1)} %param.18) | copy-start | bytes 3145732
  150.6 12.2 %collective-permute-start.20 = (bf16[384,512]{1,0:T(8,128)(2,1)}, bf16[384,512]{1,0:T(8,128)(2,1)S(1)}, u32[]{:S(2)}, u32[]{:S(2)}) collective-permute-start(bf16[384,512]{1,0:T(8,128)(2,1)} %get-tuple-element.49), channel_id=1, source_target_pairs={{0,2},{2,0},{1,3},{3,1},{4,6},{6,4},{5,7},{7,5},{8,10},{10,8},{9,1... | collective-permute-start | bytes 1179656 | tf_op jit(solution)/shard_map/ppermute | solution.py:198
  155.2 10.9 %collective-permute-start.22 = (bf16[384,512]{1,0:T(8,128)(2,1)S(1)}, bf16[384,512]{1,0:T(8,128)(2,1)S(1)}, u32[]{:S(2)}, u32[]{:S(2)}) collective-permute-start(bf16[384,512]{1,0:T(8,128)(2,1)S(1)} %add_convert_fusion.3), channel_id=1, source_target_pairs={{0,4},{4,8},{1,5},{5,9},{2,6},{6,10},{3,7},{7,11},{16,20},{20,24},... | collective-permute-start | bytes 1179656 | tf_op jit(solution)/shard_map/ppermute | solution.py:242
  158.3 12.9 %collective-permute-start.24 = (bf16[384,512]{1,0:T(8,128)(2,1)}, bf16[384,512]{1,0:T(8,128)(2,1)S(1)}, u32[]{:S(2)}, u32[]{:S(2)}) collective-permute-start(bf16[384,512]{1,0:T(8,128)(2,1)} %get-tuple-element.54), channel_id=1, source_target_pairs={{0,2},{2,0},{1,3},{3,1},{4,6},{6,4},{5,7},{7,5},{8,10},{10,8},{9,1... | collective-permute-start | bytes 1179656 | tf_op jit(solution)/shard_map/ppermute | solution.py:198
  158.9 12.3 %collective-permute-start.25 = (bf16[384,512]{1,0:T(8,128)(2,1)S(1)}, bf16[384,512]{1,0:T(8,128)(2,1)S(1)}, u32[]{:S(2)}, u32[]{:S(2)}) collective-permute-start(bf16[384,512]{1,0:T(8,128)(2,1)S(1)} %add_convert_fusion.3), channel_id=1, source_target_pairs={{12,8},{8,4},{13,9},{9,5},{14,10},{10,6},{15,11},{11,7},{28,24},{2... | collective-permute-start | bytes 1179656 | tf_op jit(solution)/shard_map/ppermute | solution.py:243
  159.6 19.5 %collective-permute-start.19 = (bf16[384,512]{1,0:T(8,128)(2,1)}, bf16[384,512]{1,0:T(8,128)(2,1)S(1)}, u32[]{:S(2)}, u32[]{:S(2)}) collective-permute-start(bf16[384,512]{1,0:T(8,128)(2,1)} %get-tuple-element.46), channel_id=1, source_target_pairs={{0,2},{2,0},{1,3},{3,1},{4,6},{6,4},{5,7},{7,5},{8,10},{10,8},{9,1... | collective-permute-start | bytes 1179656 | tf_op jit(solution)/shard_map/ppermute | solution.py:198
  167.2 13.9 %collective-permute-start.23 = (bf16[384,512]{1,0:T(8,128)(2,1)S(1)}, bf16[384,512]{1,0:T(8,128)(2,1)S(1)}, u32[]{:S(2)}, u32[]{:S(2)}) collective-permute-start(bf16[384,512]{1,0:T(8,128)(2,1)S(1)} %add_convert_fusion.2), channel_id=1, source_target_pairs={{0,4},{4,8},{8,12},{12,0},{1,5},{5,9},{9,13},{13,1},{2,6},{6,10},{... | collective-permute-start | bytes 1179656 | tf_op jit(solution)/shard_map/ppermute | solution.py:198
  172.4 14.6 %collective-permute-start.26 = (bf16[384,512]{1,0:T(8,128)(2,1)S(1)}, bf16[384,512]{1,0:T(8,128)(2,1)S(1)}, u32[]{:S(2)}, u32[]{:S(2)}) collective-permute-start(bf16[384,512]{1,0:T(8,128)(2,1)S(1)} %add_convert_fusion.1), channel_id=1, source_target_pairs={{0,12},{4,0},{8,4},{12,8},{1,13},{5,1},{9,5},{13,9},{2,14},{6,2},{... | collective-permute-start | bytes 1179656 | tf_op jit(solution)/shard_map/ppermute | solution.py:198
where the time goes:
time: 190 us; the launch traced here: 189 us
  waiting for transfers between devices  75.6 us (40%)
  starting transfers between devices  43.4 us (23%)
  Pallas kernels  28.3 us (15%)
  blocking collectives  15.5 us (8%)
  matrix products  10.4 us (5%)
  other arithmetic  10 us (5%)
  local copies, waits for them, and re-layouts  5.17 us (3%)
    ppermute x22, waiting for transfers between devices, shift(): lax.ppermute(value, axis, [(i, (i + by) % size) for i in range(size)])  41 us
    ppermute x22, starting transfers between devices, shift(): lax.ppermute(value, axis, [(i, (i + by) % size) for i in range(size)])  26.1 us
    all_to_all x1, blocking collectives, shards(): lax.all_to_all(context, ADP, split_axis=0, concat_axis=0, tiled=True)  15.5 us
    pallas_call x2, Pallas kernels, project(): pl.pallas_call(kernel, grid_spec=pltpu.PrefetchScalarGridSpec(num_scalar_...  13.8 us
    all_to_all x1, waiting for transfers between devices, shards(): lax.all_to_all(query, ADP, split_axis=0, concat_axis=1, tiled=True)  12 us
    ppermute x1, waiting for transfers between devices, gather_features(): from_above = lax.ppermute(above, 'z', [(2, 1), (1, 0)])  11.9 us
    pallas_call x2, Pallas kernels, output_partial(): pl.pallas_call(kernel, grid_spec=pltpu.PrefetchScalarGridSpec(num_scalar_...  10.9 us
    ppermute x1, waiting for transfers between devices, shards(): lax.ppermute(up, 'rep', [(i, i ^ 1) for i in range(lax.axis_size('rep'))])  7.46 us
  transfers between devices with their start and end apart: 29, of which 17 were waited for; matrix products, arithmetic and copies ran while one was open for 11% of the time, Pallas kernels for 7%

commit v1 on v0

--- a/solution.py
+++ b/solution.py
@@ -227,8 +227,9 @@
     above_side = shift(above, "y", 1)
     from_above = lax.ppermute(above, "z", [(2, 1), (1, 0)])
     sums = begin([tokens, side, below, above])
+    from_below, from_above, sums = lax.optimization_barrier((from_below, from_above, sums))
     two = jnp.where(z >= 2, from_below, from_above)
-    two, _, up = lax.optimization_barrier((two, below_side, up))
+    two, _, above_side, up = lax.optimization_barrier((two, below_side, above_side, up))
     return sums, [below_side, above_side, two, shift(two, "y", 1)], up
 
 

time: 190 us -> 188 us (0.989)
  waiting for transfers between devices: 75.6 us -> 72.4 us
  starting transfers between devices: 43.4 us -> 45.4 us
    ppermute x1, waiting for transfers between devices: 11.9 us -> 3.32 us  [gather_features(): from_above = lax.ppermute(above, 'z', [(2, 1), (1, 0)])]
    ppermute x22, waiting for transfers between devices: 41 us -> 45.2 us  [shift(): lax.ppermute(value, axis, [(i, (i + by) % size) for i in range(size)])]
    ppermute x22, starting transfers between devices: 26.1 us -> 28 us  [shift(): lax.ppermute(value, axis, [(i, (i + by) % size) for i in range(size)])]
  transfers between devices with their start and end apart: 29 -> 29, of which waited for: 17 -> 16; matrix products, arithmetic and copies ran while one was open for 11% -> 11% of each run, Pallas kernels for 7% -> 8%
where the time goes in v1:
time: 188 us; the launch traced here: 187 us
  waiting for transfers between devices  72.4 us (39%)
  starting transfers between devices  45.4 us (24%)
  Pallas kernels  28.3 us (15%)
  blocking collectives  15.5 us (8%)
  matrix products  10.4 us (6%)
  other arithmetic  8.73 us (5%)
  local copies, waits for them, and re-layouts  5.89 us (3%)
    ppermute x22, waiting for transfers between devices, shift(): lax.ppermute(value, axis, [(i, (i + by) % size) for i in range(size)])  45.2 us
    ppermute x22, starting transfers between devices, shift(): lax.ppermute(value, axis, [(i, (i + by) % size) for i in range(size)])  28 us
    all_to_all x1, blocking collectives, shards(): lax.all_to_all(context, ADP, split_axis=0, concat_axis=0, tiled=True)  15.5 us
    pallas_call x2, Pallas kernels, project(): pl.pallas_call(kernel, grid_spec=pltpu.PrefetchScalarGridSpec(num_scalar_...  13.8 us
    all_to_all x1, waiting for transfers between devices, shards(): lax.all_to_all(query, ADP, split_axis=0, concat_axis=1, tiled=True)  12 us
    pallas_call x2, Pallas kernels, output_partial(): pl.pallas_call(kernel, grid_spec=pltpu.PrefetchScalarGridSpec(num_scalar_...  10.9 us
    ppermute x1, waiting for transfers between devices, shards(): lax.ppermute(up, 'rep', [(i, i ^ 1) for i in range(lax.axis_size('rep'))])  8.54 us
    all_to_all x1, starting transfers between devices, shards(): lax.all_to_all(query, ADP, split_axis=0, concat_axis=1, tiled=True)  5.76 us
  transfers between devices with their start and end apart: 29, of which 16 were waited for; matrix products, arithmetic and copies ran while one was open for 11% of the time, Pallas kernels for 8%

profile of v1, /device:TPU:0, one launch (start us, length us, event | category | flops | bytes accessed | tf_op | source)
XLA Modules:
  0.0 187.1 jit_solution(3887667589537530467)
XLA Ops:
  0.0 0.5 collective-permute-start.6
  0.5 2.6 %collective-permute-start = (bf16[384,512]{1,0:T(8,128)(2,1)}, bf16[384,512]{1,0:T(8,128)(2,1)S(1)}, u32[]{:S(2)}, u32[]{:S(2)}) collective-permute-start(bf16[384,512]{1,0:T(8,128)(2,1)} %refs_0_.1), channel_id=1, source_target_pairs={{0,4},{4,8},{8,12},{12,0},{1,5},{5,9},{9,13},{13,1},{2,6},{6,10},{... | collective-permute-start | bytes 1179656 | tf_op jit(solution)/shard_map/ppermute | solution.py:198
  3.1 1.5 collective-permute-start.1
  4.6 2.2 %collective-permute-start.4 = (bf16[384,512]{1,0:T(8,128)(2,1)}, bf16[384,512]{1,0:T(8,128)(2,1)S(1)}, u32[]{:S(2)}, u32[]{:S(2)}) collective-permute-start(bf16[384,512]{1,0:T(8,128)(2,1)} %refs_0_.1), channel_id=1, source_target_pairs={{0,12},{4,0},{8,4},{12,8},{1,13},{5,1},{9,5},{13,9},{2,14},{6,2},{... | collective-permute-start | bytes 1179656 | tf_op jit(solution)/shard_map/ppermute | solution.py:198
  7.1 1.1 copy.36
  8.2 3.6 %all-to-all-start = ((bf16[32,16,512]{2,0,1:T(8,128)(2,1)}), bf16[32,16,512]{2,0,1:T(8,128)(2,1)S(1)}, u32[]{:S(2)}, u32[]{:S(2)}) async-start(bf16[32,16,512]{2,0,1:T(8,128)(2,1)} %copy.36), calls=%async_computation | async-start | bytes 1048576 | tf_op jit(solution)/shard_map/all_to_all | solution.py:295
  11.7 13.2 %collective-permute-done.4.refs_3_ = bf16[384,512]{1,0:T(8,128)(2,1)S(1)} collective-permute-done((bf16[384,512]{1,0:T(8,128)(2,1)}, bf16[384,512]{1,0:T(8,128)(2,1)S(1)}, u32[]{:S(2)}, u32[]{:S(2)}) %collective-permute-start.4) | collective-permute-done | bytes 393248 | tf_op jit(solution)/shard_map/ppermute | solution.py:198
  25.0 1.3 collective-permute-start.5
  26.3 1.5 collective-permute-start.3
  27.8 0.6 stack.43.places
  28.4 0.7 collective-permute-start.8
  29.1 1.3 collective-permute-start.7
  30.4 6.6 %shard_map.118 = (f32[384,512]{1,0:T(8,128)}, f32[384,512]{1,0:T(8,128)}, f32[384,128]{1,0:T(8,128)}) custom-call(s32[16]{0:T(128)} %stack.43.places, bf16[384,512]{1,0:T(8,128)(2,1)} %refs_0_.1, bf16[384,512]{1,0:T(8,128)(2,1)} %copy-done.11, bf16[384,512]{1,0:T(8,128)(2,1)} %copy-done.9, bf16[384,512]{1,0:T(8,128)(2,1)} %copy-done.10, ...), custom_call_target="tpu_custom_call" | custom-call | flops 1811939328 | bytes 7340032 | tf_op jit(solution)/shard_map/pallas_call | solution.py:64
  37.0 3.3 %collective-permute-done.5 = bf16[384,512]{1,0:T(8,128)(2,1)S(1)} collective-permute-done((bf16[384,512]{1,0:T(8,128)(2,1)S(1)}, bf16[384,512]{1,0:T(8,128)(2,1)S(1)}, u32[]{:S(2)}, u32[]{:S(2)}) %collective-permute-start.5) | collective-permute-done | bytes 393248 | tf_op jit(solution)/shard_map/ppermute | solution.py:228
  40.3 0.7 copy-done.13
  41.1 1.0 broadcast_select_fusion.refs_2_
  42.2 6.0 %collective-permute-done.7.refs_0_ = bf16[384,512]{1,0:T(8,128)(2,1)} collective-permute-done((bf16[384,512]{1,0:T(8,128)(2,1)S(1)}, bf16[384,512]{1,0:T(8,128)(2,1)}, u32[]{:S(2)}, u32[]{:S(2)}) %collective-permute-start.7) | collective-permute-done | bytes 393248 | tf_op jit(solution)/shard_map/ppermute | solution.py:198
  48.2 1.6 collective-permute-start.9
  49.8 0.8 collective-permute-start.10
  50.7 0.8 broadcast_in_dim.46.refs_23_.slot
  51.5 8.5 %collective-permute-done.9.up_other = bf16[512,512]{1,0:T(8,128)(2,1)S(1)} collective-permute-done((bf16[512,512]{1,0:T(8,128)(2,1)S(1)}, bf16[512,512]{1,0:T(8,128)(2,1)S(1)}, u32[]{:S(2)}, u32[]{:S(2)}) %collective-permute-start.9) | collective-permute-done | bytes 524320 | tf_op jit(solution)/shard_map/ppermute | solution.py:299
  60.0 0.8 copy-done.12
  60.8 7.2 %shard_map.119 = (f32[384,512]{1,0:T(8,128)}, f32[384,512]{1,0:T(8,128)}, f32[192,128]{1,0:T(8,128)}) custom-call(s32[16]{0:T(128)} %stack.43.places, bf16[384,512]{1,0:T(8,128)(2,1)} %collective-permute-done.7.refs_0_, bf16[384,512]{1,0:T(8,128)(2,1)} %collective-permute-done.8.refs_1_, bf16[384,512]{1,0:T(8,128)(2,1)} %copy-done.5, ...), custom_call_target="tpu_custom_call" | custom-call | flops 1811939328 | bytes 7340032 | tf_op jit(solution)/shard_map/pallas_call | solution.py:64
  68.1 0.5 collective-permute-start.11
  68.6 2.1 %collective-permute-done.11 = f32[192,128]{1,0:T(8,128)S(1)} collective-permute-done((f32[192,128]{1,0:T(8,128)}, f32[192,128]{1,0:T(8,128)S(1)}, u32[]{:S(2)}, u32[]{:S(2)}) %collective-permute-start.11) | collective-permute-done | bytes 98336 | tf_op jit(solution)/shard_map/ppermute | solution.py:198
  70.8 0.9 add_convert_fusion.4
  71.7 1.8 collective-permute-start.12
  73.5 2.4 %collective-permute-done.12 = bf16[192,128]{1,0:T(8,128)(2,1)S(1)} collective-permute-done((bf16[192,128]{1,0:T(8,128)(2,1)S(1)}, bf16[192,128]{1,0:T(8,128)(2,1)S(1)}, u32[]{:S(2)}, u32[]{:S(2)}) %collective-permute-start.12) | collective-permute-done | bytes 49184 | tf_op jit(solution)/shard_map/ppermute | solution.py:198
  75.9 3.6 %collective-permute-start.14 = (bf16[192,128]{1,0:T(8,128)(2,1)S(1)}, bf16[192,128]{1,0:T(8,128)(2,1)S(1)}, u32[]{:S(2)}, u32[]{:S(2)}) collective-permute-start(bf16[192,128]{1,0:T(8,128)(2,1)S(1)} %add.217), channel_id=1, source_target_pairs={{0,4},{4,8},{8,12},{12,0},{1,5},{5,9},{9,13},{13,1},{2,6},{6,10},{... | collective-permute-start | bytes 147464 | tf_op jit(solution)/shard_map/ppermute | solution.py:198
  79.5 0.4 collective-permute-start.15
  79.9 2.8 %collective-permute-start.16 = (bf16[192,128]{1,0:T(8,128)(2,1)S(1)}, bf16[192,128]{1,0:T(8,128)(2,1)S(1)}, u32[]{:S(2)}, u32[]{:S(2)}) collective-permute-start(bf16[192,128]{1,0:T(8,128)(2,1)S(1)} %add.217), channel_id=1, source_target_pairs={{0,12},{4,0},{8,4},{12,8},{1,13},{5,1},{9,5},{13,9},{2,14},{6,2},{... | collective-permute-start | bytes 147464 | tf_op jit(solution)/shard_map/ppermute | solution.py:198
  82.8 2.2 %collective-permute-done.15 = bf16[192,128]{1,0:T(8,128)(2,1)S(1)} collective-permute-done((bf16[192,128]{1,0:T(8,128)(2,1)S(1)}, bf16[192,128]{1,0:T(8,128)(2,1)S(1)}, u32[]{:S(2)}, u32[]{:S(2)}) %collective-permute-start.15) | collective-permute-done | bytes 49184 | tf_op jit(solution)/shard_map/ppermute | solution.py:198
  85.0 0.6 add_add_fusion.low
  85.7 3.6 %shard_map.120 = bf16[384,512]{1,0:T(8,128)(2,1)} custom-call(s32[1]{0:T(128)} %bitcast.8.half, f32[384,512]{1,0:T(8,128)} %get-tuple-element.50.own, f32[384,512]{1,0:T(8,128)} %copy-done.7, bf16[192,128]{1,0:T(8,128)(2,1)} %add_add_fusion.low, s32[384,1]{1,0:T(8,128)} %broadcast_in_dim.46.refs_23_.slot, bf16[512,512]{1,0:T(8,128)(2,1)} %bitcast.52, ...), custom_call_target="tpu_custom_call" | custom-call | flops 1 | bytes 1 | tf_op jit(solution)/shard_map/pallas_call | solution.py:119
  89.3 5.8 %all-to-all-start.1 = ((bf16[16,24,512]{2,1,0:T(8,128)(2,1)}), bf16[16,24,512]{2,1,0:T(8,128)(2,1)S(1)}, u32[]{:S(2)}, u32[]{:S(2)}) async-start(bf16[16,24,512]{2,1,0:T(8,128)(2,1)} %bitcast.55), calls=%async_computation.1 | async-start | bytes 786432 | tf_op jit(solution)/shard_map/all_to_all | solution.py:314
  95.2 12.0 %all-to-all-done.1 = bf16[16,24,512]{2,1,0:T(8,128)(2,1)S(1)} async-done(((bf16[16,24,512]{2,1,0:T(8,128)(2,1)}), bf16[16,24,512]{2,1,0:T(8,128)(2,1)S(1)}, u32[]{:S(2)}, u32[]{:S(2)}) %all-to-all-start.1) | async-done | bytes 393248 | tf_op jit(solution)/shard_map/all_to_all | solution.py:314
  107.6 0.3 fusion.10
  107.9 5.5 %fusion.15 = (f32[8,24,8]{2,1,0:T(8,128)S(1)}, f32[8,24,8,128]{3,2,1,0:T(8,128)S(1)}) fusion(bf16[8,24,128,128]{3,2,1,0:T(8,128)(2,1)} %param.19, bf16[24,8,8,128]{3,2,1,0:T(8,128)(2,1)S(1)} %reshape.48, pred[24,128]{1,0:T(8,128)(4,1)S(1)} %iota_compare_fusion.1), kind=kOutput, calls=%fused_computation.30 | convolution fusion | flops 50723328 | bytes 7480320 | tf_op jit(solution)/shard_map/rkge,krje->krgj/dot_general | solution.py:182
  113.5 0.5 fusion.8
  114.1 4.6 %fusion.5 = bf16[24,8,8,128]{3,2,1,0:T(8,128)(2,1)S(1)} fusion(bf16[8,24,128,128]{3,2,1,0:T(8,128)(2,1)} %param.20, f32[24,8,128]{2,1,0:T(8,128)S(1)} %bitcast.58, f32[24,8,8]{2,1,0:T(8,128)S(1)} %copy.43, f32[8,24,8,128]{3,2,1,0:T(8,128)S(1)} %get-tuple-element.70, f32[8,24,8]{2,1,0:T(8,128)S(1)} %get-tuple-element.68, f32[8,24,8]{2,1,0:T(8,128)S(1)} %max.3, ...), kind=kOutput, calls=%fused_computation.4 | convolution fusion | flops 51707904 | bytes 7590912 | tf_op jit(solution)/shard_map/krgj,krje->rkge/dot_general | solution.py:191
  119.2 15.5 %all_to_all.40 = bf16[16,24,512]{2,1,0:T(8,128)(2,1)S(1)} all-to-all(bf16[16,24,512]{2,1,0:T(8,128)(2,1)S(1)} %bitcast.54), channel_id=1, replica_groups=mesh['rep'=2,'z'=4,'y'=2,'core'=2] {'z','y','core'}, dimensions={0} | all-to-all | bytes 786432 | tf_op jit(solution)/shard_map/all_to_all | solution.py:320
  134.8 1.6 collective-permute-done.17.refs_1_
  136.4 0.8 copy-done.6
  137.2 3.4 %shard_map.122 = bf16[384,512]{1,0:T(8,128)(2,1)} custom-call(s32[16]{0:T(128)} %stack.43.places, bf16[384,512]{1,0:T(8,128)(2,1)} %bitcast.47, bf16[384,512]{1,0:T(8,128)(2,1)} %copy-done.6, bf16[512,8192]{1,0:T(8,128)(2,1)} %refs_2_.3, bf16[512,8192]{1,0:T(8,128)(2,1)} %collective-permute-done.18.refs_9_.refs_10_.refs_11_.refs_12_.refs_13_.refs_14_.refs_15_.refs_3_), custom_call_target="tpu_custom_call" | custom-call | flops 1 | bytes 1 | tf_op jit(solution)/shard_map/pallas_call | solution.py:160
  140.7 0.6 collective-permute-start.21
  141.3 7.5 %shard_map.121 = (bf16[384,512]{1,0:T(8,128)(2,1)}, bf16[384,512]{1,0:T(8,128)(2,1)}, bf16[384,512]{1,0:T(8,128)(2,1)}, bf16[384,512]{1,0:T(8,128)(2,1)}, bf16[3...) custom-call(s32[16]{0:T(128)} %stack.43.places, bf16[384,512]{1,0:T(8,128)(2,1)} %bitcast.48, ...), custom_call_target="tpu_custom_call" | custom-call | flops 1 | bytes 1 | tf_op jit(solution)/shard_map/pallas_call | solution.py:160
  148.7 1.5 collective-permute-start.20
  150.2 2.1 %collective-permute-done.21 = bf16[384,512]{1,0:T(8,128)(2,1)S(1)} collective-permute-done((bf16[384,512]{1,0:T(8,128)(2,1)}, bf16[384,512]{1,0:T(8,128)(2,1)S(1)}, u32[]{:S(2)}, u32[]{:S(2)}) %collective-permute-start.21) | collective-permute-done | bytes 393248 | tf_op jit(solution)/shard_map/ppermute | solution.py:198
  152.3 1.1 add_convert_fusion.3
  153.4 3.1 %collective-permute-start.22 = (bf16[384,512]{1,0:T(8,128)(2,1)S(1)}, bf16[384,512]{1,0:T(8,128)(2,1)S(1)}, u32[]{:S(2)}, u32[]{:S(2)}) collective-permute-start(bf16[384,512]{1,0:T(8,128)(2,1)S(1)} %add_convert_fusion.3), channel_id=1, source_target_pairs={{0,4},{4,8},{1,5},{5,9},{2,6},{6,10},{3,7},{7,11},{16,20},{20,24},... | collective-permute-start | bytes 1179656 | tf_op jit(solution)/shard_map/ppermute | solution.py:243
  156.5 0.6 collective-permute-start.24
  157.1 0.7 collective-permute-start.25
  157.8 1.5 collective-permute-start.19
  159.3 1.7 collective-permute-done.20
  161.0 3.3 %collective-permute-done.22 = bf16[384,512]{1,0:T(8,128)(2,1)S(1)} collective-permute-done((bf16[384,512]{1,0:T(8,128)(2,1)S(1)}, bf16[384,512]{1,0:T(8,128)(2,1)S(1)}, u32[]{:S(2)}, u32[]{:S(2)}) %collective-permute-start.22) | collective-permute-done | bytes 393248 | tf_op jit(solution)/shard_map/ppermute | solution.py:243
  164.2 1.1 add_convert_fusion.2
  165.4 2.5 %collective-permute-start.23 = (bf16[384,512]{1,0:T(8,128)(2,1)S(1)}, bf16[384,512]{1,0:T(8,128)(2,1)S(1)}, u32[]{:S(2)}, u32[]{:S(2)}) collective-permute-start(bf16[384,512]{1,0:T(8,128)(2,1)S(1)} %add_convert_fusion.2), channel_id=1, source_target_pairs={{0,4},{4,8},{8,12},{12,0},{1,5},{5,9},{9,13},{13,1},{2,6},{6,10},{... | collective-permute-start | bytes 1179656 | tf_op jit(solution)/shard_map/ppermute | solution.py:198
  167.9 1.5 collective-permute-done.24
  169.4 1.1 add_convert_fusion.1
  170.6 2.2 %collective-permute-start.26 = (bf16[384,512]{1,0:T(8,128)(2,1)S(1)}, bf16[384,512]{1,0:T(8,128)(2,1)S(1)}, u32[]{:S(2)}, u32[]{:S(2)}) collective-permute-start(bf16[384,512]{1,0:T(8,128)(2,1)S(1)} %add_convert_fusion.1), channel_id=1, source_target_pairs={{0,12},{4,0},{8,4},{12,8},{1,13},{5,1},{9,5},{13,9},{2,14},{6,2},{... | collective-permute-start | bytes 1179656 | tf_op jit(solution)/shard_map/ppermute | solution.py:198
  172.7 4.6 %collective-permute-done.19 = bf16[384,512]{1,0:T(8,128)(2,1)S(1)} collective-permute-done((bf16[384,512]{1,0:T(8,128)(2,1)}, bf16[384,512]{1,0:T(8,128)(2,1)S(1)}, u32[]{:S(2)}, u32[]{:S(2)}) %collective-permute-start.19) | collective-permute-done | bytes 393248 | tf_op jit(solution)/shard_map/ppermute | solution.py:198
  177.3 2.0 %collective-permute-done.23 = bf16[384,512]{1,0:T(8,128)(2,1)S(1)} collective-permute-done((bf16[384,512]{1,0:T(8,128)(2,1)S(1)}, bf16[384,512]{1,0:T(8,128)(2,1)S(1)}, u32[]{:S(2)}, u32[]{:S(2)}) %collective-permute-start.23) | collective-permute-done | bytes 393248 | tf_op jit(solution)/shard_map/ppermute | solution.py:198
  179.3 5.8 %collective-permute-done.26 = bf16[384,512]{1,0:T(8,128)(2,1)S(1)} collective-permute-done((bf16[384,512]{1,0:T(8,128)(2,1)S(1)}, bf16[384,512]{1,0:T(8,128)(2,1)S(1)}, u32[]{:S(2)}, u32[]{:S(2)}) %collective-permute-start.26) | collective-permute-done | bytes 393248 | tf_op jit(solution)/shard_map/ppermute | solution.py:198
  185.1 1.9 %add_convert_fusion = bf16[384,512]{1,0:T(8,128)(2,1)} fusion(bf16[384,512]{1,0:T(8,128)(2,1)S(1)} %collective-permute-done.26, bf16[384,512]{1,0:T(8,128)(2,1)S(1)} %collective-permute-done.23, bf16[384,512]{1,0:T(8,128)(2,1)S(1)} %collective-permute-done.19, bf16[384,512]{1,0:T(8,128)(2,1)} %get-tuple-element.57), kind=kLoop, calls=%fused_computation.5 | loop fusion | flops 1572864 | bytes 1966080 | tf_op jit(solution)/shard_map/convert_element_type | solution.py:343
  (68 shorter events, 1.6 us)
Async XLA Ops:
  0.0 6.9 %copy-start = (bf16[1,8192,64]{1,2,0:T(8,128)(2,1)S(1)}, bf16[1,8192,64]{1,2,0:T(8,128)(2,1)}, u32[]{:S(2)}) copy-start(bf16[1,8192,64]{1,2,0:T(8,128)(2,1)} %param.18) | copy-start | bytes 3145732
  0.0 30.4 %collective-permute-start.6 = (bf16[8192,512]{1,0:T(8,128)(2,1)}, bf16[8192,512]{1,0:T(8,128)(2,1)}, u32[]{:S(2)}, u32[]{:S(2)}) collective-permute-start(bf16[8192,512]{1,0:T(8,128)(2,1)} %refs_7_.4), channel_id=1, source_target_pairs={{0,1},{1,0},{2,3},{3,2},{4,5},{5,4},{6,7},{7,6},{8,9},{9,8},{10,11... | collective-permute-start | bytes 25165832 | tf_op jit(solution)/shard_map/ppermute | solution.py:198
  0.5 25.8 %collective-permute-start = (bf16[384,512]{1,0:T(8,128)(2,1)}, bf16[384,512]{1,0:T(8,128)(2,1)S(1)}, u32[]{:S(2)}, u32[]{:S(2)}) collective-permute-start(bf16[384,512]{1,0:T(8,128)(2,1)} %refs_0_.1), channel_id=1, source_target_pairs={{0,4},{4,8},{8,12},{12,0},{1,5},{5,9},{9,13},{13,1},{2,6},{6,10},{... | collective-permute-start | bytes 1179656 | tf_op jit(solution)/shard_map/ppermute | solution.py:198
  3.1 23.2 %collective-permute-start.1 = (bf16[384,512]{1,0:T(8,128)(2,1)}, bf16[384,512]{1,0:T(8,128)(2,1)S(1)}, u32[]{:S(2)}, u32[]{:S(2)}) collective-permute-start(bf16[384,512]{1,0:T(8,128)(2,1)} %refs_0_.1), channel_id=1, source_target_pairs={{0,2},{2,0},{1,3},{3,1},{4,6},{6,4},{5,7},{7,5},{8,10},{10,8},{9,1... | collective-permute-start | bytes 1179656 | tf_op jit(solution)/shard_map/ppermute | solution.py:198
  4.6 20.4 %collective-permute-start.4 = (bf16[384,512]{1,0:T(8,128)(2,1)}, bf16[384,512]{1,0:T(8,128)(2,1)S(1)}, u32[]{:S(2)}, u32[]{:S(2)}) collective-permute-start(bf16[384,512]{1,0:T(8,128)(2,1)} %refs_0_.1), channel_id=1, source_target_pairs={{0,12},{4,0},{8,4},{12,8},{1,13},{5,1},{9,5},{13,9},{2,14},{6,2},{... | collective-permute-start | bytes 1179656 | tf_op jit(solution)/shard_map/ppermute | solution.py:198
  6.9 19.4 %collective-permute-start.2 = (bf16[1,64,8192]{2,1,0:T(8,128)(2,1)}, bf16[1,64,8192]{2,1,0:T(8,128)(2,1)S(1)}, u32[]{:S(2)}, u32[]{:S(2)}) collective-permute-start(bf16[1,64,8192]{2,1,0:T(8,128)(2,1)} %bitcast.37), channel_id=1, source_target_pairs={{0,1},{1,0},{2,3},{3,2},{4,5},{5,4},{6,7},{7,6},{8,9},{9,8},{10,11... | collective-permute-start | bytes 3145736 | tf_op jit(solution)/shard_map/ppermute | solution.py:198
  8.2 34.0 %all-to-all-start = ((bf16[32,16,512]{2,0,1:T(8,128)(2,1)}), bf16[32,16,512]{2,0,1:T(8,128)(2,1)S(1)}, u32[]{:S(2)}, u32[]{:S(2)}) async-start(bf16[32,16,512]{2,0,1:T(8,128)(2,1)} %copy.36), calls=%async_computation | async-start | bytes 1048576 | tf_op jit(solution)/shard_map/all_to_all | solution.py:295
  25.0 5.4 %copy-start.10 = (bf16[384,512]{1,0:T(8,128)(2,1)}, bf16[384,512]{1,0:T(8,128)(2,1)S(1)}, u32[]{:S(2)}) copy-start(bf16[384,512]{1,0:T(8,128)(2,1)S(1)} %collective-permute-done.4.refs_3_) | copy-start | bytes 1179652
  25.0 15.4 %collective-permute-start.5 = (bf16[384,512]{1,0:T(8,128)(2,1)S(1)}, bf16[384,512]{1,0:T(8,128)(2,1)S(1)}, u32[]{:S(2)}, u32[]{:S(2)}) collective-permute-start(bf16[384,512]{1,0:T(8,128)(2,1)S(1)} %collective-permute-done.4.refs_3_), channel_id=1, source_target_pairs={{8,4},{4,0},{9,5},{5,1},{10,6},{6,2},{11,7},{7,3},{24,20},{20,16},... | collective-permute-start | bytes 1179656 | tf_op jit(solution)/shard_map/ppermute | solution.py:228
  26.3 4.1 %copy-start.9 = (bf16[384,512]{1,0:T(8,128)(2,1)}, bf16[384,512]{1,0:T(8,128)(2,1)S(1)}, u32[]{:S(2)}) copy-start(bf16[384,512]{1,0:T(8,128)(2,1)S(1)} %collective-permute-done.refs_2_) | copy-start | bytes 1179652
  26.3 4.1 %copy-start.11 = (bf16[384,512]{1,0:T(8,128)(2,1)}, bf16[384,512]{1,0:T(8,128)(2,1)S(1)}, u32[]{:S(2)}) copy-start(bf16[384,512]{1,0:T(8,128)(2,1)S(1)} %collective-permute-done.1.refs_1_) | copy-start | bytes 1179652
  26.3 4.1 %copy-start.2 = (bf16[1,64,8192]{2,1,0:T(8,128)(2,1)}, bf16[1,64,8192]{2,1,0:T(8,128)(2,1)S(1)}, u32[]{:S(2)}) copy-start(bf16[1,64,8192]{2,1,0:T(8,128)(2,1)S(1)} %collective-permute-done.2.refs_16_.refs_17_.refs_18_.refs_19_) | copy-start | bytes 3145732
  26.3 14.0 %collective-permute-start.3 = (bf16[384,512]{1,0:T(8,128)(2,1)S(1)}, bf16[384,512]{1,0:T(8,128)(2,1)}, u32[]{:S(2)}, u32[]{:S(2)}) collective-permute-start(bf16[384,512]{1,0:T(8,128)(2,1)S(1)} %collective-permute-done.refs_2_), channel_id=1, source_target_pairs={{4,8},{8,12},{5,9},{9,13},{6,10},{10,14},{7,11},{11,15},{20,24},{2... | collective-permute-start | bytes 1179656 | tf_op jit(solution)/shard_map/ppermute | solution.py:226
  28.4 22.2 %copy-start.16 = (s32[384,1]{0,1:T(1,128)S(1)}, s32[384,1]{0,1:T(1,128)}, u32[]{:S(2)}) copy-start(s32[384,1]{0,1:T(1,128)} %param.13) | copy-start | bytes 4612
  28.4 22.2 %copy-start.17 = (s32[16]{0:T(128)S(1)}, s32[16]{0:T(128)}, u32[]{:S(2)}) copy-start(s32[16]{0:T(128)} %param.14) | copy-start | bytes 196
  28.4 13.8 %collective-permute-start.8 = (bf16[384,512]{1,0:T(8,128)(2,1)S(1)}, bf16[384,512]{1,0:T(8,128)(2,1)}, u32[]{:S(2)}, u32[]{:S(2)}) collective-permute-start(bf16[384,512]{1,0:T(8,128)(2,1)S(1)} %collective-permute-done.4.refs_3_), channel_id=1, source_target_pairs={{0,2},{2,0},{1,3},{3,1},{4,6},{6,4},{5,7},{7,5},{8,10},{10,8},{9,1... | collective-permute-start | bytes 1179656 | tf_op jit(solution)/shard_map/ppermute | solution.py:198
  29.1 19.1 %collective-permute-start.7 = (bf16[384,512]{1,0:T(8,128)(2,1)S(1)}, bf16[384,512]{1,0:T(8,128)(2,1)}, u32[]{:S(2)}, u32[]{:S(2)}) collective-permute-start(bf16[384,512]{1,0:T(8,128)(2,1)S(1)} %collective-permute-done.refs_2_), channel_id=1, source_target_pairs={{0,2},{2,0},{1,3},{3,1},{4,6},{6,4},{5,7},{7,5},{8,10},{10,8},{9,1... | collective-permute-start | bytes 1179656 | tf_op jit(solution)/shard_map/ppermute | solution.py:198
  40.3 0.7 copy-start.13
  42.1 17.9 %copy-start.5 = (bf16[384,512]{1,0:T(8,128)(2,1)}, bf16[384,512]{1,0:T(8,128)(2,1)S(1)}, u32[]{:S(2)}) copy-start(bf16[384,512]{1,0:T(8,128)(2,1)S(1)} %broadcast_select_fusion.refs_2_) | copy-start | bytes 1179652
  42.2 25.9 %copy-start.4 = (bf16[32,16,512]{2,0,1:T(8,128)(2,1)}, bf16[32,16,512]{2,0,1:T(8,128)(2,1)S(1)}, u32[]{:S(2)}) copy-start(bf16[32,16,512]{2,0,1:T(8,128)(2,1)S(1)} %all-to-all-done) | copy-start | bytes 1572868
  48.2 11.8 %collective-permute-start.9 = (bf16[512,512]{1,0:T(8,128)(2,1)S(1)}, bf16[512,512]{1,0:T(8,128)(2,1)S(1)}, u32[]{:S(2)}, u32[]{:S(2)}) collective-permute-start(bf16[512,512]{1,0:T(8,128)(2,1)S(1)} %bitcast.51), channel_id=1, source_target_pairs={{0,16},{16,0},{1,17},{17,1},{2,18},{18,2},{3,19},{19,3},{4,20},{20... | collective-permute-start | bytes 1572872 | tf_op jit(solution)/shard_map/ppermute | solution.py:299
  49.8 10.3 %collective-permute-start.10 = (bf16[384,512]{1,0:T(8,128)(2,1)S(1)}, bf16[384,512]{1,0:T(8,128)(2,1)S(1)}, u32[]{:S(2)}, u32[]{:S(2)}) collective-permute-start(bf16[384,512]{1,0:T(8,128)(2,1)S(1)} %broadcast_select_fusion.refs_2_), channel_id=1, source_target_pairs={{0,2},{2,0},{1,3},{3,1},{4,6},{6,4},{5,7},{7,5},{8,10},{10,8},{9,1... | collective-permute-start | bytes 1179656 | tf_op jit(solution)/shard_map/ppermute | solution.py:198
  51.5 43.6 %copy-start.14 = (bf16[24,1024]{1,0:T(8,128)(2,1)S(1)}, bf16[24,1024]{1,0:T(8,128)(2,1)}, u32[]{:S(2)}) copy-start(bf16[24,1024]{1,0:T(8,128)(2,1)} %param.21) | copy-start | bytes 147460
  51.5 43.6 %copy-start.15 = (bf16[24,1024]{1,0:T(8,128)(2,1)S(1)}, bf16[24,1024]{1,0:T(8,128)(2,1)}, u32[]{:S(2)}) copy-start(bf16[24,1024]{1,0:T(8,128)(2,1)} %param.22) | copy-start | bytes 147460
  51.5 43.6 %copy-start.18 = (s32[24]{0:T(128)S(1)}, s32[24]{0:T(128)}, u32[]{:S(2)}) copy-start(s32[24]{0:T(128)} %param.15) | copy-start | bytes 292
  60.0 8.0 %copy-start.8 = (bf16[512,512]{1,0:T(8,128)(2,1)}, bf16[512,512]{1,0:T(8,128)(2,1)S(1)}, u32[]{:S(2)}) copy-start(bf16[512,512]{1,0:T(8,128)(2,1)S(1)} %collective-permute-done.9.up_other) | copy-start | bytes 1572868
  60.0 0.8 copy-start.12
  68.1 7.8 %collective-permute-start.13 = (f32[384,512]{1,0:T(8,128)}, f32[384,512]{1,0:T(8,128)S(1)}, u32[]{:S(2)}, u32[]{:S(2)}) collective-permute-start(f32[384,512]{1,0:T(8,128)} %get-tuple-element.52), channel_id=1, source_target_pairs={{0,1},{1,0},{2,3},{3,2},{4,5},{5,4},{6,7},{7,6},{8,9},{9,8},{10,11... | collective-permute-start | bytes 2359304 | tf_op jit(solution)/shard_map/ppermute | solution.py:198
  68.1 2.6 %collective-permute-start.11 = (f32[192,128]{1,0:T(8,128)}, f32[192,128]{1,0:T(8,128)S(1)}, u32[]{:S(2)}, u32[]{:S(2)}) collective-permute-start(f32[192,128]{1,0:T(8,128)} %get-tuple-element.51), channel_id=1, source_target_pairs={{0,1},{1,0},{2,3},{3,2},{4,5},{5,4},{6,7},{7,6},{8,9},{9,8},{10,11... | collective-permute-start | bytes 294920 | tf_op jit(solution)/shard_map/ppermute | solution.py:198
  71.7 4.2 %collective-permute-start.12 = (bf16[192,128]{1,0:T(8,128)(2,1)S(1)}, bf16[192,128]{1,0:T(8,128)(2,1)S(1)}, u32[]{:S(2)}, u32[]{:S(2)}) collective-permute-start(bf16[192,128]{1,0:T(8,128)(2,1)S(1)} %add_convert_fusion.4), channel_id=1, source_target_pairs={{0,2},{2,0},{1,3},{3,1},{4,6},{6,4},{5,7},{7,5},{8,10},{10,8},{9,1... | collective-permute-start | bytes 147464 | tf_op jit(solution)/shard_map/ppermute | solution.py:198
  75.9 9.8 %copy-start.7 = (f32[384,512]{1,0:T(8,128)}, f32[384,512]{1,0:T(8,128)S(1)}, u32[]{:S(2)}) copy-start(f32[384,512]{1,0:T(8,128)S(1)} %collective-permute-done.13.received) | copy-start | bytes 2359300
  75.9 6.9 %collective-permute-start.14 = (bf16[192,128]{1,0:T(8,128)(2,1)S(1)}, bf16[192,128]{1,0:T(8,128)(2,1)S(1)}, u32[]{:S(2)}, u32[]{:S(2)}) collective-permute-start(bf16[192,128]{1,0:T(8,128)(2,1)S(1)} %add.217), channel_id=1, source_target_pairs={{0,4},{4,8},{8,12},{12,0},{1,5},{5,9},{9,13},{13,1},{2,6},{6,10},{... | collective-permute-start | bytes 147464 | tf_op jit(solution)/shard_map/ppermute | solution.py:198
  79.5 5.5 %collective-permute-start.15 = (bf16[192,128]{1,0:T(8,128)(2,1)S(1)}, bf16[192,128]{1,0:T(8,128)(2,1)S(1)}, u32[]{:S(2)}, u32[]{:S(2)}) collective-permute-start(bf16[192,128]{1,0:T(8,128)(2,1)S(1)} %add.217), channel_id=1, source_target_pairs={{0,8},{4,12},{8,0},{12,4},{1,9},{5,13},{9,1},{13,5},{2,10},{6,14},... | collective-permute-start | bytes 147464 | tf_op jit(solution)/shard_map/ppermute | solution.py:198
  79.9 5.1 %collective-permute-start.16 = (bf16[192,128]{1,0:T(8,128)(2,1)S(1)}, bf16[192,128]{1,0:T(8,128)(2,1)S(1)}, u32[]{:S(2)}, u32[]{:S(2)}) collective-permute-start(bf16[192,128]{1,0:T(8,128)(2,1)S(1)} %add.217), channel_id=1, source_target_pairs={{0,12},{4,0},{8,4},{12,8},{1,13},{5,1},{9,5},{13,9},{2,14},{6,2},{... | collective-permute-start | bytes 147464 | tf_op jit(solution)/shard_map/ppermute | solution.py:198
  89.3 47.2 %collective-permute-start.18 = (bf16[512,8192]{1,0:T(8,128)(2,1)}, bf16[512,8192]{1,0:T(8,128)(2,1)}, u32[]{:S(2)}, u32[]{:S(2)}) collective-permute-start(bf16[512,8192]{1,0:T(8,128)(2,1)} %refs_2_.3), channel_id=1, source_target_pairs={{0,1},{1,0},{2,3},{3,2},{4,5},{5,4},{6,7},{7,6},{8,9},{9,8},{10,11... | collective-permute-start | bytes 25165832 | tf_op jit(solution)/shard_map/ppermute | solution.py:198
  89.3 18.0 %all-to-all-start.1 = ((bf16[16,24,512]{2,1,0:T(8,128)(2,1)}), bf16[16,24,512]{2,1,0:T(8,128)(2,1)S(1)}, u32[]{:S(2)}, u32[]{:S(2)}) async-start(bf16[16,24,512]{2,1,0:T(8,128)(2,1)} %bitcast.55), calls=%async_computation.1 | async-start | bytes 786432 | tf_op jit(solution)/shard_map/all_to_all | solution.py:314
  134.7 1.7 copy-start.3
  134.7 1.7 collective-permute-start.17
  136.4 0.8 copy-start.6
  140.7 11.7 %collective-permute-start.21 = (bf16[384,512]{1,0:T(8,128)(2,1)}, bf16[384,512]{1,0:T(8,128)(2,1)S(1)}, u32[]{:S(2)}, u32[]{:S(2)}) collective-permute-start(bf16[384,512]{1,0:T(8,128)(2,1)} %shard_map.122), channel_id=1, source_target_pairs={{0,2},{2,0},{1,3},{3,1},{4,6},{6,4},{5,7},{7,5},{8,10},{10,8},{9,1... | collective-permute-start | bytes 1179656 | tf_op jit(solution)/shard_map/ppermute | solution.py:198
  141.3 45.8 %copy-start.1 = (bf16[1,8192,64]{1,2,0:T(8,128)(2,1)S(1)}, bf16[1,8192,64]{1,2,0:T(8,128)(2,1)}, u32[]{:S(2)}) copy-start(bf16[1,8192,64]{1,2,0:T(8,128)(2,1)} %param.18) | copy-start | bytes 3145732
  148.7 12.2 %collective-permute-start.20 = (bf16[384,512]{1,0:T(8,128)(2,1)}, bf16[384,512]{1,0:T(8,128)(2,1)S(1)}, u32[]{:S(2)}, u32[]{:S(2)}) collective-permute-start(bf16[384,512]{1,0:T(8,128)(2,1)} %get-tuple-element.61), channel_id=1, source_target_pairs={{0,2},{2,0},{1,3},{3,1},{4,6},{6,4},{5,7},{7,5},{8,10},{10,8},{9,1... | collective-permute-start | bytes 1179656 | tf_op jit(solution)/shard_map/ppermute | solution.py:198
  153.4 10.8 %collective-permute-start.22 = (bf16[384,512]{1,0:T(8,128)(2,1)S(1)}, bf16[384,512]{1,0:T(8,128)(2,1)S(1)}, u32[]{:S(2)}, u32[]{:S(2)}) collective-permute-start(bf16[384,512]{1,0:T(8,128)(2,1)S(1)} %add_convert_fusion.3), channel_id=1, source_target_pairs={{0,4},{4,8},{1,5},{5,9},{2,6},{6,10},{3,7},{7,11},{16,20},{20,24},... | collective-permute-start | bytes 1179656 | tf_op jit(solution)/shard_map/ppermute | solution.py:243
  156.5 12.9 %collective-permute-start.24 = (bf16[384,512]{1,0:T(8,128)(2,1)}, bf16[384,512]{1,0:T(8,128)(2,1)S(1)}, u32[]{:S(2)}, u32[]{:S(2)}) collective-permute-start(bf16[384,512]{1,0:T(8,128)(2,1)} %get-tuple-element.66), channel_id=1, source_target_pairs={{0,2},{2,0},{1,3},{3,1},{4,6},{6,4},{5,7},{7,5},{8,10},{10,8},{9,1... | collective-permute-start | bytes 1179656 | tf_op jit(solution)/shard_map/ppermute | solution.py:198
  157.1 12.3 %collective-permute-start.25 = (bf16[384,512]{1,0:T(8,128)(2,1)S(1)}, bf16[384,512]{1,0:T(8,128)(2,1)S(1)}, u32[]{:S(2)}, u32[]{:S(2)}) collective-permute-start(bf16[384,512]{1,0:T(8,128)(2,1)S(1)} %add_convert_fusion.3), channel_id=1, source_target_pairs={{12,8},{8,4},{13,9},{9,5},{14,10},{10,6},{15,11},{11,7},{28,24},{2... | collective-permute-start | bytes 1179656 | tf_op jit(solution)/shard_map/ppermute | solution.py:244
  157.8 19.5 %collective-permute-start.19 = (bf16[384,512]{1,0:T(8,128)(2,1)}, bf16[384,512]{1,0:T(8,128)(2,1)S(1)}, u32[]{:S(2)}, u32[]{:S(2)}) collective-permute-start(bf16[384,512]{1,0:T(8,128)(2,1)} %get-tuple-element.58), channel_id=1, source_target_pairs={{0,2},{2,0},{1,3},{3,1},{4,6},{6,4},{5,7},{7,5},{8,10},{10,8},{9,1... | collective-permute-start | bytes 1179656 | tf_op jit(solution)/shard_map/ppermute | solution.py:198
  165.4 13.9 %collective-permute-start.23 = (bf16[384,512]{1,0:T(8,128)(2,1)S(1)}, bf16[384,512]{1,0:T(8,128)(2,1)S(1)}, u32[]{:S(2)}, u32[]{:S(2)}) collective-permute-start(bf16[384,512]{1,0:T(8,128)(2,1)S(1)} %add_convert_fusion.2), channel_id=1, source_target_pairs={{0,4},{4,8},{8,12},{12,0},{1,5},{5,9},{9,13},{13,1},{2,6},{6,10},{... | collective-permute-start | bytes 1179656 | tf_op jit(solution)/shard_map/ppermute | solution.py:198
  170.6 14.6 %collective-permute-start.26 = (bf16[384,512]{1,0:T(8,128)(2,1)S(1)}, bf16[384,512]{1,0:T(8,128)(2,1)S(1)}, u32[]{:S(2)}, u32[]{:S(2)}) collective-permute-start(bf16[384,512]{1,0:T(8,128)(2,1)S(1)} %add_convert_fusion.1), channel_id=1, source_target_pairs={{0,12},{4,0},{8,4},{12,8},{1,13},{5,1},{9,5},{13,9},{2,14},{6,2},{... | collective-permute-start | bytes 1179656 | tf_op jit(solution)/shard_map/ppermute | solution.py:198

commit v2 on v0

--- a/solution.py
+++ b/solution.py
@@ -11,7 +11,7 @@
 ADP = ("z", "y", "core")
 GATHERED = ((0, 0), (0, 1), (3, 0), (1, 0), (3, 1), (1, 1), (2, 0), (2, 1))
 NT = (((1,), (1,)), ((), ()))
-VMEM_LIMIT = 56 << 20
+VMEM_LIMIT = 63 << 20
 QUICK = pl.CostEstimate(flops=1, bytes_accessed=1, transcendentals=0)
 
 
@@ -227,8 +227,10 @@
     above_side = shift(above, "y", 1)
     from_above = lax.ppermute(above, "z", [(2, 1), (1, 0)])
     sums = begin([tokens, side, below, above])
+    from_below, from_above, sums = lax.optimization_barrier((from_below, from_above, sums))
     two = jnp.where(z >= 2, from_below, from_above)
     two, _, up = lax.optimization_barrier((two, below_side, up))
+    two, above_side = lax.optimization_barrier((two, above_side))
     return sums, [below_side, above_side, two, shift(two, "y", 1)], up
 
 

time: 190 us -> 189 us (level)
  waiting for transfers between devices: 75.6 us -> 72.2 us
  starting transfers between devices: 43.4 us -> 45.4 us
    ppermute x1, waiting for transfers between devices: 11.9 us -> 3.28 us  [gather_features(): from_above = lax.ppermute(above, 'z', [(2, 1), (1, 0)])]
    ppermute x22, waiting for transfers between devices: 41 us -> 45.8 us  [shift(): lax.ppermute(value, axis, [(i, (i + by) % size) for i in range(size)])]
    ppermute x22, starting transfers between devices: 26.1 us -> 28 us  [shift(): lax.ppermute(value, axis, [(i, (i + by) % size) for i in range(size)])]
  transfers between devices with their start and end apart: 29 -> 29, of which waited for: 17 -> 16; matrix products, arithmetic and copies ran while one was open for 11% -> 12% of each run, Pallas kernels for 7% -> 7%
where the time goes in v2:
time: 189 us; the launch traced here: 188 us
  waiting for transfers between devices  72.2 us (38%)
  starting transfers between devices  45.4 us (24%)
  Pallas kernels  28.1 us (15%)
  blocking collectives  15.5 us (8%)
  matrix products  10.5 us (6%)
  other arithmetic  9.53 us (5%)
  local copies, waits for them, and re-layouts  6.23 us (3%)
    ppermute x22, waiting for transfers between devices, shift(): lax.ppermute(value, axis, [(i, (i + by) % size) for i in range(size)])  45.8 us
    ppermute x22, starting transfers between devices, shift(): lax.ppermute(value, axis, [(i, (i + by) % size) for i in range(size)])  28 us
    all_to_all x1, blocking collectives, shards(): lax.all_to_all(context, ADP, split_axis=0, concat_axis=0, tiled=True)  15.5 us
    pallas_call x2, Pallas kernels, project(): pl.pallas_call(kernel, grid_spec=pltpu.PrefetchScalarGridSpec(num_scalar_...  13.8 us
    all_to_all x1, waiting for transfers between devices, shards(): lax.all_to_all(query, ADP, split_axis=0, concat_axis=1, tiled=True)  11.3 us
    pallas_call x2, Pallas kernels, output_partial(): pl.pallas_call(kernel, grid_spec=pltpu.PrefetchScalarGridSpec(num_scalar_...  10.8 us
    ppermute x1, waiting for transfers between devices, shards(): lax.ppermute(up, 'rep', [(i, i ^ 1) for i in range(lax.axis_size('rep'))])  8.46 us
    all_to_all x1, starting transfers between devices, shards(): lax.all_to_all(query, ADP, split_axis=0, concat_axis=1, tiled=True)  5.76 us
  transfers between devices with their start and end apart: 29, of which 16 were waited for; matrix products, arithmetic and copies ran while one was open for 12% of the time, Pallas kernels for 7%

profile of v2, /device:TPU:0, one launch (start us, length us, event | category | flops | bytes accessed | tf_op | source)
XLA Modules:
  0.0 187.7 jit_solution(13424536221163281932)
XLA Ops:
  0.0 0.5 collective-permute-start.6
  0.5 2.6 %collective-permute-start = (bf16[384,512]{1,0:T(8,128)(2,1)}, bf16[384,512]{1,0:T(8,128)(2,1)}, u32[]{:S(2)}, u32[]{:S(2)}) collective-permute-start(bf16[384,512]{1,0:T(8,128)(2,1)} %refs_0_.1), channel_id=1, source_target_pairs={{0,4},{4,8},{8,12},{12,0},{1,5},{5,9},{9,13},{13,1},{2,6},{6,10},{... | collective-permute-start | bytes 1179656 | tf_op jit(solution)/shard_map/ppermute | solution.py:198
  3.0 1.5 collective-permute-start.1
  4.5 2.2 %collective-permute-start.4 = (bf16[384,512]{1,0:T(8,128)(2,1)}, bf16[384,512]{1,0:T(8,128)(2,1)}, u32[]{:S(2)}, u32[]{:S(2)}) collective-permute-start(bf16[384,512]{1,0:T(8,128)(2,1)} %refs_0_.1), channel_id=1, source_target_pairs={{0,12},{4,0},{8,4},{12,8},{1,13},{5,1},{9,5},{13,9},{2,14},{6,2},{... | collective-permute-start | bytes 1179656 | tf_op jit(solution)/shard_map/ppermute | solution.py:198
  6.8 1.1 constant_dynamic-slice_fusion
  8.0 1.1 copy.36
  9.1 3.6 %all-to-all-start = ((bf16[32,16,512]{2,0,1:T(8,128)(2,1)}), bf16[32,16,512]{2,0,1:T(8,128)(2,1)S(1)}, u32[]{:S(2)}, u32[]{:S(2)}) async-start(bf16[32,16,512]{2,0,1:T(8,128)(2,1)} %copy.36), calls=%async_computation | async-start | bytes 1048576 | tf_op jit(solution)/shard_map/all_to_all | solution.py:296
  12.7 12.4 %collective-permute-done.4.refs_3_ = bf16[384,512]{1,0:T(8,128)(2,1)} collective-permute-done((bf16[384,512]{1,0:T(8,128)(2,1)}, bf16[384,512]{1,0:T(8,128)(2,1)}, u32[]{:S(2)}, u32[]{:S(2)}) %collective-permute-start.4) | collective-permute-done | bytes 393248 | tf_op jit(solution)/shard_map/ppermute | solution.py:198
  25.1 1.3 collective-permute-start.5
  26.5 1.4 collective-permute-start.3
  27.9 0.6 stack.43.places
  28.5 0.7 collective-permute-start.9
  29.2 1.3 collective-permute-start.7
  30.6 6.6 %shard_map.118 = (f32[384,512]{1,0:T(8,128)}, f32[384,512]{1,0:T(8,128)}, f32[384,128]{1,0:T(8,128)}) custom-call(s32[16]{0:T(128)} %stack.43.places, bf16[384,512]{1,0:T(8,128)(2,1)} %refs_0_.1, bf16[384,512]{1,0:T(8,128)(2,1)} %copy-done.5, bf16[384,512]{1,0:T(8,128)(2,1)} %collective-permute-done.refs_2_, ...), custom_call_target="tpu_custom_call" | custom-call | flops 1811939328 | bytes 7340032 | tf_op jit(solution)/shard_map/pallas_call | solution.py:64
  37.2 3.3 %collective-permute-done.5 = bf16[384,512]{1,0:T(8,128)(2,1)} collective-permute-done((bf16[384,512]{1,0:T(8,128)(2,1)}, bf16[384,512]{1,0:T(8,128)(2,1)}, u32[]{:S(2)}, u32[]{:S(2)}) %collective-permute-start.5) | collective-permute-done | bytes 393248 | tf_op jit(solution)/shard_map/ppermute | solution.py:228
  40.4 1.0 broadcast_select_fusion.refs_2_
  41.5 6.8 %collective-permute-done.7.refs_0_ = bf16[384,512]{1,0:T(8,128)(2,1)} collective-permute-done((bf16[384,512]{1,0:T(8,128)(2,1)}, bf16[384,512]{1,0:T(8,128)(2,1)}, u32[]{:S(2)}, u32[]{:S(2)}) %collective-permute-start.7) | collective-permute-done | bytes 393248 | tf_op jit(solution)/shard_map/ppermute | solution.py:198
  48.3 1.6 collective-permute-start.8
  49.9 0.8 collective-permute-start.10
  50.8 0.8 broadcast_in_dim.46.refs_23_.slot
  51.6 8.5 %collective-permute-done.8.up_other = bf16[512,512]{1,0:T(8,128)(2,1)S(1)} collective-permute-done((bf16[512,512]{1,0:T(8,128)(2,1)S(1)}, bf16[512,512]{1,0:T(8,128)(2,1)S(1)}, u32[]{:S(2)}, u32[]{:S(2)}) %collective-permute-start.8) | collective-permute-done | bytes 524320 | tf_op jit(solution)/shard_map/ppermute | solution.py:300
  60.1 0.8 copy-done.4
  60.9 7.2 %shard_map.119 = (f32[384,512]{1,0:T(8,128)}, f32[384,512]{1,0:T(8,128)}, f32[192,128]{1,0:T(8,128)}) custom-call(s32[16]{0:T(128)} %stack.43.places, bf16[384,512]{1,0:T(8,128)(2,1)} %collective-permute-done.7.refs_0_, bf16[384,512]{1,0:T(8,128)(2,1)} %collective-permute-done.9.refs_1_, bf16[384,512]{1,0:T(8,128)(2,1)} %copy-done.2, ...), custom_call_target="tpu_custom_call" | custom-call | flops 1811939328 | bytes 7340032 | tf_op jit(solution)/shard_map/pallas_call | solution.py:64
  68.1 0.5 collective-permute-start.11
  68.6 1.9 %collective-permute-done.11 = f32[192,128]{1,0:T(8,128)S(1)} collective-permute-done((f32[192,128]{1,0:T(8,128)}, f32[192,128]{1,0:T(8,128)S(1)}, u32[]{:S(2)}, u32[]{:S(2)}) %collective-permute-start.11) | collective-permute-done | bytes 98336 | tf_op jit(solution)/shard_map/ppermute | solution.py:198
  70.6 0.9 add_convert_fusion.4
  71.5 1.5 collective-permute-start.12
  73.0 2.6 %collective-permute-done.12 = bf16[192,128]{1,0:T(8,128)(2,1)S(1)} collective-permute-done((bf16[192,128]{1,0:T(8,128)(2,1)S(1)}, bf16[192,128]{1,0:T(8,128)(2,1)S(1)}, u32[]{:S(2)}, u32[]{:S(2)}) %collective-permute-start.12) | collective-permute-done | bytes 49184 | tf_op jit(solution)/shard_map/ppermute | solution.py:198
  75.7 4.9 %collective-permute-start.14 = (bf16[192,128]{1,0:T(8,128)(2,1)S(1)}, bf16[192,128]{1,0:T(8,128)(2,1)S(1)}, u32[]{:S(2)}, u32[]{:S(2)}) collective-permute-start(bf16[192,128]{1,0:T(8,128)(2,1)S(1)} %add.217), channel_id=1, source_target_pairs={{0,4},{4,8},{8,12},{12,0},{1,5},{5,9},{9,13},{13,1},{2,6},{6,10},{... | collective-permute-start | bytes 147464 | tf_op jit(solution)/shard_map/ppermute | solution.py:198
  80.6 2.4 %collective-permute-start.16 = (bf16[192,128]{1,0:T(8,128)(2,1)S(1)}, bf16[192,128]{1,0:T(8,128)(2,1)S(1)}, u32[]{:S(2)}, u32[]{:S(2)}) collective-permute-start(bf16[192,128]{1,0:T(8,128)(2,1)S(1)} %add.217), channel_id=1, source_target_pairs={{0,12},{4,0},{8,4},{12,8},{1,13},{5,1},{9,5},{13,9},{2,14},{6,2},{... | collective-permute-start | bytes 147464 | tf_op jit(solution)/shard_map/ppermute | solution.py:198
  83.1 2.6 %collective-permute-done.15 = bf16[192,128]{1,0:T(8,128)(2,1)S(1)} collective-permute-done((bf16[192,128]{1,0:T(8,128)(2,1)S(1)}, bf16[192,128]{1,0:T(8,128)(2,1)S(1)}, u32[]{:S(2)}, u32[]{:S(2)}) %collective-permute-start.15) | collective-permute-done | bytes 49184 | tf_op jit(solution)/shard_map/ppermute | solution.py:198
  85.6 0.6 add_add_fusion.low
  86.3 3.6 %shard_map.120 = bf16[384,512]{1,0:T(8,128)(2,1)} custom-call(s32[1]{0:T(128)} %bitcast.8.half, f32[384,512]{1,0:T(8,128)} %get-tuple-element.52.own, f32[384,512]{1,0:T(8,128)} %collective-permute-done.13.received, bf16[192,128]{1,0:T(8,128)(2,1)} %add_add_fusion.low, s32[384,1]{1,0:T(8,128)} %broadcast_in_dim.46.refs_23_.slot, bf16[512,512]{1,0:T(8,128)(2,1)} %bitcast.52, ...), custom_call_target="tpu_custom_call" | custom-call | flops 1 | bytes 1 | tf_op jit(solution)/shard_map/pallas_call | solution.py:119
  89.9 5.8 %all-to-all-start.1 = ((bf16[16,24,512]{2,1,0:T(8,128)(2,1)}), bf16[16,24,512]{2,1,0:T(8,128)(2,1)S(1)}, u32[]{:S(2)}, u32[]{:S(2)}) async-start(bf16[16,24,512]{2,1,0:T(8,128)(2,1)} %bitcast.55), calls=%async_computation.1 | async-start | bytes 786432 | tf_op jit(solution)/shard_map/all_to_all | solution.py:315
  95.7 0.8 convert_bitcast_fusion
  96.6 11.3 %all-to-all-done.1 = bf16[16,24,512]{2,1,0:T(8,128)(2,1)S(1)} async-done(((bf16[16,24,512]{2,1,0:T(8,128)(2,1)}), bf16[16,24,512]{2,1,0:T(8,128)(2,1)S(1)}, u32[]{:S(2)}, u32[]{:S(2)}) %all-to-all-start.1) | async-done | bytes 393248 | tf_op jit(solution)/shard_map/all_to_all | solution.py:315
  108.2 0.3 fusion.10
  108.6 5.5 %fusion.15 = (f32[8,24,8]{2,1,0:T(8,128)S(1)}, f32[8,24,8,128]{3,2,1,0:T(8,128)S(1)}) fusion(bf16[8,24,128,128]{3,2,1,0:T(8,128)(2,1)} %param.19, bf16[24,8,8,128]{3,2,1,0:T(8,128)(2,1)S(1)} %reshape.48, pred[24,128]{1,0:T(8,128)(4,1)S(1)} %iota_compare_fusion.1), kind=kOutput, calls=%fused_computation.30 | convolution fusion | flops 50723328 | bytes 7480320 | tf_op jit(solution)/shard_map/rkge,krje->krgj/dot_general | solution.py:182
  114.1 0.6 fusion.8
  114.7 4.6 %fusion.5 = bf16[24,8,8,128]{3,2,1,0:T(8,128)(2,1)S(1)} fusion(bf16[8,24,128,128]{3,2,1,0:T(8,128)(2,1)} %param.20, f32[24,8,128]{2,1,0:T(8,128)S(1)} %bitcast.58, f32[24,8,8]{2,1,0:T(8,128)S(1)} %copy.43, f32[8,24,8,128]{3,2,1,0:T(8,128)S(1)} %get-tuple-element.72, f32[8,24,8]{2,1,0:T(8,128)S(1)} %get-tuple-element.70, f32[8,24,8]{2,1,0:T(8,128)S(1)} %max.3, ...), kind=kOutput, calls=%fused_computation.4 | convolution fusion | flops 51707904 | bytes 7590912 | tf_op jit(solution)/shard_map/krgj,krje->rkge/dot_general | solution.py:191
  119.8 15.5 %all_to_all.40 = bf16[16,24,512]{2,1,0:T(8,128)(2,1)S(1)} all-to-all(bf16[16,24,512]{2,1,0:T(8,128)(2,1)S(1)} %bitcast.54), channel_id=1, replica_groups=mesh['rep'=2,'z'=4,'y'=2,'core'=2] {'z','y','core'}, dimensions={0} | all-to-all | bytes 786432 | tf_op jit(solution)/shard_map/all_to_all | solution.py:321
  135.4 1.6 collective-permute-done.17.refs_1_
  137.1 0.8 copy-done.3
  137.8 3.4 %shard_map.122 = bf16[384,512]{1,0:T(8,128)(2,1)} custom-call(s32[16]{0:T(128)} %stack.43.places, bf16[384,512]{1,0:T(8,128)(2,1)} %bitcast.47, bf16[384,512]{1,0:T(8,128)(2,1)} %copy-done.3, bf16[512,8192]{1,0:T(8,128)(2,1)} %refs_2_.3, bf16[512,8192]{1,0:T(8,128)(2,1)} %collective-permute-done.18.refs_9_.refs_10_.refs_11_.refs_12_.refs_13_.refs_14_.refs_15_.refs_3_), custom_call_target="tpu_custom_call" | custom-call | flops 1 | bytes 1 | tf_op jit(solution)/shard_map/pallas_call | solution.py:160
  141.3 0.6 collective-permute-start.21
  141.9 7.3 %shard_map.121 = (bf16[384,512]{1,0:T(8,128)(2,1)}, bf16[384,512]{1,0:T(8,128)(2,1)}, bf16[384,512]{1,0:T(8,128)(2,1)}, bf16[384,512]{1,0:T(8,128)(2,1)}, bf16[3...) custom-call(s32[16]{0:T(128)} %stack.43.places, bf16[384,512]{1,0:T(8,128)(2,1)} %bitcast.48, ...), custom_call_target="tpu_custom_call" | custom-call | flops 1 | bytes 1 | tf_op jit(solution)/shard_map/pallas_call | solution.py:160
  149.2 1.5 collective-permute-start.20
  150.7 2.4 %collective-permute-done.21 = bf16[384,512]{1,0:T(8,128)(2,1)S(1)} collective-permute-done((bf16[384,512]{1,0:T(8,128)(2,1)}, bf16[384,512]{1,0:T(8,128)(2,1)S(1)}, u32[]{:S(2)}, u32[]{:S(2)}) %collective-permute-start.21) | collective-permute-done | bytes 393248 | tf_op jit(solution)/shard_map/ppermute | solution.py:198
  153.1 1.1 add_convert_fusion.3
  154.2 3.1 %collective-permute-start.22 = (bf16[384,512]{1,0:T(8,128)(2,1)S(1)}, bf16[384,512]{1,0:T(8,128)(2,1)S(1)}, u32[]{:S(2)}, u32[]{:S(2)}) collective-permute-start(bf16[384,512]{1,0:T(8,128)(2,1)S(1)} %add_convert_fusion.3), channel_id=1, source_target_pairs={{0,4},{4,8},{1,5},{5,9},{2,6},{6,10},{3,7},{7,11},{16,20},{20,24},... | collective-permute-start | bytes 1179656 | tf_op jit(solution)/shard_map/ppermute | solution.py:244
  157.2 0.5 collective-permute-start.24
  157.8 0.7 collective-permute-start.25
  158.4 1.6 collective-permute-start.19
  160.1 1.4 collective-permute-done.20
  161.5 3.4 %collective-permute-done.22 = bf16[384,512]{1,0:T(8,128)(2,1)S(1)} collective-permute-done((bf16[384,512]{1,0:T(8,128)(2,1)S(1)}, bf16[384,512]{1,0:T(8,128)(2,1)S(1)}, u32[]{:S(2)}, u32[]{:S(2)}) %collective-permute-start.22) | collective-permute-done | bytes 393248 | tf_op jit(solution)/shard_map/ppermute | solution.py:244
  164.9 1.1 add_convert_fusion.2
  166.0 2.5 %collective-permute-start.23 = (bf16[384,512]{1,0:T(8,128)(2,1)S(1)}, bf16[384,512]{1,0:T(8,128)(2,1)S(1)}, u32[]{:S(2)}, u32[]{:S(2)}) collective-permute-start(bf16[384,512]{1,0:T(8,128)(2,1)S(1)} %add_convert_fusion.2), channel_id=1, source_target_pairs={{0,4},{4,8},{8,12},{12,0},{1,5},{5,9},{9,13},{13,1},{2,6},{6,10},{... | collective-permute-start | bytes 1179656 | tf_op jit(solution)/shard_map/ppermute | solution.py:198
  168.5 1.4 collective-permute-done.24
  169.9 1.1 add_convert_fusion.1
  171.1 2.1 %collective-permute-start.26 = (bf16[384,512]{1,0:T(8,128)(2,1)S(1)}, bf16[384,512]{1,0:T(8,128)(2,1)S(1)}, u32[]{:S(2)}, u32[]{:S(2)}) collective-permute-start(bf16[384,512]{1,0:T(8,128)(2,1)S(1)} %add_convert_fusion.1), channel_id=1, source_target_pairs={{0,12},{4,0},{8,4},{12,8},{1,13},{5,1},{9,5},{13,9},{2,14},{6,2},{... | collective-permute-start | bytes 1179656 | tf_op jit(solution)/shard_map/ppermute | solution.py:198
  173.2 4.7 %collective-permute-done.19 = bf16[384,512]{1,0:T(8,128)(2,1)S(1)} collective-permute-done((bf16[384,512]{1,0:T(8,128)(2,1)}, bf16[384,512]{1,0:T(8,128)(2,1)S(1)}, u32[]{:S(2)}, u32[]{:S(2)}) %collective-permute-start.19) | collective-permute-done | bytes 393248 | tf_op jit(solution)/shard_map/ppermute | solution.py:198
  177.9 2.0 %collective-permute-done.23 = bf16[384,512]{1,0:T(8,128)(2,1)S(1)} collective-permute-done((bf16[384,512]{1,0:T(8,128)(2,1)S(1)}, bf16[384,512]{1,0:T(8,128)(2,1)S(1)}, u32[]{:S(2)}, u32[]{:S(2)}) %collective-permute-start.23) | collective-permute-done | bytes 393248 | tf_op jit(solution)/shard_map/ppermute | solution.py:198
  179.9 5.8 %collective-permute-done.26 = bf16[384,512]{1,0:T(8,128)(2,1)S(1)} collective-permute-done((bf16[384,512]{1,0:T(8,128)(2,1)S(1)}, bf16[384,512]{1,0:T(8,128)(2,1)S(1)}, u32[]{:S(2)}, u32[]{:S(2)}) %collective-permute-start.26) | collective-permute-done | bytes 393248 | tf_op jit(solution)/shard_map/ppermute | solution.py:198
  185.7 1.9 %add_convert_fusion = bf16[384,512]{1,0:T(8,128)(2,1)} fusion(bf16[384,512]{1,0:T(8,128)(2,1)S(1)} %collective-permute-done.26, bf16[384,512]{1,0:T(8,128)(2,1)S(1)} %collective-permute-done.23, bf16[384,512]{1,0:T(8,128)(2,1)S(1)} %collective-permute-done.19, bf16[384,512]{1,0:T(8,128)(2,1)} %get-tuple-element.59), kind=kLoop, calls=%fused_computation.5 | loop fusion | flops 1572864 | bytes 1966080 | tf_op jit(solution)/shard_map/convert_element_type | solution.py:344
  (50 shorter events, 1.6 us)
Async XLA Ops:
  0.0 30.6 %collective-permute-start.6 = (bf16[8192,512]{1,0:T(8,128)(2,1)}, bf16[8192,512]{1,0:T(8,128)(2,1)}, u32[]{:S(2)}, u32[]{:S(2)}) collective-permute-start(bf16[8192,512]{1,0:T(8,128)(2,1)} %refs_7_.4), channel_id=1, source_target_pairs={{0,1},{1,0},{2,3},{3,2},{4,5},{5,4},{6,7},{7,6},{8,9},{9,8},{10,11... | collective-permute-start | bytes 25165832 | tf_op jit(solution)/shard_map/ppermute | solution.py:198
  0.5 26.0 %collective-permute-start = (bf16[384,512]{1,0:T(8,128)(2,1)}, bf16[384,512]{1,0:T(8,128)(2,1)}, u32[]{:S(2)}, u32[]{:S(2)}) collective-permute-start(bf16[384,512]{1,0:T(8,128)(2,1)} %refs_0_.1), channel_id=1, source_target_pairs={{0,4},{4,8},{8,12},{12,0},{1,5},{5,9},{9,13},{13,1},{2,6},{6,10},{... | collective-permute-start | bytes 1179656 | tf_op jit(solution)/shard_map/ppermute | solution.py:198
  3.0 23.4 %collective-permute-start.1 = (bf16[384,512]{1,0:T(8,128)(2,1)}, bf16[384,512]{1,0:T(8,128)(2,1)S(1)}, u32[]{:S(2)}, u32[]{:S(2)}) collective-permute-start(bf16[384,512]{1,0:T(8,128)(2,1)} %refs_0_.1), channel_id=1, source_target_pairs={{0,2},{2,0},{1,3},{3,1},{4,6},{6,4},{5,7},{7,5},{8,10},{10,8},{9,1... | collective-permute-start | bytes 1179656 | tf_op jit(solution)/shard_map/ppermute | solution.py:198
  4.5 20.6 %collective-permute-start.4 = (bf16[384,512]{1,0:T(8,128)(2,1)}, bf16[384,512]{1,0:T(8,128)(2,1)}, u32[]{:S(2)}, u32[]{:S(2)}) collective-permute-start(bf16[384,512]{1,0:T(8,128)(2,1)} %refs_0_.1), channel_id=1, source_target_pairs={{0,12},{4,0},{8,4},{12,8},{1,13},{5,1},{9,5},{13,9},{2,14},{6,2},{... | collective-permute-start | bytes 1179656 | tf_op jit(solution)/shard_map/ppermute | solution.py:198
  6.8 19.7 %collective-permute-start.2 = (bf16[1,64,8192]{2,1,0:T(8,128)(2,1)}, bf16[1,64,8192]{2,1,0:T(8,128)(2,1)}, u32[]{:S(2)}, u32[]{:S(2)}) collective-permute-start(bf16[1,64,8192]{2,1,0:T(8,128)(2,1)} %bitcast.37), channel_id=1, source_target_pairs={{0,1},{1,0},{2,3},{3,2},{4,5},{5,4},{6,7},{7,6},{8,9},{9,8},{10,11... | collective-permute-start | bytes 3145736 | tf_op jit(solution)/shard_map/ppermute | solution.py:198
  9.1 32.4 %all-to-all-start = ((bf16[32,16,512]{2,0,1:T(8,128)(2,1)}), bf16[32,16,512]{2,0,1:T(8,128)(2,1)S(1)}, u32[]{:S(2)}, u32[]{:S(2)}) async-start(bf16[32,16,512]{2,0,1:T(8,128)(2,1)} %copy.36), calls=%async_computation | async-start | bytes 1048576 | tf_op jit(solution)/shard_map/all_to_all | solution.py:296
  25.1 15.3 %collective-permute-start.5 = (bf16[384,512]{1,0:T(8,128)(2,1)}, bf16[384,512]{1,0:T(8,128)(2,1)}, u32[]{:S(2)}, u32[]{:S(2)}) collective-permute-start(bf16[384,512]{1,0:T(8,128)(2,1)} %collective-permute-done.4.refs_3_), channel_id=1, source_target_pairs={{8,4},{4,0},{9,5},{5,1},{10,6},{6,2},{11,7},{7,3},{24,20},{20,16},... | collective-permute-start | bytes 1179656 | tf_op jit(solution)/shard_map/ppermute | solution.py:228
  26.4 4.1 %copy-start.5 = (bf16[384,512]{1,0:T(8,128)(2,1)}, bf16[384,512]{1,0:T(8,128)(2,1)S(1)}, u32[]{:S(2)}) copy-start(bf16[384,512]{1,0:T(8,128)(2,1)S(1)} %collective-permute-done.1.refs_1_) | copy-start | bytes 1179652
  26.5 14.0 %collective-permute-start.3 = (bf16[384,512]{1,0:T(8,128)(2,1)}, bf16[384,512]{1,0:T(8,128)(2,1)}, u32[]{:S(2)}, u32[]{:S(2)}) collective-permute-start(bf16[384,512]{1,0:T(8,128)(2,1)} %collective-permute-done.refs_2_), channel_id=1, source_target_pairs={{4,8},{8,12},{5,9},{9,13},{6,10},{10,14},{7,11},{11,15},{20,24},{2... | collective-permute-start | bytes 1179656 | tf_op jit(solution)/shard_map/ppermute | solution.py:226
  28.5 22.2 %copy-start.7 = (s32[384,1]{0,1:T(1,128)S(1)}, s32[384,1]{0,1:T(1,128)}, u32[]{:S(2)}) copy-start(s32[384,1]{0,1:T(1,128)} %param.13) | copy-start | bytes 4612
  28.5 22.2 %copy-start.8 = (s32[16]{0:T(128)S(1)}, s32[16]{0:T(128)}, u32[]{:S(2)}) copy-start(s32[16]{0:T(128)} %param.14) | copy-start | bytes 196
  28.5 21.4 %collective-permute-start.9 = (bf16[384,512]{1,0:T(8,128)(2,1)}, bf16[384,512]{1,0:T(8,128)(2,1)}, u32[]{:S(2)}, u32[]{:S(2)}) collective-permute-start(bf16[384,512]{1,0:T(8,128)(2,1)} %collective-permute-done.4.refs_3_), channel_id=1, source_target_pairs={{0,2},{2,0},{1,3},{3,1},{4,6},{6,4},{5,7},{7,5},{8,10},{10,8},{9,1... | collective-permute-start | bytes 1179656 | tf_op jit(solution)/shard_map/ppermute | solution.py:198
  29.2 19.1 %collective-permute-start.7 = (bf16[384,512]{1,0:T(8,128)(2,1)}, bf16[384,512]{1,0:T(8,128)(2,1)}, u32[]{:S(2)}, u32[]{:S(2)}) collective-permute-start(bf16[384,512]{1,0:T(8,128)(2,1)} %collective-permute-done.refs_2_), channel_id=1, source_target_pairs={{0,2},{2,0},{1,3},{3,1},{4,6},{6,4},{5,7},{7,5},{8,10},{10,8},{9,1... | collective-permute-start | bytes 1179656 | tf_op jit(solution)/shard_map/ppermute | solution.py:198
  41.5 19.4 %copy-start.2 = (bf16[384,512]{1,0:T(8,128)(2,1)}, bf16[384,512]{1,0:T(8,128)(2,1)S(1)}, u32[]{:S(2)}) copy-start(bf16[384,512]{1,0:T(8,128)(2,1)S(1)} %broadcast_select_fusion.refs_2_) | copy-start | bytes 1179652
  41.5 26.6 %copy-start.1 = (bf16[32,16,512]{2,0,1:T(8,128)(2,1)}, bf16[32,16,512]{2,0,1:T(8,128)(2,1)S(1)}, u32[]{:S(2)}) copy-start(bf16[32,16,512]{2,0,1:T(8,128)(2,1)S(1)} %all-to-all-done) | copy-start | bytes 1572868
  48.3 11.7 %collective-permute-start.8 = (bf16[512,512]{1,0:T(8,128)(2,1)S(1)}, bf16[512,512]{1,0:T(8,128)(2,1)S(1)}, u32[]{:S(2)}, u32[]{:S(2)}) collective-permute-start(bf16[512,512]{1,0:T(8,128)(2,1)S(1)} %bitcast.51), channel_id=1, source_target_pairs={{0,16},{16,0},{1,17},{17,1},{2,18},{18,2},{3,19},{19,3},{4,20},{20... | collective-permute-start | bytes 1572872 | tf_op jit(solution)/shard_map/ppermute | solution.py:300
  49.9 11.0 %collective-permute-start.10 = (bf16[384,512]{1,0:T(8,128)(2,1)S(1)}, bf16[384,512]{1,0:T(8,128)(2,1)}, u32[]{:S(2)}, u32[]{:S(2)}) collective-permute-start(bf16[384,512]{1,0:T(8,128)(2,1)S(1)} %broadcast_select_fusion.refs_2_), channel_id=1, source_target_pairs={{0,2},{2,0},{1,3},{3,1},{4,6},{6,4},{5,7},{7,5},{8,10},{10,8},{9,1... | collective-permute-start | bytes 1179656 | tf_op jit(solution)/shard_map/ppermute | solution.py:198
  51.6 44.0 %copy-start.6 = (bf16[24,1024]{1,0:T(8,128)(2,1)S(1)}, bf16[24,1024]{1,0:T(8,128)(2,1)}, u32[]{:S(2)}) copy-start(bf16[24,1024]{1,0:T(8,128)(2,1)} %param.21) | copy-start | bytes 147460
  51.6 44.9 %copy-start.9 = (s32[24]{0:T(128)S(1)}, s32[24]{0:T(128)}, u32[]{:S(2)}) copy-start(s32[24]{0:T(128)} %param.15) | copy-start | bytes 292
  60.1 0.8 copy-start.4
  68.1 7.6 %collective-permute-start.13 = (f32[384,512]{1,0:T(8,128)}, f32[384,512]{1,0:T(8,128)}, u32[]{:S(2)}, u32[]{:S(2)}) collective-permute-start(f32[384,512]{1,0:T(8,128)} %get-tuple-element.54), channel_id=1, source_target_pairs={{0,1},{1,0},{2,3},{3,2},{4,5},{5,4},{6,7},{7,6},{8,9},{9,8},{10,11... | collective-permute-start | bytes 2359304 | tf_op jit(solution)/shard_map/ppermute | solution.py:198
  68.1 2.4 %collective-permute-start.11 = (f32[192,128]{1,0:T(8,128)}, f32[192,128]{1,0:T(8,128)S(1)}, u32[]{:S(2)}, u32[]{:S(2)}) collective-permute-start(f32[192,128]{1,0:T(8,128)} %get-tuple-element.53), channel_id=1, source_target_pairs={{0,1},{1,0},{2,3},{3,2},{4,5},{5,4},{6,7},{7,6},{8,9},{9,8},{10,11... | collective-permute-start | bytes 294920 | tf_op jit(solution)/shard_map/ppermute | solution.py:198
  71.5 4.2 %collective-permute-start.12 = (bf16[192,128]{1,0:T(8,128)(2,1)S(1)}, bf16[192,128]{1,0:T(8,128)(2,1)S(1)}, u32[]{:S(2)}, u32[]{:S(2)}) collective-permute-start(bf16[192,128]{1,0:T(8,128)(2,1)S(1)} %add_convert_fusion.4), channel_id=1, source_target_pairs={{0,2},{2,0},{1,3},{3,1},{4,6},{6,4},{5,7},{7,5},{8,10},{10,8},{9,1... | collective-permute-start | bytes 147464 | tf_op jit(solution)/shard_map/ppermute | solution.py:198
  75.7 7.4 %collective-permute-start.14 = (bf16[192,128]{1,0:T(8,128)(2,1)S(1)}, bf16[192,128]{1,0:T(8,128)(2,1)S(1)}, u32[]{:S(2)}, u32[]{:S(2)}) collective-permute-start(bf16[192,128]{1,0:T(8,128)(2,1)S(1)} %add.217), channel_id=1, source_target_pairs={{0,4},{4,8},{8,12},{12,0},{1,5},{5,9},{9,13},{13,1},{2,6},{6,10},{... | collective-permute-start | bytes 147464 | tf_op jit(solution)/shard_map/ppermute | solution.py:198
  80.6 5.0 %collective-permute-start.15 = (bf16[192,128]{1,0:T(8,128)(2,1)S(1)}, bf16[192,128]{1,0:T(8,128)(2,1)S(1)}, u32[]{:S(2)}, u32[]{:S(2)}) collective-permute-start(bf16[192,128]{1,0:T(8,128)(2,1)S(1)} %add.217), channel_id=1, source_target_pairs={{0,8},{4,12},{8,0},{12,4},{1,9},{5,13},{9,1},{13,5},{2,10},{6,14},... | collective-permute-start | bytes 147464 | tf_op jit(solution)/shard_map/ppermute | solution.py:198
  80.6 5.0 %collective-permute-start.16 = (bf16[192,128]{1,0:T(8,128)(2,1)S(1)}, bf16[192,128]{1,0:T(8,128)(2,1)S(1)}, u32[]{:S(2)}, u32[]{:S(2)}) collective-permute-start(bf16[192,128]{1,0:T(8,128)(2,1)S(1)} %add.217), channel_id=1, source_target_pairs={{0,12},{4,0},{8,4},{12,8},{1,13},{5,1},{9,5},{13,9},{2,14},{6,2},{... | collective-permute-start | bytes 147464 | tf_op jit(solution)/shard_map/ppermute | solution.py:198
  89.9 47.2 %collective-permute-start.18 = (bf16[512,8192]{1,0:T(8,128)(2,1)}, bf16[512,8192]{1,0:T(8,128)(2,1)}, u32[]{:S(2)}, u32[]{:S(2)}) collective-permute-start(bf16[512,8192]{1,0:T(8,128)(2,1)} %refs_2_.3), channel_id=1, source_target_pairs={{0,1},{1,0},{2,3},{3,2},{4,5},{5,4},{6,7},{7,6},{8,9},{9,8},{10,11... | collective-permute-start | bytes 25165832 | tf_op jit(solution)/shard_map/ppermute | solution.py:198
  89.9 18.0 %all-to-all-start.1 = ((bf16[16,24,512]{2,1,0:T(8,128)(2,1)}), bf16[16,24,512]{2,1,0:T(8,128)(2,1)S(1)}, u32[]{:S(2)}, u32[]{:S(2)}) async-start(bf16[16,24,512]{2,1,0:T(8,128)(2,1)} %bitcast.55), calls=%async_computation.1 | async-start | bytes 786432 | tf_op jit(solution)/shard_map/all_to_all | solution.py:315
  135.3 1.7 copy-start
  135.3 1.7 collective-permute-start.17
  137.1 0.8 copy-start.3
  141.3 11.8 %collective-permute-start.21 = (bf16[384,512]{1,0:T(8,128)(2,1)}, bf16[384,512]{1,0:T(8,128)(2,1)S(1)}, u32[]{:S(2)}, u32[]{:S(2)}) collective-permute-start(bf16[384,512]{1,0:T(8,128)(2,1)} %shard_map.122), channel_id=1, source_target_pairs={{0,2},{2,0},{1,3},{3,1},{4,6},{6,4},{5,7},{7,5},{8,10},{10,8},{9,1... | collective-permute-start | bytes 1179656 | tf_op jit(solution)/shard_map/ppermute | solution.py:198
  149.2 12.3 %collective-permute-start.20 = (bf16[384,512]{1,0:T(8,128)(2,1)}, bf16[384,512]{1,0:T(8,128)(2,1)S(1)}, u32[]{:S(2)}, u32[]{:S(2)}) collective-permute-start(bf16[384,512]{1,0:T(8,128)(2,1)} %get-tuple-element.63), channel_id=1, source_target_pairs={{0,2},{2,0},{1,3},{3,1},{4,6},{6,4},{5,7},{7,5},{8,10},{10,8},{9,1... | collective-permute-start | bytes 1179656 | tf_op jit(solution)/shard_map/ppermute | solution.py:198
  154.2 10.7 %collective-permute-start.22 = (bf16[384,512]{1,0:T(8,128)(2,1)S(1)}, bf16[384,512]{1,0:T(8,128)(2,1)S(1)}, u32[]{:S(2)}, u32[]{:S(2)}) collective-permute-start(bf16[384,512]{1,0:T(8,128)(2,1)S(1)} %add_convert_fusion.3), channel_id=1, source_target_pairs={{0,4},{4,8},{1,5},{5,9},{2,6},{6,10},{3,7},{7,11},{16,20},{20,24},... | collective-permute-start | bytes 1179656 | tf_op jit(solution)/shard_map/ppermute | solution.py:244
  157.2 12.7 %collective-permute-start.24 = (bf16[384,512]{1,0:T(8,128)(2,1)}, bf16[384,512]{1,0:T(8,128)(2,1)S(1)}, u32[]{:S(2)}, u32[]{:S(2)}) collective-permute-start(bf16[384,512]{1,0:T(8,128)(2,1)} %get-tuple-element.68), channel_id=1, source_target_pairs={{0,2},{2,0},{1,3},{3,1},{4,6},{6,4},{5,7},{7,5},{8,10},{10,8},{9,1... | collective-permute-start | bytes 1179656 | tf_op jit(solution)/shard_map/ppermute | solution.py:198
  157.8 12.2 %collective-permute-start.25 = (bf16[384,512]{1,0:T(8,128)(2,1)S(1)}, bf16[384,512]{1,0:T(8,128)(2,1)S(1)}, u32[]{:S(2)}, u32[]{:S(2)}) collective-permute-start(bf16[384,512]{1,0:T(8,128)(2,1)S(1)} %add_convert_fusion.3), channel_id=1, source_target_pairs={{12,8},{8,4},{13,9},{9,5},{14,10},{10,6},{15,11},{11,7},{28,24},{2... | collective-permute-start | bytes 1179656 | tf_op jit(solution)/shard_map/ppermute | solution.py:245
  158.4 19.5 %collective-permute-start.19 = (bf16[384,512]{1,0:T(8,128)(2,1)}, bf16[384,512]{1,0:T(8,128)(2,1)S(1)}, u32[]{:S(2)}, u32[]{:S(2)}) collective-permute-start(bf16[384,512]{1,0:T(8,128)(2,1)} %get-tuple-element.60), channel_id=1, source_target_pairs={{0,2},{2,0},{1,3},{3,1},{4,6},{6,4},{5,7},{7,5},{8,10},{10,8},{9,1... | collective-permute-start | bytes 1179656 | tf_op jit(solution)/shard_map/ppermute | solution.py:198
  166.0 13.9 %collective-permute-start.23 = (bf16[384,512]{1,0:T(8,128)(2,1)S(1)}, bf16[384,512]{1,0:T(8,128)(2,1)S(1)}, u32[]{:S(2)}, u32[]{:S(2)}) collective-permute-start(bf16[384,512]{1,0:T(8,128)(2,1)S(1)} %add_convert_fusion.2), channel_id=1, source_target_pairs={{0,4},{4,8},{8,12},{12,0},{1,5},{5,9},{9,13},{13,1},{2,6},{6,10},{... | collective-permute-start | bytes 1179656 | tf_op jit(solution)/shard_map/ppermute | solution.py:198
  171.1 14.7 %collective-permute-start.26 = (bf16[384,512]{1,0:T(8,128)(2,1)S(1)}, bf16[384,512]{1,0:T(8,128)(2,1)S(1)}, u32[]{:S(2)}, u32[]{:S(2)}) collective-permute-start(bf16[384,512]{1,0:T(8,128)(2,1)S(1)} %add_convert_fusion.1), channel_id=1, source_target_pairs={{0,12},{4,0},{8,4},{12,8},{1,13},{5,1},{9,5},{13,9},{2,14},{6,2},{... | collective-permute-start | bytes 1179656 | tf_op jit(solution)/shard_map/ppermute | solution.py:198

commit v3 on v2

--- a/solution.py
+++ b/solution.py
@@ -223,7 +223,7 @@
     below, above = shift(tokens, "z", 1), shift(tokens, "z", 3)
     below, side, _ = lax.optimization_barrier((below, side, down_other))
     below_side = shift(below, "y", 1)
-    from_below = lax.ppermute(below, "z", [(1, 2), (2, 3)])
+    from_below = lax.ppermute(after(below, below_side), "z", [(1, 2), (2, 3)])
     above_side = shift(above, "y", 1)
     from_above = lax.ppermute(above, "z", [(2, 1), (1, 0)])
     sums = begin([tokens, side, below, above])

time: 189 us -> 194 us (1.026)
  starting transfers between devices: 45.4 us -> 55.4 us
  waiting for transfers between devices: 72.2 us -> 67.4 us
    ppermute x22, waiting for transfers between devices: 45.8 us -> 35 us  [shift(): lax.ppermute(value, axis, [(i, (i + by) % size) for i in range(size)])]
    all_to_all x1, starting transfers between devices: 3.57 us -> 10.2 us  [shards(): up = lax.all_to_all(up, ADP, split_axis=1, concat_axis=0, tiled=True)]
    ppermute x1, waiting for transfers between devices: 3.28 us -> 8.2 us  [gather_features(): from_above = lax.ppermute(above, 'z', [(2, 1), (1, 0)])]
    ppermute x22, starting transfers between devices: 28 us -> 31.4 us  [shift(): lax.ppermute(value, axis, [(i, (i + by) % size) for i in range(size)])]
  transfers between devices with their start and end apart: 29 -> 29, of which waited for: 16 -> 15; matrix products, arithmetic and copies ran while one was open for 12% -> 11% of each run, Pallas kernels for 7% -> 7%
where the time goes in v3:
time: 194 us; the launch traced here: 193 us
  waiting for transfers between devices  67.4 us (35%)
  starting transfers between devices  55.4 us (29%)
  Pallas kernels  28.1 us (14%)
  blocking collectives  15.5 us (8%)
  matrix products  10.5 us (5%)
  other arithmetic  9.52 us (5%)
  local copies, waits for them, and re-layouts  6.23 us (3%)
    ppermute x22, waiting for transfers between devices, shift(): lax.ppermute(value, axis, [(i, (i + by) % size) for i in range(size)])  35 us
    ppermute x22, starting transfers between devices, shift(): lax.ppermute(value, axis, [(i, (i + by) % size) for i in range(size)])  31.4 us
    all_to_all x1, blocking collectives, shards(): lax.all_to_all(context, ADP, split_axis=0, concat_axis=0, tiled=True)  15.5 us
    pallas_call x2, Pallas kernels, project(): pl.pallas_call(kernel, grid_spec=pltpu.PrefetchScalarGridSpec(num_scalar_...  13.8 us
    all_to_all x1, waiting for transfers between devices, shards(): lax.all_to_all(query, ADP, split_axis=0, concat_axis=1, tiled=True)  11.3 us
    pallas_call x2, Pallas kernels, output_partial(): pl.pallas_call(kernel, grid_spec=pltpu.PrefetchScalarGridSpec(num_scalar_...  10.8 us
    all_to_all x1, starting transfers between devices, shards(): up = lax.all_to_all(up, ADP, split_axis=1, concat_axis=0, tiled=True)  10.2 us
    ppermute x1, waiting for transfers between devices, shards(): lax.ppermute(up, 'rep', [(i, i ^ 1) for i in range(lax.axis_size('rep'))])  9.58 us
  transfers between devices with their start and end apart: 29, of which 15 were waited for; matrix products, arithmetic and copies ran while one was open for 11% of the time, Pallas kernels for 7%

profile of v3, /device:TPU:0, one launch (start us, length us, event | category | flops | bytes accessed | tf_op | source)
XLA Modules:
  0.0 193.0 jit_solution(7671319549531693875)
XLA Ops:
  0.0 0.5 collective-permute-start.7
  0.5 3.0 %collective-permute-start = (bf16[384,512]{1,0:T(8,128)(2,1)}, bf16[384,512]{1,0:T(8,128)(2,1)S(1)}, u32[]{:S(2)}, u32[]{:S(2)}) collective-permute-start(bf16[384,512]{1,0:T(8,128)(2,1)} %refs_0_.1), channel_id=1, source_target_pairs={{0,4},{4,8},{8,12},{12,0},{1,5},{5,9},{9,13},{13,1},{2,6},{6,10},{... | collective-permute-start | bytes 1179656 | tf_op jit(solution)/shard_map/ppermute | solution.py:198
  3.5 1.5 collective-permute-start.1
  5.1 2.2 %collective-permute-start.5 = (bf16[384,512]{1,0:T(8,128)(2,1)}, bf16[384,512]{1,0:T(8,128)(2,1)}, u32[]{:S(2)}, u32[]{:S(2)}) collective-permute-start(bf16[384,512]{1,0:T(8,128)(2,1)} %refs_0_.1), channel_id=1, source_target_pairs={{0,12},{4,0},{8,4},{12,8},{1,13},{5,1},{9,5},{13,9},{2,14},{6,2},{... | collective-permute-start | bytes 1179656 | tf_op jit(solution)/shard_map/ppermute | solution.py:198
  7.3 8.4 %collective-permute-done.refs_2_ = bf16[384,512]{1,0:T(8,128)(2,1)S(1)} collective-permute-done((bf16[384,512]{1,0:T(8,128)(2,1)}, bf16[384,512]{1,0:T(8,128)(2,1)S(1)}, u32[]{:S(2)}, u32[]{:S(2)}) %collective-permute-start) | collective-permute-done | bytes 393248 | tf_op jit(solution)/shard_map/ppermute | solution.py:198
  15.8 2.2 %collective-permute-start.3 = (bf16[384,512]{1,0:T(8,128)(2,1)S(1)}, bf16[384,512]{1,0:T(8,128)(2,1)S(1)}, u32[]{:S(2)}, u32[]{:S(2)}) collective-permute-start(bf16[384,512]{1,0:T(8,128)(2,1)S(1)} %collective-permute-done.refs_2_), channel_id=1, source_target_pairs={{0,2},{2,0},{1,3},{3,1},{4,6},{6,4},{5,7},{7,5},{8,10},{10,8},{9,1... | collective-permute-start | bytes 1179656 | tf_op jit(solution)/shard_map/ppermute | solution.py:198
  18.0 1.1 constant_dynamic-slice_fusion
  19.2 1.1 copy.36
  20.3 10.2 %all-to-all-start = ((bf16[32,16,512]{2,0,1:T(8,128)(2,1)}), bf16[32,16,512]{2,0,1:T(8,128)(2,1)S(1)}, u32[]{:S(2)}, u32[]{:S(2)}) async-start(bf16[32,16,512]{2,0,1:T(8,128)(2,1)} %copy.36), calls=%async_computation | async-start | bytes 1048576 | tf_op jit(solution)/shard_map/all_to_all | solution.py:296
  30.5 1.3 collective-permute-start.6
  31.9 1.4 collective-permute-start.4
  33.3 0.6 stack.43.places
  33.9 1.9 collective-permute-start.9
  35.9 6.6 %shard_map.118 = (f32[384,512]{1,0:T(8,128)}, f32[384,512]{1,0:T(8,128)}, f32[384,128]{1,0:T(8,128)}) custom-call(s32[16]{0:T(128)} %stack.43.places, bf16[384,512]{1,0:T(8,128)(2,1)} %refs_0_.1, bf16[384,512]{1,0:T(8,128)(2,1)} %copy-done.7, bf16[384,512]{1,0:T(8,128)(2,1)} %copy-done.6, bf16[384,512]{1,0:T(8,128)(2,1)} %collective-permute-done.5.refs_3_, ...), custom_call_target="tpu_custom_call" | custom-call | flops 1811939328 | bytes 7340032 | tf_op jit(solution)/shard_map/pallas_call | solution.py:64
  42.4 8.2 %collective-permute-done.6 = bf16[384,512]{1,0:T(8,128)(2,1)} collective-permute-done((bf16[384,512]{1,0:T(8,128)(2,1)}, bf16[384,512]{1,0:T(8,128)(2,1)}, u32[]{:S(2)}, u32[]{:S(2)}) %collective-permute-start.6) | collective-permute-done | bytes 393248 | tf_op jit(solution)/shard_map/ppermute | solution.py:228
  50.6 1.0 broadcast_select_fusion.refs_2_
  51.7 1.6 collective-permute-start.8
  53.3 1.5 collective-permute-start.10
  54.8 0.8 broadcast_in_dim.46.refs_23_.slot
  55.6 9.6 %collective-permute-done.8.up_other = bf16[512,512]{1,0:T(8,128)(2,1)S(1)} collective-permute-done((bf16[512,512]{1,0:T(8,128)(2,1)S(1)}, bf16[512,512]{1,0:T(8,128)(2,1)S(1)}, u32[]{:S(2)}, u32[]{:S(2)}) %collective-permute-start.8) | collective-permute-done | bytes 524320 | tf_op jit(solution)/shard_map/ppermute | solution.py:300
  65.2 0.8 copy-done.5
  66.0 7.2 %shard_map.119 = (f32[384,512]{1,0:T(8,128)}, f32[384,512]{1,0:T(8,128)}, f32[192,128]{1,0:T(8,128)}) custom-call(s32[16]{0:T(128)} %stack.43.places, bf16[384,512]{1,0:T(8,128)(2,1)} %copy-done.8, bf16[384,512]{1,0:T(8,128)(2,1)} %collective-permute-done.9.refs_1_, bf16[384,512]{1,0:T(8,128)(2,1)} %copy-done.2, ...), custom_call_target="tpu_custom_call" | custom-call | flops 1811939328 | bytes 7340032 | tf_op jit(solution)/shard_map/pallas_call | solution.py:64
  73.3 0.5 collective-permute-start.11
  73.8 2.1 %collective-permute-done.11 = f32[192,128]{1,0:T(8,128)S(1)} collective-permute-done((f32[192,128]{1,0:T(8,128)}, f32[192,128]{1,0:T(8,128)S(1)}, u32[]{:S(2)}, u32[]{:S(2)}) %collective-permute-start.11) | collective-permute-done | bytes 98336 | tf_op jit(solution)/shard_map/ppermute | solution.py:198
  75.9 0.9 add_convert_fusion.4
  76.8 1.5 collective-permute-start.12
  78.4 2.6 %collective-permute-done.12 = bf16[192,128]{1,0:T(8,128)(2,1)S(1)} collective-permute-done((bf16[192,128]{1,0:T(8,128)(2,1)S(1)}, bf16[192,128]{1,0:T(8,128)(2,1)S(1)}, u32[]{:S(2)}, u32[]{:S(2)}) %collective-permute-start.12) | collective-permute-done | bytes 49184 | tf_op jit(solution)/shard_map/ppermute | solution.py:198
  81.0 4.3 %collective-permute-start.14 = (bf16[192,128]{1,0:T(8,128)(2,1)S(1)}, bf16[192,128]{1,0:T(8,128)(2,1)S(1)}, u32[]{:S(2)}, u32[]{:S(2)}) collective-permute-start(bf16[192,128]{1,0:T(8,128)(2,1)S(1)} %add.217), channel_id=1, source_target_pairs={{0,4},{4,8},{8,12},{12,0},{1,5},{5,9},{9,13},{13,1},{2,6},{6,10},{... | collective-permute-start | bytes 147464 | tf_op jit(solution)/shard_map/ppermute | solution.py:198
  85.5 2.8 %collective-permute-start.16 = (bf16[192,128]{1,0:T(8,128)(2,1)S(1)}, bf16[192,128]{1,0:T(8,128)(2,1)S(1)}, u32[]{:S(2)}, u32[]{:S(2)}) collective-permute-start(bf16[192,128]{1,0:T(8,128)(2,1)S(1)} %add.217), channel_id=1, source_target_pairs={{0,12},{4,0},{8,4},{12,8},{1,13},{5,1},{9,5},{13,9},{2,14},{6,2},{... | collective-permute-start | bytes 147464 | tf_op jit(solution)/shard_map/ppermute | solution.py:198
  88.4 2.5 %collective-permute-done.15 = bf16[192,128]{1,0:T(8,128)(2,1)S(1)} collective-permute-done((bf16[192,128]{1,0:T(8,128)(2,1)S(1)}, bf16[192,128]{1,0:T(8,128)(2,1)S(1)}, u32[]{:S(2)}, u32[]{:S(2)}) %collective-permute-start.15) | collective-permute-done | bytes 49184 | tf_op jit(solution)/shard_map/ppermute | solution.py:198
  90.9 0.6 add_add_fusion.low
  91.5 3.6 %shard_map.120 = bf16[384,512]{1,0:T(8,128)(2,1)} custom-call(s32[1]{0:T(128)} %bitcast.8.half, f32[384,512]{1,0:T(8,128)} %get-tuple-element.54.own, f32[384,512]{1,0:T(8,128)} %copy-done.4, bf16[192,128]{1,0:T(8,128)(2,1)} %add_add_fusion.low, s32[384,1]{1,0:T(8,128)} %broadcast_in_dim.46.refs_23_.slot, bf16[512,512]{1,0:T(8,128)(2,1)} %bitcast.52, ...), custom_call_target="tpu_custom_call" | custom-call | flops 1 | bytes 1 | tf_op jit(solution)/shard_map/pallas_call | solution.py:119
  95.1 5.8 %all-to-all-start.1 = ((bf16[16,24,512]{2,1,0:T(8,128)(2,1)}), bf16[16,24,512]{2,1,0:T(8,128)(2,1)S(1)}, u32[]{:S(2)}, u32[]{:S(2)}) async-start(bf16[16,24,512]{2,1,0:T(8,128)(2,1)} %bitcast.55), calls=%async_computation.1 | async-start | bytes 786432 | tf_op jit(solution)/shard_map/all_to_all | solution.py:315
  100.9 0.8 convert_bitcast_fusion
  101.8 11.3 %all-to-all-done.1 = bf16[16,24,512]{2,1,0:T(8,128)(2,1)S(1)} async-done(((bf16[16,24,512]{2,1,0:T(8,128)(2,1)}), bf16[16,24,512]{2,1,0:T(8,128)(2,1)S(1)}, u32[]{:S(2)}, u32[]{:S(2)}) %all-to-all-start.1) | async-done | bytes 393248 | tf_op jit(solution)/shard_map/all_to_all | solution.py:315
  113.5 0.3 fusion.10
  113.8 5.5 %fusion.15 = (f32[8,24,8]{2,1,0:T(8,128)S(1)}, f32[8,24,8,128]{3,2,1,0:T(8,128)S(1)}) fusion(bf16[8,24,128,128]{3,2,1,0:T(8,128)(2,1)} %param.19, bf16[24,8,8,128]{3,2,1,0:T(8,128)(2,1)S(1)} %reshape.48, pred[24,128]{1,0:T(8,128)(4,1)S(1)} %iota_compare_fusion.1), kind=kOutput, calls=%fused_computation.30 | convolution fusion | flops 50723328 | bytes 7480320 | tf_op jit(solution)/shard_map/rkge,krje->krgj/dot_general | solution.py:182
  119.3 0.5 fusion.8
  120.0 4.6 %fusion.5 = bf16[24,8,8,128]{3,2,1,0:T(8,128)(2,1)S(1)} fusion(bf16[8,24,128,128]{3,2,1,0:T(8,128)(2,1)} %param.20, f32[24,8,128]{2,1,0:T(8,128)S(1)} %bitcast.58, f32[24,8,8]{2,1,0:T(8,128)S(1)} %copy.43, f32[8,24,8,128]{3,2,1,0:T(8,128)S(1)} %get-tuple-element.74, f32[8,24,8]{2,1,0:T(8,128)S(1)} %get-tuple-element.72, f32[8,24,8]{2,1,0:T(8,128)S(1)} %max.3, ...), kind=kOutput, calls=%fused_computation.4 | convolution fusion | flops 51707904 | bytes 7590912 | tf_op jit(solution)/shard_map/krgj,krje->rkge/dot_general | solution.py:191
  124.6 0.2 reshape_reshape.3
  125.1 15.5 %all_to_all.40 = bf16[16,24,512]{2,1,0:T(8,128)(2,1)S(1)} all-to-all(bf16[16,24,512]{2,1,0:T(8,128)(2,1)S(1)} %bitcast.54), channel_id=1, replica_groups=mesh['rep'=2,'z'=4,'y'=2,'core'=2] {'z','y','core'}, dimensions={0} | all-to-all | bytes 786432 | tf_op jit(solution)/shard_map/all_to_all | solution.py:321
  140.7 1.6 collective-permute-done.17.refs_1_
  142.3 0.8 copy-done.3
  143.1 3.4 %shard_map.122 = bf16[384,512]{1,0:T(8,128)(2,1)} custom-call(s32[16]{0:T(128)} %stack.43.places, bf16[384,512]{1,0:T(8,128)(2,1)} %bitcast.47, bf16[384,512]{1,0:T(8,128)(2,1)} %copy-done.3, bf16[512,8192]{1,0:T(8,128)(2,1)} %refs_2_.3, bf16[512,8192]{1,0:T(8,128)(2,1)} %collective-permute-done.18.refs_9_.refs_10_.refs_11_.refs_12_.refs_13_.refs_14_.refs_15_.refs_3_), custom_call_target="tpu_custom_call" | custom-call | flops 1 | bytes 1 | tf_op jit(solution)/shard_map/pallas_call | solution.py:160
  146.6 0.6 collective-permute-start.21
  147.2 7.3 %shard_map.121 = (bf16[384,512]{1,0:T(8,128)(2,1)}, bf16[384,512]{1,0:T(8,128)(2,1)}, bf16[384,512]{1,0:T(8,128)(2,1)}, bf16[384,512]{1,0:T(8,128)(2,1)}, bf16[3...) custom-call(s32[16]{0:T(128)} %stack.43.places, bf16[384,512]{1,0:T(8,128)(2,1)} %bitcast.48, ...), custom_call_target="tpu_custom_call" | custom-call | flops 1 | bytes 1 | tf_op jit(solution)/shard_map/pallas_call | solution.py:160
  154.5 1.5 collective-permute-start.20
  156.0 2.3 %collective-permute-done.21 = bf16[384,512]{1,0:T(8,128)(2,1)S(1)} collective-permute-done((bf16[384,512]{1,0:T(8,128)(2,1)}, bf16[384,512]{1,0:T(8,128)(2,1)S(1)}, u32[]{:S(2)}, u32[]{:S(2)}) %collective-permute-start.21) | collective-permute-done | bytes 393248 | tf_op jit(solution)/shard_map/ppermute | solution.py:198
  158.3 1.1 add_convert_fusion.3
  159.4 3.1 %collective-permute-start.22 = (bf16[384,512]{1,0:T(8,128)(2,1)S(1)}, bf16[384,512]{1,0:T(8,128)(2,1)S(1)}, u32[]{:S(2)}, u32[]{:S(2)}) collective-permute-start(bf16[384,512]{1,0:T(8,128)(2,1)S(1)} %add_convert_fusion.3), channel_id=1, source_target_pairs={{0,4},{4,8},{1,5},{5,9},{2,6},{6,10},{3,7},{7,11},{16,20},{20,24},... | collective-permute-start | bytes 1179656 | tf_op jit(solution)/shard_map/ppermute | solution.py:244
  162.5 0.5 collective-permute-start.24
  163.0 0.7 collective-permute-start.25
  163.7 1.6 collective-permute-start.19
  165.3 1.4 collective-permute-done.20
  166.8 3.4 %collective-permute-done.22 = bf16[384,512]{1,0:T(8,128)(2,1)S(1)} collective-permute-done((bf16[384,512]{1,0:T(8,128)(2,1)S(1)}, bf16[384,512]{1,0:T(8,128)(2,1)S(1)}, u32[]{:S(2)}, u32[]{:S(2)}) %collective-permute-start.22) | collective-permute-done | bytes 393248 | tf_op jit(solution)/shard_map/ppermute | solution.py:244
  170.2 1.1 add_convert_fusion.2
  171.3 2.5 %collective-permute-start.23 = (bf16[384,512]{1,0:T(8,128)(2,1)S(1)}, bf16[384,512]{1,0:T(8,128)(2,1)S(1)}, u32[]{:S(2)}, u32[]{:S(2)}) collective-permute-start(bf16[384,512]{1,0:T(8,128)(2,1)S(1)} %add_convert_fusion.2), channel_id=1, source_target_pairs={{0,4},{4,8},{8,12},{12,0},{1,5},{5,9},{9,13},{13,1},{2,6},{6,10},{... | collective-permute-start | bytes 1179656 | tf_op jit(solution)/shard_map/ppermute | solution.py:198
  173.8 1.3 collective-permute-done.24
  175.2 1.1 add_convert_fusion.1
  176.3 2.2 %collective-permute-start.26 = (bf16[384,512]{1,0:T(8,128)(2,1)S(1)}, bf16[384,512]{1,0:T(8,128)(2,1)S(1)}, u32[]{:S(2)}, u32[]{:S(2)}) collective-permute-start(bf16[384,512]{1,0:T(8,128)(2,1)S(1)} %add_convert_fusion.1), channel_id=1, source_target_pairs={{0,12},{4,0},{8,4},{12,8},{1,13},{5,1},{9,5},{13,9},{2,14},{6,2},{... | collective-permute-start | bytes 1179656 | tf_op jit(solution)/shard_map/ppermute | solution.py:198
  178.5 4.7 %collective-permute-done.19 = bf16[384,512]{1,0:T(8,128)(2,1)S(1)} collective-permute-done((bf16[384,512]{1,0:T(8,128)(2,1)}, bf16[384,512]{1,0:T(8,128)(2,1)S(1)}, u32[]{:S(2)}, u32[]{:S(2)}) %collective-permute-start.19) | collective-permute-done | bytes 393248 | tf_op jit(solution)/shard_map/ppermute | solution.py:198
  183.2 2.0 %collective-permute-done.23 = bf16[384,512]{1,0:T(8,128)(2,1)S(1)} collective-permute-done((bf16[384,512]{1,0:T(8,128)(2,1)S(1)}, bf16[384,512]{1,0:T(8,128)(2,1)S(1)}, u32[]{:S(2)}, u32[]{:S(2)}) %collective-permute-start.23) | collective-permute-done | bytes 393248 | tf_op jit(solution)/shard_map/ppermute | solution.py:198
  185.2 5.8 %collective-permute-done.26 = bf16[384,512]{1,0:T(8,128)(2,1)S(1)} collective-permute-done((bf16[384,512]{1,0:T(8,128)(2,1)S(1)}, bf16[384,512]{1,0:T(8,128)(2,1)S(1)}, u32[]{:S(2)}, u32[]{:S(2)}) %collective-permute-start.26) | collective-permute-done | bytes 393248 | tf_op jit(solution)/shard_map/ppermute | solution.py:198
  191.0 1.9 %add_convert_fusion = bf16[384,512]{1,0:T(8,128)(2,1)} fusion(bf16[384,512]{1,0:T(8,128)(2,1)S(1)} %collective-permute-done.26, bf16[384,512]{1,0:T(8,128)(2,1)S(1)} %collective-permute-done.23, bf16[384,512]{1,0:T(8,128)(2,1)S(1)} %collective-permute-done.19, bf16[384,512]{1,0:T(8,128)(2,1)} %get-tuple-element.61), kind=kLoop, calls=%fused_computation.5 | loop fusion | flops 1572864 | bytes 1966080 | tf_op jit(solution)/shard_map/convert_element_type | solution.py:344
  (56 shorter events, 1.5 us)
Async XLA Ops:
  0.0 35.9 %collective-permute-start.7 = (bf16[8192,512]{1,0:T(8,128)(2,1)}, bf16[8192,512]{1,0:T(8,128)(2,1)}, u32[]{:S(2)}, u32[]{:S(2)}) collective-permute-start(bf16[8192,512]{1,0:T(8,128)(2,1)} %refs_7_.4), channel_id=1, source_target_pairs={{0,1},{1,0},{2,3},{3,2},{4,5},{5,4},{6,7},{7,6},{8,9},{9,8},{10,11... | collective-permute-start | bytes 25165832 | tf_op jit(solution)/shard_map/ppermute | solution.py:198
  0.5 15.3 %collective-permute-start.2 = (bf16[1,64,8192]{2,1,0:T(8,128)(2,1)}, bf16[1,64,8192]{2,1,0:T(8,128)(2,1)}, u32[]{:S(2)}, u32[]{:S(2)}) collective-permute-start(bf16[1,64,8192]{2,1,0:T(8,128)(2,1)} %bitcast.37), channel_id=1, source_target_pairs={{0,1},{1,0},{2,3},{3,2},{4,5},{5,4},{6,7},{7,6},{8,9},{9,8},{10,11... | collective-permute-start | bytes 3145736 | tf_op jit(solution)/shard_map/ppermute | solution.py:198
  0.5 15.2 %collective-permute-start = (bf16[384,512]{1,0:T(8,128)(2,1)}, bf16[384,512]{1,0:T(8,128)(2,1)S(1)}, u32[]{:S(2)}, u32[]{:S(2)}) collective-permute-start(bf16[384,512]{1,0:T(8,128)(2,1)} %refs_0_.1), channel_id=1, source_target_pairs={{0,4},{4,8},{8,12},{12,0},{1,5},{5,9},{9,13},{13,1},{2,6},{6,10},{... | collective-permute-start | bytes 1179656 | tf_op jit(solution)/shard_map/ppermute | solution.py:198
  3.5 12.2 %collective-permute-start.1 = (bf16[384,512]{1,0:T(8,128)(2,1)}, bf16[384,512]{1,0:T(8,128)(2,1)S(1)}, u32[]{:S(2)}, u32[]{:S(2)}) collective-permute-start(bf16[384,512]{1,0:T(8,128)(2,1)} %refs_0_.1), channel_id=1, source_target_pairs={{0,2},{2,0},{1,3},{3,1},{4,6},{6,4},{5,7},{7,5},{8,10},{10,8},{9,1... | collective-permute-start | bytes 1179656 | tf_op jit(solution)/shard_map/ppermute | solution.py:198
  5.1 25.5 %collective-permute-start.5 = (bf16[384,512]{1,0:T(8,128)(2,1)}, bf16[384,512]{1,0:T(8,128)(2,1)}, u32[]{:S(2)}, u32[]{:S(2)}) collective-permute-start(bf16[384,512]{1,0:T(8,128)(2,1)} %refs_0_.1), channel_id=1, source_target_pairs={{0,12},{4,0},{8,4},{12,8},{1,13},{5,1},{9,5},{13,9},{2,14},{6,2},{... | collective-permute-start | bytes 1179656 | tf_op jit(solution)/shard_map/ppermute | solution.py:198
  15.7 20.1 %copy-start.6 = (bf16[384,512]{1,0:T(8,128)(2,1)}, bf16[384,512]{1,0:T(8,128)(2,1)S(1)}, u32[]{:S(2)}) copy-start(bf16[384,512]{1,0:T(8,128)(2,1)S(1)} %collective-permute-done.refs_2_) | copy-start | bytes 1179652
  15.7 16.1 %copy-start.7 = (bf16[384,512]{1,0:T(8,128)(2,1)}, bf16[384,512]{1,0:T(8,128)(2,1)S(1)}, u32[]{:S(2)}) copy-start(bf16[384,512]{1,0:T(8,128)(2,1)S(1)} %collective-permute-done.1.refs_1_) | copy-start | bytes 1179652
  15.8 16.1 %collective-permute-start.3 = (bf16[384,512]{1,0:T(8,128)(2,1)S(1)}, bf16[384,512]{1,0:T(8,128)(2,1)S(1)}, u32[]{:S(2)}, u32[]{:S(2)}) collective-permute-start(bf16[384,512]{1,0:T(8,128)(2,1)S(1)} %collective-permute-done.refs_2_), channel_id=1, source_target_pairs={{0,2},{2,0},{1,3},{3,1},{4,6},{6,4},{5,7},{7,5},{8,10},{10,8},{9,1... | collective-permute-start | bytes 1179656 | tf_op jit(solution)/shard_map/ppermute | solution.py:198
  20.3 31.4 %all-to-all-start = ((bf16[32,16,512]{2,0,1:T(8,128)(2,1)}), bf16[32,16,512]{2,0,1:T(8,128)(2,1)S(1)}, u32[]{:S(2)}, u32[]{:S(2)}) async-start(bf16[32,16,512]{2,0,1:T(8,128)(2,1)} %copy.36), calls=%async_computation | async-start | bytes 1048576 | tf_op jit(solution)/shard_map/all_to_all | solution.py:296
  30.5 20.1 %collective-permute-start.6 = (bf16[384,512]{1,0:T(8,128)(2,1)}, bf16[384,512]{1,0:T(8,128)(2,1)}, u32[]{:S(2)}, u32[]{:S(2)}) collective-permute-start(bf16[384,512]{1,0:T(8,128)(2,1)} %collective-permute-done.5.refs_3_), channel_id=1, source_target_pairs={{8,4},{4,0},{9,5},{5,1},{10,6},{6,2},{11,7},{7,3},{24,20},{20,16},... | collective-permute-start | bytes 1179656 | tf_op jit(solution)/shard_map/ppermute | solution.py:228
  31.9 1.4 copy-start.8
  31.9 18.7 %collective-permute-start.4 = (bf16[384,512]{1,0:T(8,128)(2,1)S(1)}, bf16[384,512]{1,0:T(8,128)(2,1)}, u32[]{:S(2)}, u32[]{:S(2)}) collective-permute-start(bf16[384,512]{1,0:T(8,128)(2,1)S(1)} %collective-permute-done.refs_2_), channel_id=1, source_target_pairs={{4,8},{8,12},{5,9},{9,13},{6,10},{10,14},{7,11},{11,15},{20,24},{2... | collective-permute-start | bytes 1179656 | tf_op jit(solution)/shard_map/ppermute | solution.py:226
  33.9 20.8 %copy-start.10 = (s32[384,1]{0,1:T(1,128)S(1)}, s32[384,1]{0,1:T(1,128)}, u32[]{:S(2)}) copy-start(s32[384,1]{0,1:T(1,128)} %param.13) | copy-start | bytes 4612
  33.9 20.8 %copy-start.11 = (s32[16]{0:T(128)S(1)}, s32[16]{0:T(128)}, u32[]{:S(2)}) copy-start(s32[16]{0:T(128)} %param.14) | copy-start | bytes 196
  33.9 19.3 %collective-permute-start.9 = (bf16[384,512]{1,0:T(8,128)(2,1)}, bf16[384,512]{1,0:T(8,128)(2,1)}, u32[]{:S(2)}, u32[]{:S(2)}) collective-permute-start(bf16[384,512]{1,0:T(8,128)(2,1)} %collective-permute-done.5.refs_3_), channel_id=1, source_target_pairs={{0,2},{2,0},{1,3},{3,1},{4,6},{6,4},{5,7},{7,5},{8,10},{10,8},{9,1... | collective-permute-start | bytes 1179656 | tf_op jit(solution)/shard_map/ppermute | solution.py:198
  51.7 14.4 %copy-start.2 = (bf16[384,512]{1,0:T(8,128)(2,1)}, bf16[384,512]{1,0:T(8,128)(2,1)S(1)}, u32[]{:S(2)}) copy-start(bf16[384,512]{1,0:T(8,128)(2,1)S(1)} %broadcast_select_fusion.refs_2_) | copy-start | bytes 1179652
  51.7 21.5 %copy-start.1 = (bf16[32,16,512]{2,0,1:T(8,128)(2,1)}, bf16[32,16,512]{2,0,1:T(8,128)(2,1)S(1)}, u32[]{:S(2)}) copy-start(bf16[32,16,512]{2,0,1:T(8,128)(2,1)S(1)} %all-to-all-done) | copy-start | bytes 1572868
  51.7 13.5 %collective-permute-start.8 = (bf16[512,512]{1,0:T(8,128)(2,1)S(1)}, bf16[512,512]{1,0:T(8,128)(2,1)S(1)}, u32[]{:S(2)}, u32[]{:S(2)}) collective-permute-start(bf16[512,512]{1,0:T(8,128)(2,1)S(1)} %bitcast.51), channel_id=1, source_target_pairs={{0,16},{16,0},{1,17},{17,1},{2,18},{18,2},{3,19},{19,3},{4,20},{20... | collective-permute-start | bytes 1572872 | tf_op jit(solution)/shard_map/ppermute | solution.py:300
  53.3 12.8 %collective-permute-start.10 = (bf16[384,512]{1,0:T(8,128)(2,1)S(1)}, bf16[384,512]{1,0:T(8,128)(2,1)}, u32[]{:S(2)}, u32[]{:S(2)}) collective-permute-start(bf16[384,512]{1,0:T(8,128)(2,1)S(1)} %broadcast_select_fusion.refs_2_), channel_id=1, source_target_pairs={{0,2},{2,0},{1,3},{3,1},{4,6},{6,4},{5,7},{7,5},{8,10},{10,8},{9,1... | collective-permute-start | bytes 1179656 | tf_op jit(solution)/shard_map/ppermute | solution.py:198
  55.6 45.2 %copy-start.9 = (bf16[24,1024]{1,0:T(8,128)(2,1)S(1)}, bf16[24,1024]{1,0:T(8,128)(2,1)}, u32[]{:S(2)}) copy-start(bf16[24,1024]{1,0:T(8,128)(2,1)} %param.21) | copy-start | bytes 147460
  55.6 46.1 %copy-start.12 = (s32[24]{0:T(128)S(1)}, s32[24]{0:T(128)}, u32[]{:S(2)}) copy-start(s32[24]{0:T(128)} %param.15) | copy-start | bytes 292
  65.2 0.8 copy-start.5
  73.2 7.8 %collective-permute-start.13 = (f32[384,512]{1,0:T(8,128)}, f32[384,512]{1,0:T(8,128)S(1)}, u32[]{:S(2)}, u32[]{:S(2)}) collective-permute-start(f32[384,512]{1,0:T(8,128)} %get-tuple-element.56), channel_id=1, source_target_pairs={{0,1},{1,0},{2,3},{3,2},{4,5},{5,4},{6,7},{7,6},{8,9},{9,8},{10,11... | collective-permute-start | bytes 2359304 | tf_op jit(solution)/shard_map/ppermute | solution.py:198
  73.3 2.6 %collective-permute-start.11 = (f32[192,128]{1,0:T(8,128)}, f32[192,128]{1,0:T(8,128)S(1)}, u32[]{:S(2)}, u32[]{:S(2)}) collective-permute-start(f32[192,128]{1,0:T(8,128)} %get-tuple-element.55), channel_id=1, source_target_pairs={{0,1},{1,0},{2,3},{3,2},{4,5},{5,4},{6,7},{7,6},{8,9},{9,8},{10,11... | collective-permute-start | bytes 294920 | tf_op jit(solution)/shard_map/ppermute | solution.py:198
  76.8 4.2 %collective-permute-start.12 = (bf16[192,128]{1,0:T(8,128)(2,1)S(1)}, bf16[192,128]{1,0:T(8,128)(2,1)S(1)}, u32[]{:S(2)}, u32[]{:S(2)}) collective-permute-start(bf16[192,128]{1,0:T(8,128)(2,1)S(1)} %add_convert_fusion.4), channel_id=1, source_target_pairs={{0,2},{2,0},{1,3},{3,1},{4,6},{6,4},{5,7},{7,5},{8,10},{10,8},{9,1... | collective-permute-start | bytes 147464 | tf_op jit(solution)/shard_map/ppermute | solution.py:198
  81.0 10.5 %copy-start.4 = (f32[384,512]{1,0:T(8,128)}, f32[384,512]{1,0:T(8,128)S(1)}, u32[]{:S(2)}) copy-start(f32[384,512]{1,0:T(8,128)S(1)} %collective-permute-done.13.received) | copy-start | bytes 2359300
  81.0 7.3 %collective-permute-start.14 = (bf16[192,128]{1,0:T(8,128)(2,1)S(1)}, bf16[192,128]{1,0:T(8,128)(2,1)S(1)}, u32[]{:S(2)}, u32[]{:S(2)}) collective-permute-start(bf16[192,128]{1,0:T(8,128)(2,1)S(1)} %add.217), channel_id=1, source_target_pairs={{0,4},{4,8},{8,12},{12,0},{1,5},{5,9},{9,13},{13,1},{2,6},{6,10},{... | collective-permute-start | bytes 147464 | tf_op jit(solution)/shard_map/ppermute | solution.py:198
  85.4 5.5 %collective-permute-start.15 = (bf16[192,128]{1,0:T(8,128)(2,1)S(1)}, bf16[192,128]{1,0:T(8,128)(2,1)S(1)}, u32[]{:S(2)}, u32[]{:S(2)}) collective-permute-start(bf16[192,128]{1,0:T(8,128)(2,1)S(1)} %add.217), channel_id=1, source_target_pairs={{0,8},{4,12},{8,0},{12,4},{1,9},{5,13},{9,1},{13,5},{2,10},{6,14},... | collective-permute-start | bytes 147464 | tf_op jit(solution)/shard_map/ppermute | solution.py:198
  85.5 5.4 %collective-permute-start.16 = (bf16[192,128]{1,0:T(8,128)(2,1)S(1)}, bf16[192,128]{1,0:T(8,128)(2,1)S(1)}, u32[]{:S(2)}, u32[]{:S(2)}) collective-permute-start(bf16[192,128]{1,0:T(8,128)(2,1)S(1)} %add.217), channel_id=1, source_target_pairs={{0,12},{4,0},{8,4},{12,8},{1,13},{5,1},{9,5},{13,9},{2,14},{6,2},{... | collective-permute-start | bytes 147464 | tf_op jit(solution)/shard_map/ppermute | solution.py:198
  95.1 47.2 %collective-permute-start.18 = (bf16[512,8192]{1,0:T(8,128)(2,1)}, bf16[512,8192]{1,0:T(8,128)(2,1)}, u32[]{:S(2)}, u32[]{:S(2)}) collective-permute-start(bf16[512,8192]{1,0:T(8,128)(2,1)} %refs_2_.3), channel_id=1, source_target_pairs={{0,1},{1,0},{2,3},{3,2},{4,5},{5,4},{6,7},{7,6},{8,9},{9,8},{10,11... | collective-permute-start | bytes 25165832 | tf_op jit(solution)/shard_map/ppermute | solution.py:198
  95.1 18.0 %all-to-all-start.1 = ((bf16[16,24,512]{2,1,0:T(8,128)(2,1)}), bf16[16,24,512]{2,1,0:T(8,128)(2,1)S(1)}, u32[]{:S(2)}, u32[]{:S(2)}) async-start(bf16[16,24,512]{2,1,0:T(8,128)(2,1)} %bitcast.55), calls=%async_computation.1 | async-start | bytes 786432 | tf_op jit(solution)/shard_map/all_to_all | solution.py:315
  140.6 1.7 copy-start
  140.6 1.7 collective-permute-start.17
  142.3 0.8 copy-start.3
  146.6 11.8 %collective-permute-start.21 = (bf16[384,512]{1,0:T(8,128)(2,1)}, bf16[384,512]{1,0:T(8,128)(2,1)S(1)}, u32[]{:S(2)}, u32[]{:S(2)}) collective-permute-start(bf16[384,512]{1,0:T(8,128)(2,1)} %shard_map.122), channel_id=1, source_target_pairs={{0,2},{2,0},{1,3},{3,1},{4,6},{6,4},{5,7},{7,5},{8,10},{10,8},{9,1... | collective-permute-start | bytes 1179656 | tf_op jit(solution)/shard_map/ppermute | solution.py:198
  154.5 12.2 %collective-permute-start.20 = (bf16[384,512]{1,0:T(8,128)(2,1)}, bf16[384,512]{1,0:T(8,128)(2,1)S(1)}, u32[]{:S(2)}, u32[]{:S(2)}) collective-permute-start(bf16[384,512]{1,0:T(8,128)(2,1)} %get-tuple-element.65), channel_id=1, source_target_pairs={{0,2},{2,0},{1,3},{3,1},{4,6},{6,4},{5,7},{7,5},{8,10},{10,8},{9,1... | collective-permute-start | bytes 1179656 | tf_op jit(solution)/shard_map/ppermute | solution.py:198
  159.4 10.7 %collective-permute-start.22 = (bf16[384,512]{1,0:T(8,128)(2,1)S(1)}, bf16[384,512]{1,0:T(8,128)(2,1)S(1)}, u32[]{:S(2)}, u32[]{:S(2)}) collective-permute-start(bf16[384,512]{1,0:T(8,128)(2,1)S(1)} %add_convert_fusion.3), channel_id=1, source_target_pairs={{0,4},{4,8},{1,5},{5,9},{2,6},{6,10},{3,7},{7,11},{16,20},{20,24},... | collective-permute-start | bytes 1179656 | tf_op jit(solution)/shard_map/ppermute | solution.py:244
  162.5 12.7 %collective-permute-start.24 = (bf16[384,512]{1,0:T(8,128)(2,1)}, bf16[384,512]{1,0:T(8,128)(2,1)S(1)}, u32[]{:S(2)}, u32[]{:S(2)}) collective-permute-start(bf16[384,512]{1,0:T(8,128)(2,1)} %get-tuple-element.70), channel_id=1, source_target_pairs={{0,2},{2,0},{1,3},{3,1},{4,6},{6,4},{5,7},{7,5},{8,10},{10,8},{9,1... | collective-permute-start | bytes 1179656 | tf_op jit(solution)/shard_map/ppermute | solution.py:198
  163.0 12.2 %collective-permute-start.25 = (bf16[384,512]{1,0:T(8,128)(2,1)S(1)}, bf16[384,512]{1,0:T(8,128)(2,1)S(1)}, u32[]{:S(2)}, u32[]{:S(2)}) collective-permute-start(bf16[384,512]{1,0:T(8,128)(2,1)S(1)} %add_convert_fusion.3), channel_id=1, source_target_pairs={{12,8},{8,4},{13,9},{9,5},{14,10},{10,6},{15,11},{11,7},{28,24},{2... | collective-permute-start | bytes 1179656 | tf_op jit(solution)/shard_map/ppermute | solution.py:245
  163.7 19.5 %collective-permute-start.19 = (bf16[384,512]{1,0:T(8,128)(2,1)}, bf16[384,512]{1,0:T(8,128)(2,1)S(1)}, u32[]{:S(2)}, u32[]{:S(2)}) collective-permute-start(bf16[384,512]{1,0:T(8,128)(2,1)} %get-tuple-element.62), channel_id=1, source_target_pairs={{0,2},{2,0},{1,3},{3,1},{4,6},{6,4},{5,7},{7,5},{8,10},{10,8},{9,1... | collective-permute-start | bytes 1179656 | tf_op jit(solution)/shard_map/ppermute | solution.py:198
  171.3 13.9 %collective-permute-start.23 = (bf16[384,512]{1,0:T(8,128)(2,1)S(1)}, bf16[384,512]{1,0:T(8,128)(2,1)S(1)}, u32[]{:S(2)}, u32[]{:S(2)}) collective-permute-start(bf16[384,512]{1,0:T(8,128)(2,1)S(1)} %add_convert_fusion.2), channel_id=1, source_target_pairs={{0,4},{4,8},{8,12},{12,0},{1,5},{5,9},{9,13},{13,1},{2,6},{6,10},{... | collective-permute-start | bytes 1179656 | tf_op jit(solution)/shard_map/ppermute | solution.py:198
  176.3 14.7 %collective-permute-start.26 = (bf16[384,512]{1,0:T(8,128)(2,1)S(1)}, bf16[384,512]{1,0:T(8,128)(2,1)S(1)}, u32[]{:S(2)}, u32[]{:S(2)}) collective-permute-start(bf16[384,512]{1,0:T(8,128)(2,1)S(1)} %add_convert_fusion.1), channel_id=1, source_target_pairs={{0,12},{4,0},{8,4},{12,8},{1,13},{5,1},{9,5},{13,9},{2,14},{6,2},{... | collective-permute-start | bytes 1179656 | tf_op jit(solution)/shard_map/ppermute | solution.py:198

commit v4 on v3

--- a/solution.py
+++ b/solution.py
@@ -226,7 +226,7 @@
     from_below = lax.ppermute(after(below, below_side), "z", [(1, 2), (2, 3)])
     above_side = shift(above, "y", 1)
     from_above = lax.ppermute(above, "z", [(2, 1), (1, 0)])
-    sums = begin([tokens, side, below, above])
+    sums = begin([after(tokens, up), side, below, above])
     from_below, from_above, sums = lax.optimization_barrier((from_below, from_above, sums))
     two = jnp.where(z >= 2, from_below, from_above)
     two, _, up = lax.optimization_barrier((two, below_side, up))

time: 194 us -> 190 us (0.979)
  starting transfers between devices: 55.4 us -> 51.2 us
    all_to_all x1, starting transfers between devices: 10.2 us -> 4.08 us  [shards(): up = lax.all_to_all(up, ADP, split_axis=1, concat_axis=0, tiled=True)]
    ppermute x22, waiting for transfers between devices: 35 us -> 40.7 us  [shift(): lax.ppermute(value, axis, [(i, (i + by) % size) for i in range(size)])]
    ppermute x1, waiting for transfers between devices: 8.2 us -> 3.02 us  [gather_features(): from_above = lax.ppermute(above, 'z', [(2, 1), (1, 0)])]
  transfers between devices with their start and end apart: 29 -> 29, of which waited for: 15 -> 16; matrix products, arithmetic and copies ran while one was open for 11% -> 12% of each run, Pallas kernels for 7% -> 7%
where the time goes in v4:
time: 190 us; the launch traced here: 189 us
  waiting for transfers between devices  67.2 us (35%)
  starting transfers between devices  51.2 us (27%)
  Pallas kernels  28.3 us (15%)
  blocking collectives  15.5 us (8%)
  matrix products  10.5 us (6%)
  other arithmetic  9.52 us (5%)
  local copies, waits for them, and re-layouts  6.16 us (3%)
    ppermute x22, waiting for transfers between devices, shift(): lax.ppermute(value, axis, [(i, (i + by) % size) for i in range(size)])  40.7 us
    ppermute x22, starting transfers between devices, shift(): lax.ppermute(value, axis, [(i, (i + by) % size) for i in range(size)])  33.2 us
    all_to_all x1, blocking collectives, shards(): lax.all_to_all(context, ADP, split_axis=0, concat_axis=0, tiled=True)  15.5 us
    pallas_call x2, Pallas kernels, project(): pl.pallas_call(kernel, grid_spec=pltpu.PrefetchScalarGridSpec(num_scalar_...  13.9 us
    all_to_all x1, waiting for transfers between devices, shards(): lax.all_to_all(query, ADP, split_axis=0, concat_axis=1, tiled=True)  11.3 us
    pallas_call x2, Pallas kernels, output_partial(): pl.pallas_call(kernel, grid_spec=pltpu.PrefetchScalarGridSpec(num_scalar_...  10.8 us
    ppermute x1, waiting for transfers between devices, shards(): lax.ppermute(up, 'rep', [(i, i ^ 1) for i in range(lax.axis_size('rep'))])  8.93 us
    all_to_all x1, starting transfers between devices, shards(): lax.all_to_all(query, ADP, split_axis=0, concat_axis=1, tiled=True)  5.9 us
  transfers between devices with their start and end apart: 29, of which 16 were waited for; matrix products, arithmetic and copies ran while one was open for 12% of the time, Pallas kernels for 7%

profile of v4, /device:TPU:0, one launch (start us, length us, event | category | flops | bytes accessed | tf_op | source)
XLA Modules:
  0.0 188.7 jit_solution(9157731056909073204)
XLA Ops:
  0.0 0.5 collective-permute-start.7
  0.5 2.6 %collective-permute-start = (bf16[384,512]{1,0:T(8,128)(2,1)}, bf16[384,512]{1,0:T(8,128)(2,1)S(1)}, u32[]{:S(2)}, u32[]{:S(2)}) collective-permute-start(bf16[384,512]{1,0:T(8,128)(2,1)} %refs_0_), channel_id=1, source_target_pairs={{0,4},{4,8},{8,12},{12,0},{1,5},{5,9},{9,13},{13,1},{2,6},{6,10},{... | collective-permute-start | bytes 1179656 | tf_op jit(solution)/shard_map/ppermute | solution.py:198
  3.0 1.5 collective-permute-start.1
  4.6 1.1 constant_dynamic-slice_fusion
  5.8 1.1 copy.36
  6.9 4.1 %all-to-all-start = ((bf16[32,16,512]{2,0,1:T(8,128)(2,1)}), bf16[32,16,512]{2,0,1:T(8,128)(2,1)S(1)}, u32[]{:S(2)}, u32[]{:S(2)}) async-start(bf16[32,16,512]{2,0,1:T(8,128)(2,1)} %copy.36), calls=%async_computation | async-start | bytes 1048576 | tf_op jit(solution)/shard_map/all_to_all | solution.py:296
  11.0 3.7 %collective-permute-start.5 = (bf16[384,512]{1,0:T(8,128)(2,1)}, bf16[384,512]{1,0:T(8,128)(2,1)}, u32[]{:S(2)}, u32[]{:S(2)}) collective-permute-start(bf16[384,512]{1,0:T(8,128)(2,1)} %refs_0_), channel_id=1, source_target_pairs={{0,12},{4,0},{8,4},{12,8},{1,13},{5,1},{9,5},{13,9},{2,14},{6,2},{... | collective-permute-start | bytes 1179656 | tf_op jit(solution)/shard_map/ppermute | solution.py:198
  14.7 0.5 collective-permute-done.refs_2_
  15.2 2.9 %collective-permute-start.3 = (bf16[384,512]{1,0:T(8,128)(2,1)S(1)}, bf16[384,512]{1,0:T(8,128)(2,1)S(1)}, u32[]{:S(2)}, u32[]{:S(2)}) collective-permute-start(bf16[384,512]{1,0:T(8,128)(2,1)S(1)} %collective-permute-done.refs_2_), channel_id=1, source_target_pairs={{0,2},{2,0},{1,3},{3,1},{4,6},{6,4},{5,7},{7,5},{8,10},{10,8},{9,1... | collective-permute-start | bytes 1179656 | tf_op jit(solution)/shard_map/ppermute | solution.py:198
  18.0 14.0 %collective-permute-done.5.refs_3_ = bf16[384,512]{1,0:T(8,128)(2,1)} collective-permute-done((bf16[384,512]{1,0:T(8,128)(2,1)}, bf16[384,512]{1,0:T(8,128)(2,1)}, u32[]{:S(2)}, u32[]{:S(2)}) %collective-permute-start.5) | collective-permute-done | bytes 393248 | tf_op jit(solution)/shard_map/ppermute | solution.py:198
  32.0 1.3 collective-permute-start.6
  33.3 1.4 collective-permute-start.4
  34.7 0.6 stack.43.places
  35.3 1.5 collective-permute-start.9
  36.9 6.7 %shard_map.118 = (f32[384,512]{1,0:T(8,128)}, f32[384,512]{1,0:T(8,128)}, f32[384,128]{1,0:T(8,128)}) custom-call(s32[16]{0:T(128)} %stack.43.places, bf16[384,512]{1,0:T(8,128)(2,1)} %refs_0_, bf16[384,512]{1,0:T(8,128)(2,1)} %copy-done.6, bf16[384,512]{1,0:T(8,128)(2,1)} %copy-done.5, bf16[384,512]{1,0:T(8,128)(2,1)} %collective-permute-done.5.refs_3_, ...), custom_call_target="tpu_custom_call" | custom-call | flops 1811939328 | bytes 7340032 | tf_op jit(solution)/shard_map/pallas_call | solution.py:64
  43.6 3.0 %collective-permute-done.6 = bf16[384,512]{1,0:T(8,128)(2,1)} collective-permute-done((bf16[384,512]{1,0:T(8,128)(2,1)}, bf16[384,512]{1,0:T(8,128)(2,1)}, u32[]{:S(2)}, u32[]{:S(2)}) %collective-permute-start.6) | collective-permute-done | bytes 393248 | tf_op jit(solution)/shard_map/ppermute | solution.py:228
  46.6 1.0 broadcast_select_fusion.refs_2_
  47.7 1.6 collective-permute-start.8
  49.2 1.6 collective-permute-start.10
  51.0 0.8 broadcast_in_dim.46.refs_23_.slot
  51.8 8.9 %collective-permute-done.8.up_other = bf16[512,512]{1,0:T(8,128)(2,1)S(1)} collective-permute-done((bf16[512,512]{1,0:T(8,128)(2,1)S(1)}, bf16[512,512]{1,0:T(8,128)(2,1)S(1)}, u32[]{:S(2)}, u32[]{:S(2)}) %collective-permute-start.8) | collective-permute-done | bytes 524320 | tf_op jit(solution)/shard_map/ppermute | solution.py:300
  60.7 0.8 copy-done.4
  61.5 7.2 %shard_map.119 = (f32[384,512]{1,0:T(8,128)}, f32[384,512]{1,0:T(8,128)}, f32[192,128]{1,0:T(8,128)}) custom-call(s32[16]{0:T(128)} %stack.43.places, bf16[384,512]{1,0:T(8,128)(2,1)} %copy-done.7, bf16[384,512]{1,0:T(8,128)(2,1)} %collective-permute-done.9.refs_1_, bf16[384,512]{1,0:T(8,128)(2,1)} %copy-done.2, ...), custom_call_target="tpu_custom_call" | custom-call | flops 1811939328 | bytes 7340032 | tf_op jit(solution)/shard_map/pallas_call | solution.py:64
  68.7 0.5 collective-permute-start.11
  69.2 1.9 %collective-permute-done.11 = f32[192,128]{1,0:T(8,128)S(1)} collective-permute-done((f32[192,128]{1,0:T(8,128)}, f32[192,128]{1,0:T(8,128)S(1)}, u32[]{:S(2)}, u32[]{:S(2)}) %collective-permute-start.11) | collective-permute-done | bytes 98336 | tf_op jit(solution)/shard_map/ppermute | solution.py:198
  71.1 0.9 add_convert_fusion.4
  72.0 1.7 collective-permute-start.12
  73.8 2.4 %collective-permute-done.12 = bf16[192,128]{1,0:T(8,128)(2,1)S(1)} collective-permute-done((bf16[192,128]{1,0:T(8,128)(2,1)S(1)}, bf16[192,128]{1,0:T(8,128)(2,1)S(1)}, u32[]{:S(2)}, u32[]{:S(2)}) %collective-permute-start.12) | collective-permute-done | bytes 49184 | tf_op jit(solution)/shard_map/ppermute | solution.py:198
  76.2 4.9 %collective-permute-start.14 = (bf16[192,128]{1,0:T(8,128)(2,1)S(1)}, bf16[192,128]{1,0:T(8,128)(2,1)S(1)}, u32[]{:S(2)}, u32[]{:S(2)}) collective-permute-start(bf16[192,128]{1,0:T(8,128)(2,1)S(1)} %add.217), channel_id=1, source_target_pairs={{0,4},{4,8},{8,12},{12,0},{1,5},{5,9},{9,13},{13,1},{2,6},{6,10},{... | collective-permute-start | bytes 147464 | tf_op jit(solution)/shard_map/ppermute | solution.py:198
  81.1 0.5 collective-permute-start.15
  81.6 2.3 %collective-permute-start.16 = (bf16[192,128]{1,0:T(8,128)(2,1)S(1)}, bf16[192,128]{1,0:T(8,128)(2,1)S(1)}, u32[]{:S(2)}, u32[]{:S(2)}) collective-permute-start(bf16[192,128]{1,0:T(8,128)(2,1)S(1)} %add.217), channel_id=1, source_target_pairs={{0,12},{4,0},{8,4},{12,8},{1,13},{5,1},{9,5},{13,9},{2,14},{6,2},{... | collective-permute-start | bytes 147464 | tf_op jit(solution)/shard_map/ppermute | solution.py:198
  83.9 2.6 %collective-permute-done.15 = bf16[192,128]{1,0:T(8,128)(2,1)S(1)} collective-permute-done((bf16[192,128]{1,0:T(8,128)(2,1)S(1)}, bf16[192,128]{1,0:T(8,128)(2,1)S(1)}, u32[]{:S(2)}, u32[]{:S(2)}) %collective-permute-start.15) | collective-permute-done | bytes 49184 | tf_op jit(solution)/shard_map/ppermute | solution.py:198
  86.5 0.6 add_add_fusion.low
  87.1 3.6 %shard_map.120 = bf16[384,512]{1,0:T(8,128)(2,1)} custom-call(s32[1]{0:T(128)} %bitcast.8.half, f32[384,512]{1,0:T(8,128)} %get-tuple-element.56.own, f32[384,512]{1,0:T(8,128)} %collective-permute-done.13.received, bf16[192,128]{1,0:T(8,128)(2,1)} %add_add_fusion.low, s32[384,1]{1,0:T(8,128)} %broadcast_in_dim.46.refs_23_.slot, bf16[512,512]{1,0:T(8,128)(2,1)} %bitcast.52, ...), custom_call_target="tpu_custom_call" | custom-call | flops 1 | bytes 1 | tf_op jit(solution)/shard_map/pallas_call | solution.py:119
  90.7 5.9 %all-to-all-start.1 = ((bf16[16,24,512]{2,1,0:T(8,128)(2,1)}), bf16[16,24,512]{2,1,0:T(8,128)(2,1)S(1)}, u32[]{:S(2)}, u32[]{:S(2)}) async-start(bf16[16,24,512]{2,1,0:T(8,128)(2,1)} %bitcast.55), calls=%async_computation.1 | async-start | bytes 786432 | tf_op jit(solution)/shard_map/all_to_all | solution.py:315
  96.6 0.8 convert_bitcast_fusion
  97.6 11.3 %all-to-all-done.1 = bf16[16,24,512]{2,1,0:T(8,128)(2,1)S(1)} async-done(((bf16[16,24,512]{2,1,0:T(8,128)(2,1)}), bf16[16,24,512]{2,1,0:T(8,128)(2,1)S(1)}, u32[]{:S(2)}, u32[]{:S(2)}) %all-to-all-start.1) | async-done | bytes 393248 | tf_op jit(solution)/shard_map/all_to_all | solution.py:315
  109.5 5.5 %fusion.15 = (f32[8,24,8]{2,1,0:T(8,128)S(1)}, f32[8,24,8,128]{3,2,1,0:T(8,128)S(1)}) fusion(bf16[8,24,128,128]{3,2,1,0:T(8,128)(2,1)} %param.19, bf16[24,8,8,128]{3,2,1,0:T(8,128)(2,1)S(1)} %reshape.48, pred[24,128]{1,0:T(8,128)(4,1)S(1)} %iota_compare_fusion.1), kind=kOutput, calls=%fused_computation.30 | convolution fusion | flops 50723328 | bytes 7480320 | tf_op jit(solution)/shard_map/rkge,krje->krgj/dot_general | solution.py:182
  115.1 0.6 fusion.8
  115.7 4.6 %fusion.5 = bf16[24,8,8,128]{3,2,1,0:T(8,128)(2,1)S(1)} fusion(bf16[8,24,128,128]{3,2,1,0:T(8,128)(2,1)} %param.20, f32[24,8,128]{2,1,0:T(8,128)S(1)} %bitcast.58, f32[24,8,8]{2,1,0:T(8,128)S(1)} %copy.43, f32[8,24,8,128]{3,2,1,0:T(8,128)S(1)} %get-tuple-element.76, f32[8,24,8]{2,1,0:T(8,128)S(1)} %get-tuple-element.74, f32[8,24,8]{2,1,0:T(8,128)S(1)} %max.3, ...), kind=kOutput, calls=%fused_computation.4 | convolution fusion | flops 51707904 | bytes 7590912 | tf_op jit(solution)/shard_map/krgj,krje->rkge/dot_general | solution.py:191
  120.8 15.5 %all_to_all.40 = bf16[16,24,512]{2,1,0:T(8,128)(2,1)S(1)} all-to-all(bf16[16,24,512]{2,1,0:T(8,128)(2,1)S(1)} %bitcast.54), channel_id=1, replica_groups=mesh['rep'=2,'z'=4,'y'=2,'core'=2] {'z','y','core'}, dimensions={0} | all-to-all | bytes 786432 | tf_op jit(solution)/shard_map/all_to_all | solution.py:321
  136.4 1.6 collective-permute-done.17.refs_1_
  138.0 0.8 copy-done.3
  138.8 3.4 %shard_map.122 = bf16[384,512]{1,0:T(8,128)(2,1)} custom-call(s32[16]{0:T(128)} %stack.43.places, bf16[384,512]{1,0:T(8,128)(2,1)} %bitcast.47, bf16[384,512]{1,0:T(8,128)(2,1)} %copy-done.3, bf16[512,8192]{1,0:T(8,128)(2,1)} %refs_2_.3, bf16[512,8192]{1,0:T(8,128)(2,1)} %collective-permute-done.18.refs_9_.refs_10_.refs_11_.refs_12_.refs_13_.refs_14_.refs_15_.refs_3_), custom_call_target="tpu_custom_call" | custom-call | flops 1 | bytes 1 | tf_op jit(solution)/shard_map/pallas_call | solution.py:160
  142.3 0.6 collective-permute-start.21
  142.9 7.3 %shard_map.121 = (bf16[384,512]{1,0:T(8,128)(2,1)}, bf16[384,512]{1,0:T(8,128)(2,1)}, bf16[384,512]{1,0:T(8,128)(2,1)}, bf16[384,512]{1,0:T(8,128)(2,1)}, bf16[3...) custom-call(s32[16]{0:T(128)} %stack.43.places, bf16[384,512]{1,0:T(8,128)(2,1)} %bitcast.48, ...), custom_call_target="tpu_custom_call" | custom-call | flops 1 | bytes 1 | tf_op jit(solution)/shard_map/pallas_call | solution.py:160
  150.2 1.5 collective-permute-start.20
  151.7 2.4 %collective-permute-done.21 = bf16[384,512]{1,0:T(8,128)(2,1)S(1)} collective-permute-done((bf16[384,512]{1,0:T(8,128)(2,1)}, bf16[384,512]{1,0:T(8,128)(2,1)S(1)}, u32[]{:S(2)}, u32[]{:S(2)}) %collective-permute-start.21) | collective-permute-done | bytes 393248 | tf_op jit(solution)/shard_map/ppermute | solution.py:198
  154.0 1.1 add_convert_fusion.3
  155.1 3.1 %collective-permute-start.22 = (bf16[384,512]{1,0:T(8,128)(2,1)S(1)}, bf16[384,512]{1,0:T(8,128)(2,1)S(1)}, u32[]{:S(2)}, u32[]{:S(2)}) collective-permute-start(bf16[384,512]{1,0:T(8,128)(2,1)S(1)} %add_convert_fusion.3), channel_id=1, source_target_pairs={{0,4},{4,8},{1,5},{5,9},{2,6},{6,10},{3,7},{7,11},{16,20},{20,24},... | collective-permute-start | bytes 1179656 | tf_op jit(solution)/shard_map/ppermute | solution.py:244
  158.2 0.5 collective-permute-start.24
  158.7 0.7 collective-permute-start.25
  159.4 1.6 collective-permute-start.19
  161.1 1.4 collective-permute-done.20
  162.5 3.4 %collective-permute-done.22 = bf16[384,512]{1,0:T(8,128)(2,1)S(1)} collective-permute-done((bf16[384,512]{1,0:T(8,128)(2,1)S(1)}, bf16[384,512]{1,0:T(8,128)(2,1)S(1)}, u32[]{:S(2)}, u32[]{:S(2)}) %collective-permute-start.22) | collective-permute-done | bytes 393248 | tf_op jit(solution)/shard_map/ppermute | solution.py:244
  165.8 1.1 add_convert_fusion.2
  167.0 2.5 %collective-permute-start.23 = (bf16[384,512]{1,0:T(8,128)(2,1)S(1)}, bf16[384,512]{1,0:T(8,128)(2,1)S(1)}, u32[]{:S(2)}, u32[]{:S(2)}) collective-permute-start(bf16[384,512]{1,0:T(8,128)(2,1)S(1)} %add_convert_fusion.2), channel_id=1, source_target_pairs={{0,4},{4,8},{8,12},{12,0},{1,5},{5,9},{9,13},{13,1},{2,6},{6,10},{... | collective-permute-start | bytes 1179656 | tf_op jit(solution)/shard_map/ppermute | solution.py:198
  169.5 1.4 collective-permute-done.24
  170.9 1.1 add_convert_fusion.1
  172.0 2.1 %collective-permute-start.26 = (bf16[384,512]{1,0:T(8,128)(2,1)S(1)}, bf16[384,512]{1,0:T(8,128)(2,1)S(1)}, u32[]{:S(2)}, u32[]{:S(2)}) collective-permute-start(bf16[384,512]{1,0:T(8,128)(2,1)S(1)} %add_convert_fusion.1), channel_id=1, source_target_pairs={{0,12},{4,0},{8,4},{12,8},{1,13},{5,1},{9,5},{13,9},{2,14},{6,2},{... | collective-permute-start | bytes 1179656 | tf_op jit(solution)/shard_map/ppermute | solution.py:198
  174.2 4.7 %collective-permute-done.19 = bf16[384,512]{1,0:T(8,128)(2,1)S(1)} collective-permute-done((bf16[384,512]{1,0:T(8,128)(2,1)}, bf16[384,512]{1,0:T(8,128)(2,1)S(1)}, u32[]{:S(2)}, u32[]{:S(2)}) %collective-permute-start.19) | collective-permute-done | bytes 393248 | tf_op jit(solution)/shard_map/ppermute | solution.py:198
  178.9 2.0 %collective-permute-done.23 = bf16[384,512]{1,0:T(8,128)(2,1)S(1)} collective-permute-done((bf16[384,512]{1,0:T(8,128)(2,1)S(1)}, bf16[384,512]{1,0:T(8,128)(2,1)S(1)}, u32[]{:S(2)}, u32[]{:S(2)}) %collective-permute-start.23) | collective-permute-done | bytes 393248 | tf_op jit(solution)/shard_map/ppermute | solution.py:198
  180.9 5.8 %collective-permute-done.26 = bf16[384,512]{1,0:T(8,128)(2,1)S(1)} collective-permute-done((bf16[384,512]{1,0:T(8,128)(2,1)S(1)}, bf16[384,512]{1,0:T(8,128)(2,1)S(1)}, u32[]{:S(2)}, u32[]{:S(2)}) %collective-permute-start.26) | collective-permute-done | bytes 393248 | tf_op jit(solution)/shard_map/ppermute | solution.py:198
  186.7 1.9 %add_convert_fusion = bf16[384,512]{1,0:T(8,128)(2,1)} fusion(bf16[384,512]{1,0:T(8,128)(2,1)S(1)} %collective-permute-done.26, bf16[384,512]{1,0:T(8,128)(2,1)S(1)} %collective-permute-done.23, bf16[384,512]{1,0:T(8,128)(2,1)S(1)} %collective-permute-done.19, bf16[384,512]{1,0:T(8,128)(2,1)} %get-tuple-element.63), kind=kLoop, calls=%fused_computation.5 | loop fusion | flops 1572864 | bytes 1966080 | tf_op jit(solution)/shard_map/convert_element_type | solution.py:344
  (54 shorter events, 1.9 us)
Async XLA Ops:
  0.0 36.9 %collective-permute-start.7 = (bf16[8192,512]{1,0:T(8,128)(2,1)}, bf16[8192,512]{1,0:T(8,128)(2,1)}, u32[]{:S(2)}, u32[]{:S(2)}) collective-permute-start(bf16[8192,512]{1,0:T(8,128)(2,1)} %refs_7_.4), channel_id=1, source_target_pairs={{0,1},{1,0},{2,3},{3,2},{4,5},{5,4},{6,7},{7,6},{8,9},{9,8},{10,11... | collective-permute-start | bytes 25165832 | tf_op jit(solution)/shard_map/ppermute | solution.py:198
  0.5 14.7 %collective-permute-start = (bf16[384,512]{1,0:T(8,128)(2,1)}, bf16[384,512]{1,0:T(8,128)(2,1)S(1)}, u32[]{:S(2)}, u32[]{:S(2)}) collective-permute-start(bf16[384,512]{1,0:T(8,128)(2,1)} %refs_0_), channel_id=1, source_target_pairs={{0,4},{4,8},{8,12},{12,0},{1,5},{5,9},{9,13},{13,1},{2,6},{6,10},{... | collective-permute-start | bytes 1179656 | tf_op jit(solution)/shard_map/ppermute | solution.py:198
  3.0 12.1 %collective-permute-start.1 = (bf16[384,512]{1,0:T(8,128)(2,1)}, bf16[384,512]{1,0:T(8,128)(2,1)S(1)}, u32[]{:S(2)}, u32[]{:S(2)}) collective-permute-start(bf16[384,512]{1,0:T(8,128)(2,1)} %refs_0_), channel_id=1, source_target_pairs={{0,2},{2,0},{1,3},{3,1},{4,6},{6,4},{5,7},{7,5},{8,10},{10,8},{9,1... | collective-permute-start | bytes 1179656 | tf_op jit(solution)/shard_map/ppermute | solution.py:198
  4.5 10.6 %collective-permute-start.2 = (bf16[1,64,8192]{2,1,0:T(8,128)(2,1)}, bf16[1,64,8192]{2,1,0:T(8,128)(2,1)}, u32[]{:S(2)}, u32[]{:S(2)}) collective-permute-start(bf16[1,64,8192]{2,1,0:T(8,128)(2,1)} %bitcast.37), channel_id=1, source_target_pairs={{0,1},{1,0},{2,3},{3,2},{4,5},{5,4},{6,7},{7,6},{8,9},{9,8},{10,11... | collective-permute-start | bytes 3145736 | tf_op jit(solution)/shard_map/ppermute | solution.py:198
  6.9 30.0 %all-to-all-start = ((bf16[32,16,512]{2,0,1:T(8,128)(2,1)}), bf16[32,16,512]{2,0,1:T(8,128)(2,1)S(1)}, u32[]{:S(2)}, u32[]{:S(2)}) async-start(bf16[32,16,512]{2,0,1:T(8,128)(2,1)} %copy.36), calls=%async_computation | async-start | bytes 1048576 | tf_op jit(solution)/shard_map/all_to_all | solution.py:296
  11.0 21.0 %collective-permute-start.5 = (bf16[384,512]{1,0:T(8,128)(2,1)}, bf16[384,512]{1,0:T(8,128)(2,1)}, u32[]{:S(2)}, u32[]{:S(2)}) collective-permute-start(bf16[384,512]{1,0:T(8,128)(2,1)} %refs_0_), channel_id=1, source_target_pairs={{0,12},{4,0},{8,4},{12,8},{1,13},{5,1},{9,5},{13,9},{2,14},{6,2},{... | collective-permute-start | bytes 1179656 | tf_op jit(solution)/shard_map/ppermute | solution.py:198
  15.1 21.7 %copy-start.5 = (bf16[384,512]{1,0:T(8,128)(2,1)}, bf16[384,512]{1,0:T(8,128)(2,1)S(1)}, u32[]{:S(2)}) copy-start(bf16[384,512]{1,0:T(8,128)(2,1)S(1)} %collective-permute-done.refs_2_) | copy-start | bytes 1179652
  15.2 21.7 %copy-start.6 = (bf16[384,512]{1,0:T(8,128)(2,1)}, bf16[384,512]{1,0:T(8,128)(2,1)S(1)}, u32[]{:S(2)}) copy-start(bf16[384,512]{1,0:T(8,128)(2,1)S(1)} %collective-permute-done.1.refs_1_) | copy-start | bytes 1179652
  15.2 18.1 %collective-permute-start.3 = (bf16[384,512]{1,0:T(8,128)(2,1)S(1)}, bf16[384,512]{1,0:T(8,128)(2,1)S(1)}, u32[]{:S(2)}, u32[]{:S(2)}) collective-permute-start(bf16[384,512]{1,0:T(8,128)(2,1)S(1)} %collective-permute-done.refs_2_), channel_id=1, source_target_pairs={{0,2},{2,0},{1,3},{3,1},{4,6},{6,4},{5,7},{7,5},{8,10},{10,8},{9,1... | collective-permute-start | bytes 1179656 | tf_op jit(solution)/shard_map/ppermute | solution.py:198
  32.0 14.6 %collective-permute-start.6 = (bf16[384,512]{1,0:T(8,128)(2,1)}, bf16[384,512]{1,0:T(8,128)(2,1)}, u32[]{:S(2)}, u32[]{:S(2)}) collective-permute-start(bf16[384,512]{1,0:T(8,128)(2,1)} %collective-permute-done.5.refs_3_), channel_id=1, source_target_pairs={{8,4},{4,0},{9,5},{5,1},{10,6},{6,2},{11,7},{7,3},{24,20},{20,16},... | collective-permute-start | bytes 1179656 | tf_op jit(solution)/shard_map/ppermute | solution.py:228
  33.3 3.5 %copy-start.7 = (bf16[384,512]{1,0:T(8,128)(2,1)}, bf16[384,512]{1,0:T(8,128)(2,1)S(1)}, u32[]{:S(2)}) copy-start(bf16[384,512]{1,0:T(8,128)(2,1)S(1)} %collective-permute-done.3.refs_0_) | copy-start | bytes 1179652
  33.3 13.3 %collective-permute-start.4 = (bf16[384,512]{1,0:T(8,128)(2,1)S(1)}, bf16[384,512]{1,0:T(8,128)(2,1)}, u32[]{:S(2)}, u32[]{:S(2)}) collective-permute-start(bf16[384,512]{1,0:T(8,128)(2,1)S(1)} %collective-permute-done.refs_2_), channel_id=1, source_target_pairs={{4,8},{8,12},{5,9},{9,13},{6,10},{10,14},{7,11},{11,15},{20,24},{2... | collective-permute-start | bytes 1179656 | tf_op jit(solution)/shard_map/ppermute | solution.py:226
  35.3 13.9 %collective-permute-start.9 = (bf16[384,512]{1,0:T(8,128)(2,1)}, bf16[384,512]{1,0:T(8,128)(2,1)}, u32[]{:S(2)}, u32[]{:S(2)}) collective-permute-start(bf16[384,512]{1,0:T(8,128)(2,1)} %collective-permute-done.5.refs_3_), channel_id=1, source_target_pairs={{0,2},{2,0},{1,3},{3,1},{4,6},{6,4},{5,7},{7,5},{8,10},{10,8},{9,1... | collective-permute-start | bytes 1179656 | tf_op jit(solution)/shard_map/ppermute | solution.py:198
  36.8 10.8 %copy-start.1 = (bf16[32,16,512]{2,0,1:T(8,128)(2,1)}, bf16[32,16,512]{2,0,1:T(8,128)(2,1)S(1)}, u32[]{:S(2)}) copy-start(bf16[32,16,512]{2,0,1:T(8,128)(2,1)S(1)} %all-to-all-done) | copy-start | bytes 1572868
  36.8 14.0 %copy-start.9 = (s32[384,1]{0,1:T(1,128)S(1)}, s32[384,1]{0,1:T(1,128)}, u32[]{:S(2)}) copy-start(s32[384,1]{0,1:T(1,128)} %param.13) | copy-start | bytes 4612
  36.9 14.0 %copy-start.10 = (s32[16]{0:T(128)S(1)}, s32[16]{0:T(128)}, u32[]{:S(2)}) copy-start(s32[16]{0:T(128)} %param.14) | copy-start | bytes 196
  47.7 13.8 %copy-start.2 = (bf16[384,512]{1,0:T(8,128)(2,1)}, bf16[384,512]{1,0:T(8,128)(2,1)S(1)}, u32[]{:S(2)}) copy-start(bf16[384,512]{1,0:T(8,128)(2,1)S(1)} %broadcast_select_fusion.refs_2_) | copy-start | bytes 1179652
  47.7 13.0 %collective-permute-start.8 = (bf16[512,512]{1,0:T(8,128)(2,1)S(1)}, bf16[512,512]{1,0:T(8,128)(2,1)S(1)}, u32[]{:S(2)}, u32[]{:S(2)}) collective-permute-start(bf16[512,512]{1,0:T(8,128)(2,1)S(1)} %bitcast.51), channel_id=1, source_target_pairs={{0,16},{16,0},{1,17},{17,1},{2,18},{18,2},{3,19},{19,3},{4,20},{20... | collective-permute-start | bytes 1572872 | tf_op jit(solution)/shard_map/ppermute | solution.py:300
  49.2 12.2 %collective-permute-start.10 = (bf16[384,512]{1,0:T(8,128)(2,1)S(1)}, bf16[384,512]{1,0:T(8,128)(2,1)}, u32[]{:S(2)}, u32[]{:S(2)}) collective-permute-start(bf16[384,512]{1,0:T(8,128)(2,1)S(1)} %broadcast_select_fusion.refs_2_), channel_id=1, source_target_pairs={{0,2},{2,0},{1,3},{3,1},{4,6},{6,4},{5,7},{7,5},{8,10},{10,8},{9,1... | collective-permute-start | bytes 1179656 | tf_op jit(solution)/shard_map/ppermute | solution.py:198
  51.8 44.8 %copy-start.8 = (bf16[24,1024]{1,0:T(8,128)(2,1)S(1)}, bf16[24,1024]{1,0:T(8,128)(2,1)}, u32[]{:S(2)}) copy-start(bf16[24,1024]{1,0:T(8,128)(2,1)} %param.21) | copy-start | bytes 147460
  51.8 45.7 %copy-start.11 = (s32[24]{0:T(128)S(1)}, s32[24]{0:T(128)}, u32[]{:S(2)}) copy-start(s32[24]{0:T(128)} %param.15) | copy-start | bytes 292
  60.7 0.8 copy-start.4
  68.7 7.5 %collective-permute-start.13 = (f32[384,512]{1,0:T(8,128)}, f32[384,512]{1,0:T(8,128)}, u32[]{:S(2)}, u32[]{:S(2)}) collective-permute-start(f32[384,512]{1,0:T(8,128)} %get-tuple-element.58), channel_id=1, source_target_pairs={{0,1},{1,0},{2,3},{3,2},{4,5},{5,4},{6,7},{7,6},{8,9},{9,8},{10,11... | collective-permute-start | bytes 2359304 | tf_op jit(solution)/shard_map/ppermute | solution.py:198
  68.7 2.4 %collective-permute-start.11 = (f32[192,128]{1,0:T(8,128)}, f32[192,128]{1,0:T(8,128)S(1)}, u32[]{:S(2)}, u32[]{:S(2)}) collective-permute-start(f32[192,128]{1,0:T(8,128)} %get-tuple-element.57), channel_id=1, source_target_pairs={{0,1},{1,0},{2,3},{3,2},{4,5},{5,4},{6,7},{7,6},{8,9},{9,8},{10,11... | collective-permute-start | bytes 294920 | tf_op jit(solution)/shard_map/ppermute | solution.py:198
  72.0 4.2 %collective-permute-start.12 = (bf16[192,128]{1,0:T(8,128)(2,1)S(1)}, bf16[192,128]{1,0:T(8,128)(2,1)S(1)}, u32[]{:S(2)}, u32[]{:S(2)}) collective-permute-start(bf16[192,128]{1,0:T(8,128)(2,1)S(1)} %add_convert_fusion.4), channel_id=1, source_target_pairs={{0,2},{2,0},{1,3},{3,1},{4,6},{6,4},{5,7},{7,5},{8,10},{10,8},{9,1... | collective-permute-start | bytes 147464 | tf_op jit(solution)/shard_map/ppermute | solution.py:198
  76.2 7.7 %collective-permute-start.14 = (bf16[192,128]{1,0:T(8,128)(2,1)S(1)}, bf16[192,128]{1,0:T(8,128)(2,1)S(1)}, u32[]{:S(2)}, u32[]{:S(2)}) collective-permute-start(bf16[192,128]{1,0:T(8,128)(2,1)S(1)} %add.217), channel_id=1, source_target_pairs={{0,4},{4,8},{8,12},{12,0},{1,5},{5,9},{9,13},{13,1},{2,6},{6,10},{... | collective-permute-start | bytes 147464 | tf_op jit(solution)/shard_map/ppermute | solution.py:198
  81.1 5.4 %collective-permute-start.15 = (bf16[192,128]{1,0:T(8,128)(2,1)S(1)}, bf16[192,128]{1,0:T(8,128)(2,1)S(1)}, u32[]{:S(2)}, u32[]{:S(2)}) collective-permute-start(bf16[192,128]{1,0:T(8,128)(2,1)S(1)} %add.217), channel_id=1, source_target_pairs={{0,8},{4,12},{8,0},{12,4},{1,9},{5,13},{9,1},{13,5},{2,10},{6,14},... | collective-permute-start | bytes 147464 | tf_op jit(solution)/shard_map/ppermute | solution.py:198
  81.6 4.9 %collective-permute-start.16 = (bf16[192,128]{1,0:T(8,128)(2,1)S(1)}, bf16[192,128]{1,0:T(8,128)(2,1)S(1)}, u32[]{:S(2)}, u32[]{:S(2)}) collective-permute-start(bf16[192,128]{1,0:T(8,128)(2,1)S(1)} %add.217), channel_id=1, source_target_pairs={{0,12},{4,0},{8,4},{12,8},{1,13},{5,1},{9,5},{13,9},{2,14},{6,2},{... | collective-permute-start | bytes 147464 | tf_op jit(solution)/shard_map/ppermute | solution.py:198
  90.7 47.3 %collective-permute-start.18 = (bf16[512,8192]{1,0:T(8,128)(2,1)}, bf16[512,8192]{1,0:T(8,128)(2,1)}, u32[]{:S(2)}, u32[]{:S(2)}) collective-permute-start(bf16[512,8192]{1,0:T(8,128)(2,1)} %refs_2_.3), channel_id=1, source_target_pairs={{0,1},{1,0},{2,3},{3,2},{4,5},{5,4},{6,7},{7,6},{8,9},{9,8},{10,11... | collective-permute-start | bytes 25165832 | tf_op jit(solution)/shard_map/ppermute | solution.py:198
  90.7 18.1 %all-to-all-start.1 = ((bf16[16,24,512]{2,1,0:T(8,128)(2,1)}), bf16[16,24,512]{2,1,0:T(8,128)(2,1)S(1)}, u32[]{:S(2)}, u32[]{:S(2)}) async-start(bf16[16,24,512]{2,1,0:T(8,128)(2,1)} %bitcast.55), calls=%async_computation.1 | async-start | bytes 786432 | tf_op jit(solution)/shard_map/all_to_all | solution.py:315
  136.3 1.7 copy-start
  136.3 1.7 collective-permute-start.17
  138.0 0.8 copy-start.3
  142.3 11.8 %collective-permute-start.21 = (bf16[384,512]{1,0:T(8,128)(2,1)}, bf16[384,512]{1,0:T(8,128)(2,1)S(1)}, u32[]{:S(2)}, u32[]{:S(2)}) collective-permute-start(bf16[384,512]{1,0:T(8,128)(2,1)} %shard_map.122), channel_id=1, source_target_pairs={{0,2},{2,0},{1,3},{3,1},{4,6},{6,4},{5,7},{7,5},{8,10},{10,8},{9,1... | collective-permute-start | bytes 1179656 | tf_op jit(solution)/shard_map/ppermute | solution.py:198
  150.2 12.3 %collective-permute-start.20 = (bf16[384,512]{1,0:T(8,128)(2,1)}, bf16[384,512]{1,0:T(8,128)(2,1)S(1)}, u32[]{:S(2)}, u32[]{:S(2)}) collective-permute-start(bf16[384,512]{1,0:T(8,128)(2,1)} %get-tuple-element.67), channel_id=1, source_target_pairs={{0,2},{2,0},{1,3},{3,1},{4,6},{6,4},{5,7},{7,5},{8,10},{10,8},{9,1... | collective-permute-start | bytes 1179656 | tf_op jit(solution)/shard_map/ppermute | solution.py:198
  155.1 10.7 %collective-permute-start.22 = (bf16[384,512]{1,0:T(8,128)(2,1)S(1)}, bf16[384,512]{1,0:T(8,128)(2,1)S(1)}, u32[]{:S(2)}, u32[]{:S(2)}) collective-permute-start(bf16[384,512]{1,0:T(8,128)(2,1)S(1)} %add_convert_fusion.3), channel_id=1, source_target_pairs={{0,4},{4,8},{1,5},{5,9},{2,6},{6,10},{3,7},{7,11},{16,20},{20,24},... | collective-permute-start | bytes 1179656 | tf_op jit(solution)/shard_map/ppermute | solution.py:244
  158.2 12.7 %collective-permute-start.24 = (bf16[384,512]{1,0:T(8,128)(2,1)}, bf16[384,512]{1,0:T(8,128)(2,1)S(1)}, u32[]{:S(2)}, u32[]{:S(2)}) collective-permute-start(bf16[384,512]{1,0:T(8,128)(2,1)} %get-tuple-element.72), channel_id=1, source_target_pairs={{0,2},{2,0},{1,3},{3,1},{4,6},{6,4},{5,7},{7,5},{8,10},{10,8},{9,1... | collective-permute-start | bytes 1179656 | tf_op jit(solution)/shard_map/ppermute | solution.py:198
  158.7 12.2 %collective-permute-start.25 = (bf16[384,512]{1,0:T(8,128)(2,1)S(1)}, bf16[384,512]{1,0:T(8,128)(2,1)S(1)}, u32[]{:S(2)}, u32[]{:S(2)}) collective-permute-start(bf16[384,512]{1,0:T(8,128)(2,1)S(1)} %add_convert_fusion.3), channel_id=1, source_target_pairs={{12,8},{8,4},{13,9},{9,5},{14,10},{10,6},{15,11},{11,7},{28,24},{2... | collective-permute-start | bytes 1179656 | tf_op jit(solution)/shard_map/ppermute | solution.py:245
  159.4 19.5 %collective-permute-start.19 = (bf16[384,512]{1,0:T(8,128)(2,1)}, bf16[384,512]{1,0:T(8,128)(2,1)S(1)}, u32[]{:S(2)}, u32[]{:S(2)}) collective-permute-start(bf16[384,512]{1,0:T(8,128)(2,1)} %get-tuple-element.64), channel_id=1, source_target_pairs={{0,2},{2,0},{1,3},{3,1},{4,6},{6,4},{5,7},{7,5},{8,10},{10,8},{9,1... | collective-permute-start | bytes 1179656 | tf_op jit(solution)/shard_map/ppermute | solution.py:198
  167.0 13.9 %collective-permute-start.23 = (bf16[384,512]{1,0:T(8,128)(2,1)S(1)}, bf16[384,512]{1,0:T(8,128)(2,1)S(1)}, u32[]{:S(2)}, u32[]{:S(2)}) collective-permute-start(bf16[384,512]{1,0:T(8,128)(2,1)S(1)} %add_convert_fusion.2), channel_id=1, source_target_pairs={{0,4},{4,8},{8,12},{12,0},{1,5},{5,9},{9,13},{13,1},{2,6},{6,10},{... | collective-permute-start | bytes 1179656 | tf_op jit(solution)/shard_map/ppermute | solution.py:198
  172.0 14.7 %collective-permute-start.26 = (bf16[384,512]{1,0:T(8,128)(2,1)S(1)}, bf16[384,512]{1,0:T(8,128)(2,1)S(1)}, u32[]{:S(2)}, u32[]{:S(2)}) collective-permute-start(bf16[384,512]{1,0:T(8,128)(2,1)S(1)} %add_convert_fusion.1), channel_id=1, source_target_pairs={{0,12},{4,0},{8,4},{12,8},{1,13},{5,1},{9,5},{13,9},{2,14},{6,2},{... | collective-permute-start | bytes 1179656 | tf_op jit(solution)/shard_map/ppermute | solution.py:198

commit v5 on v1

--- a/solution.py
+++ b/solution.py
@@ -242,9 +242,11 @@
     two = narrow(parts[2])
     up = lax.ppermute(two, "z", [(0, 1), (1, 2)])
     down = lax.ppermute(two, "z", [(3, 2), (2, 1)])
-    above = shift(narrow(parts[1] + wide(up)), "z", 1)
+    early = lax.optimization_barrier(parts[1])
+    above = shift(narrow(early + wide(up)), "z", 1)
     below = shift(narrow(parts[3] + wide(down)), "z", 3)
-    return parts[0] + wide(above) + wide(below)
+    early = lax.optimization_barrier(parts[0] + wide(above))
+    return early + wide(below)
 
 
 def shards(

time: 188 us -> 188 us (level)
    add x0 -> x2, other arithmetic: none -> 2.24 us  [the longest x1 1.13 us: scatter_layers(): early = lax.optimization_barrier(parts[0] + wide(above))]
where the time goes in v5:
time: 188 us; the launch traced here: 187 us
  waiting for transfers between devices  72.5 us (39%)
  starting transfers between devices  45.4 us (24%)
  Pallas kernels  28.3 us (15%)
  blocking collectives  15.5 us (8%)
  matrix products  10.4 us (6%)
  other arithmetic  8.87 us (5%)
  local copies, waits for them, and re-layouts  5.89 us (3%)
    ppermute x22, waiting for transfers between devices, shift(): lax.ppermute(value, axis, [(i, (i + by) % size) for i in range(size)])  46.4 us
    ppermute x22, starting transfers between devices, shift(): lax.ppermute(value, axis, [(i, (i + by) % size) for i in range(size)])  27.9 us
    all_to_all x1, blocking collectives, shards(): lax.all_to_all(context, ADP, split_axis=0, concat_axis=0, tiled=True)  15.5 us
    pallas_call x2, Pallas kernels, project(): pl.pallas_call(kernel, grid_spec=pltpu.PrefetchScalarGridSpec(num_scalar_...  13.8 us
    all_to_all x1, waiting for transfers between devices, shards(): lax.all_to_all(query, ADP, split_axis=0, concat_axis=1, tiled=True)  12 us
    pallas_call x2, Pallas kernels, output_partial(): pl.pallas_call(kernel, grid_spec=pltpu.PrefetchScalarGridSpec(num_scalar_...  10.9 us
    ppermute x1, waiting for transfers between devices, shards(): lax.ppermute(up, 'rep', [(i, i ^ 1) for i in range(lax.axis_size('rep'))])  8.54 us
    all_to_all x1, starting transfers between devices, shards(): lax.all_to_all(query, ADP, split_axis=0, concat_axis=1, tiled=True)  5.76 us
  transfers between devices with their start and end apart: 29, of which 16 were waited for; matrix products, arithmetic and copies ran while one was open for 11% of the time, Pallas kernels for 8%

profile of v5, /device:TPU:0, one launch (start us, length us, event | category | flops | bytes accessed | tf_op | source)
XLA Modules:
  0.0 187.3 jit_solution(17862717982018330992)
XLA Ops:
  0.0 0.5 collective-permute-start.6
  0.5 2.6 %collective-permute-start = (bf16[384,512]{1,0:T(8,128)(2,1)}, bf16[384,512]{1,0:T(8,128)(2,1)S(1)}, u32[]{:S(2)}, u32[]{:S(2)}) collective-permute-start(bf16[384,512]{1,0:T(8,128)(2,1)} %refs_0_.1), channel_id=1, source_target_pairs={{0,4},{4,8},{8,12},{12,0},{1,5},{5,9},{9,13},{13,1},{2,6},{6,10},{... | collective-permute-start | bytes 1179656 | tf_op jit(solution)/shard_map/ppermute | solution.py:198
  3.1 1.5 collective-permute-start.1
  4.6 2.2 %collective-permute-start.4 = (bf16[384,512]{1,0:T(8,128)(2,1)}, bf16[384,512]{1,0:T(8,128)(2,1)S(1)}, u32[]{:S(2)}, u32[]{:S(2)}) collective-permute-start(bf16[384,512]{1,0:T(8,128)(2,1)} %refs_0_.1), channel_id=1, source_target_pairs={{0,12},{4,0},{8,4},{12,8},{1,13},{5,1},{9,5},{13,9},{2,14},{6,2},{... | collective-permute-start | bytes 1179656 | tf_op jit(solution)/shard_map/ppermute | solution.py:198
  7.1 1.1 copy.36
  8.2 3.6 %all-to-all-start = ((bf16[32,16,512]{2,0,1:T(8,128)(2,1)}), bf16[32,16,512]{2,0,1:T(8,128)(2,1)S(1)}, u32[]{:S(2)}, u32[]{:S(2)}) async-start(bf16[32,16,512]{2,0,1:T(8,128)(2,1)} %copy.36), calls=%async_computation | async-start | bytes 1048576 | tf_op jit(solution)/shard_map/all_to_all | solution.py:297
  11.7 13.2 %collective-permute-done.4.refs_3_ = bf16[384,512]{1,0:T(8,128)(2,1)S(1)} collective-permute-done((bf16[384,512]{1,0:T(8,128)(2,1)}, bf16[384,512]{1,0:T(8,128)(2,1)S(1)}, u32[]{:S(2)}, u32[]{:S(2)}) %collective-permute-start.4) | collective-permute-done | bytes 393248 | tf_op jit(solution)/shard_map/ppermute | solution.py:198
  25.0 1.3 collective-permute-start.5
  26.3 1.5 collective-permute-start.3
  27.8 0.6 stack.43.places
  28.4 0.7 collective-permute-start.8
  29.1 1.3 collective-permute-start.7
  30.4 6.6 %shard_map.118 = (f32[384,512]{1,0:T(8,128)}, f32[384,512]{1,0:T(8,128)}, f32[384,128]{1,0:T(8,128)}) custom-call(s32[16]{0:T(128)} %stack.43.places, bf16[384,512]{1,0:T(8,128)(2,1)} %refs_0_.1, bf16[384,512]{1,0:T(8,128)(2,1)} %copy-done.11, bf16[384,512]{1,0:T(8,128)(2,1)} %copy-done.9, bf16[384,512]{1,0:T(8,128)(2,1)} %copy-done.10, ...), custom_call_target="tpu_custom_call" | custom-call | flops 1811939328 | bytes 7340032 | tf_op jit(solution)/shard_map/pallas_call | solution.py:64
  37.0 3.3 %collective-permute-done.5 = bf16[384,512]{1,0:T(8,128)(2,1)S(1)} collective-permute-done((bf16[384,512]{1,0:T(8,128)(2,1)S(1)}, bf16[384,512]{1,0:T(8,128)(2,1)S(1)}, u32[]{:S(2)}, u32[]{:S(2)}) %collective-permute-start.5) | collective-permute-done | bytes 393248 | tf_op jit(solution)/shard_map/ppermute | solution.py:228
  40.3 0.7 copy-done.13
  41.1 1.0 broadcast_select_fusion.refs_2_
  42.2 6.0 %collective-permute-done.7.refs_0_ = bf16[384,512]{1,0:T(8,128)(2,1)} collective-permute-done((bf16[384,512]{1,0:T(8,128)(2,1)S(1)}, bf16[384,512]{1,0:T(8,128)(2,1)}, u32[]{:S(2)}, u32[]{:S(2)}) %collective-permute-start.7) | collective-permute-done | bytes 393248 | tf_op jit(solution)/shard_map/ppermute | solution.py:198
  48.2 1.6 collective-permute-start.9
  49.8 0.8 collective-permute-start.10
  50.7 0.8 broadcast_in_dim.46.refs_23_.slot
  51.5 8.5 %collective-permute-done.9.up_other = bf16[512,512]{1,0:T(8,128)(2,1)S(1)} collective-permute-done((bf16[512,512]{1,0:T(8,128)(2,1)S(1)}, bf16[512,512]{1,0:T(8,128)(2,1)S(1)}, u32[]{:S(2)}, u32[]{:S(2)}) %collective-permute-start.9) | collective-permute-done | bytes 524320 | tf_op jit(solution)/shard_map/ppermute | solution.py:301
  60.0 0.8 copy-done.12
  60.8 7.2 %shard_map.119 = (f32[384,512]{1,0:T(8,128)}, f32[384,512]{1,0:T(8,128)}, f32[192,128]{1,0:T(8,128)}) custom-call(s32[16]{0:T(128)} %stack.43.places, bf16[384,512]{1,0:T(8,128)(2,1)} %collective-permute-done.7.refs_0_, bf16[384,512]{1,0:T(8,128)(2,1)} %collective-permute-done.8.refs_1_, bf16[384,512]{1,0:T(8,128)(2,1)} %copy-done.5, ...), custom_call_target="tpu_custom_call" | custom-call | flops 1811939328 | bytes 7340032 | tf_op jit(solution)/shard_map/pallas_call | solution.py:64
  68.1 0.5 collective-permute-start.11
  68.6 2.1 %collective-permute-done.11 = f32[192,128]{1,0:T(8,128)S(1)} collective-permute-done((f32[192,128]{1,0:T(8,128)}, f32[192,128]{1,0:T(8,128)S(1)}, u32[]{:S(2)}, u32[]{:S(2)}) %collective-permute-start.11) | collective-permute-done | bytes 98336 | tf_op jit(solution)/shard_map/ppermute | solution.py:198
  70.8 0.9 add_convert_fusion.4
  71.7 1.8 collective-permute-start.12
  73.5 2.4 %collective-permute-done.12 = bf16[192,128]{1,0:T(8,128)(2,1)S(1)} collective-permute-done((bf16[192,128]{1,0:T(8,128)(2,1)S(1)}, bf16[192,128]{1,0:T(8,128)(2,1)S(1)}, u32[]{:S(2)}, u32[]{:S(2)}) %collective-permute-start.12) | collective-permute-done | bytes 49184 | tf_op jit(solution)/shard_map/ppermute | solution.py:198
  75.9 3.6 %collective-permute-start.14 = (bf16[192,128]{1,0:T(8,128)(2,1)S(1)}, bf16[192,128]{1,0:T(8,128)(2,1)S(1)}, u32[]{:S(2)}, u32[]{:S(2)}) collective-permute-start(bf16[192,128]{1,0:T(8,128)(2,1)S(1)} %add.217), channel_id=1, source_target_pairs={{0,4},{4,8},{8,12},{12,0},{1,5},{5,9},{9,13},{13,1},{2,6},{6,10},{... | collective-permute-start | bytes 147464 | tf_op jit(solution)/shard_map/ppermute | solution.py:198
  79.5 0.4 collective-permute-start.15
  79.9 2.8 %collective-permute-start.16 = (bf16[192,128]{1,0:T(8,128)(2,1)S(1)}, bf16[192,128]{1,0:T(8,128)(2,1)S(1)}, u32[]{:S(2)}, u32[]{:S(2)}) collective-permute-start(bf16[192,128]{1,0:T(8,128)(2,1)S(1)} %add.217), channel_id=1, source_target_pairs={{0,12},{4,0},{8,4},{12,8},{1,13},{5,1},{9,5},{13,9},{2,14},{6,2},{... | collective-permute-start | bytes 147464 | tf_op jit(solution)/shard_map/ppermute | solution.py:198
  82.8 2.2 %collective-permute-done.15 = bf16[192,128]{1,0:T(8,128)(2,1)S(1)} collective-permute-done((bf16[192,128]{1,0:T(8,128)(2,1)S(1)}, bf16[192,128]{1,0:T(8,128)(2,1)S(1)}, u32[]{:S(2)}, u32[]{:S(2)}) %collective-permute-start.15) | collective-permute-done | bytes 49184 | tf_op jit(solution)/shard_map/ppermute | solution.py:198
  85.0 0.6 add_add_fusion.low
  85.7 3.6 %shard_map.120 = bf16[384,512]{1,0:T(8,128)(2,1)} custom-call(s32[1]{0:T(128)} %bitcast.8.half, f32[384,512]{1,0:T(8,128)} %get-tuple-element.50.own, f32[384,512]{1,0:T(8,128)} %copy-done.7, bf16[192,128]{1,0:T(8,128)(2,1)} %add_add_fusion.low, s32[384,1]{1,0:T(8,128)} %broadcast_in_dim.46.refs_23_.slot, bf16[512,512]{1,0:T(8,128)(2,1)} %bitcast.52, ...), custom_call_target="tpu_custom_call" | custom-call | flops 1 | bytes 1 | tf_op jit(solution)/shard_map/pallas_call | solution.py:119
  89.3 5.8 %all-to-all-start.1 = ((bf16[16,24,512]{2,1,0:T(8,128)(2,1)}), bf16[16,24,512]{2,1,0:T(8,128)(2,1)S(1)}, u32[]{:S(2)}, u32[]{:S(2)}) async-start(bf16[16,24,512]{2,1,0:T(8,128)(2,1)} %bitcast.55), calls=%async_computation.1 | async-start | bytes 786432 | tf_op jit(solution)/shard_map/all_to_all | solution.py:316
  95.2 12.0 %all-to-all-done.1 = bf16[16,24,512]{2,1,0:T(8,128)(2,1)S(1)} async-done(((bf16[16,24,512]{2,1,0:T(8,128)(2,1)}), bf16[16,24,512]{2,1,0:T(8,128)(2,1)S(1)}, u32[]{:S(2)}, u32[]{:S(2)}) %all-to-all-start.1) | async-done | bytes 393248 | tf_op jit(solution)/shard_map/all_to_all | solution.py:316
  107.9 5.5 %fusion.15 = (f32[8,24,8]{2,1,0:T(8,128)S(1)}, f32[8,24,8,128]{3,2,1,0:T(8,128)S(1)}) fusion(bf16[8,24,128,128]{3,2,1,0:T(8,128)(2,1)} %param.19, bf16[24,8,8,128]{3,2,1,0:T(8,128)(2,1)S(1)} %reshape.48, pred[24,128]{1,0:T(8,128)(4,1)S(1)} %iota_compare_fusion.1), kind=kOutput, calls=%fused_computation.32 | convolution fusion | flops 50723328 | bytes 7480320 | tf_op jit(solution)/shard_map/rkge,krje->krgj/dot_general | solution.py:182
  113.5 0.5 fusion.8
  114.1 4.6 %fusion.5 = bf16[24,8,8,128]{3,2,1,0:T(8,128)(2,1)S(1)} fusion(bf16[8,24,128,128]{3,2,1,0:T(8,128)(2,1)} %param.20, f32[24,8,128]{2,1,0:T(8,128)S(1)} %bitcast.58, f32[24,8,8]{2,1,0:T(8,128)S(1)} %copy.43, f32[8,24,8,128]{3,2,1,0:T(8,128)S(1)} %get-tuple-element.70, f32[8,24,8]{2,1,0:T(8,128)S(1)} %get-tuple-element.68, f32[8,24,8]{2,1,0:T(8,128)S(1)} %max.3, ...), kind=kOutput, calls=%fused_computation.4 | convolution fusion | flops 51707904 | bytes 7590912 | tf_op jit(solution)/shard_map/krgj,krje->rkge/dot_general | solution.py:191
  119.2 15.5 %all_to_all.40 = bf16[16,24,512]{2,1,0:T(8,128)(2,1)S(1)} all-to-all(bf16[16,24,512]{2,1,0:T(8,128)(2,1)S(1)} %bitcast.54), channel_id=1, replica_groups=mesh['rep'=2,'z'=4,'y'=2,'core'=2] {'z','y','core'}, dimensions={0} | all-to-all | bytes 786432 | tf_op jit(solution)/shard_map/all_to_all | solution.py:322
  134.8 1.6 collective-permute-done.17.refs_1_
  136.4 0.8 copy-done.6
  137.2 3.5 %shard_map.122 = bf16[384,512]{1,0:T(8,128)(2,1)} custom-call(s32[16]{0:T(128)} %stack.43.places, bf16[384,512]{1,0:T(8,128)(2,1)} %bitcast.47, bf16[384,512]{1,0:T(8,128)(2,1)} %copy-done.6, bf16[512,8192]{1,0:T(8,128)(2,1)} %refs_2_.3, bf16[512,8192]{1,0:T(8,128)(2,1)} %collective-permute-done.18.refs_9_.refs_10_.refs_11_.refs_12_.refs_13_.refs_14_.refs_15_.refs_3_), custom_call_target="tpu_custom_call" | custom-call | flops 1 | bytes 1 | tf_op jit(solution)/shard_map/pallas_call | solution.py:160
  140.7 0.6 collective-permute-start.21
  141.3 7.5 %shard_map.121 = (bf16[384,512]{1,0:T(8,128)(2,1)}, bf16[384,512]{1,0:T(8,128)(2,1)}, bf16[384,512]{1,0:T(8,128)(2,1)}, bf16[384,512]{1,0:T(8,128)(2,1)}, bf16[3...) custom-call(s32[16]{0:T(128)} %stack.43.places, bf16[384,512]{1,0:T(8,128)(2,1)} %bitcast.48, ...), custom_call_target="tpu_custom_call" | custom-call | flops 1 | bytes 1 | tf_op jit(solution)/shard_map/pallas_call | solution.py:160
  148.7 1.5 collective-permute-start.20
  150.2 2.1 %collective-permute-done.21 = bf16[384,512]{1,0:T(8,128)(2,1)S(1)} collective-permute-done((bf16[384,512]{1,0:T(8,128)(2,1)}, bf16[384,512]{1,0:T(8,128)(2,1)S(1)}, u32[]{:S(2)}, u32[]{:S(2)}) %collective-permute-start.21) | collective-permute-done | bytes 393248 | tf_op jit(solution)/shard_map/ppermute | solution.py:198
  152.3 1.1 add_convert_fusion.3
  153.4 3.1 %collective-permute-start.22 = (bf16[384,512]{1,0:T(8,128)(2,1)S(1)}, bf16[384,512]{1,0:T(8,128)(2,1)S(1)}, u32[]{:S(2)}, u32[]{:S(2)}) collective-permute-start(bf16[384,512]{1,0:T(8,128)(2,1)S(1)} %add_convert_fusion.3), channel_id=1, source_target_pairs={{0,4},{4,8},{1,5},{5,9},{2,6},{6,10},{3,7},{7,11},{16,20},{20,24},... | collective-permute-start | bytes 1179656 | tf_op jit(solution)/shard_map/ppermute | solution.py:243
  156.5 0.6 collective-permute-start.24
  157.1 1.5 collective-permute-start.19
  158.6 0.7 collective-permute-start.25
  159.3 1.7 collective-permute-done.20
  161.0 1.1 convert_add_fusion.1
  162.1 2.2 %collective-permute-done.22 = bf16[384,512]{1,0:T(8,128)(2,1)S(1)} collective-permute-done((bf16[384,512]{1,0:T(8,128)(2,1)S(1)}, bf16[384,512]{1,0:T(8,128)(2,1)S(1)}, u32[]{:S(2)}, u32[]{:S(2)}) %collective-permute-start.22) | collective-permute-done | bytes 393248 | tf_op jit(solution)/shard_map/ppermute | solution.py:243
  164.4 2.5 %collective-permute-start.23 = (bf16[384,512]{1,0:T(8,128)(2,1)S(1)}, bf16[384,512]{1,0:T(8,128)(2,1)S(1)}, u32[]{:S(2)}, u32[]{:S(2)}) collective-permute-start(bf16[384,512]{1,0:T(8,128)(2,1)S(1)} %add_convert_fusion.2), channel_id=1, source_target_pairs={{0,4},{4,8},{8,12},{12,0},{1,5},{5,9},{9,13},{13,1},{2,6},{6,10},{... | collective-permute-start | bytes 1179656 | tf_op jit(solution)/shard_map/ppermute | solution.py:198
  166.9 2.5 %collective-permute-done.24 = bf16[384,512]{1,0:T(8,128)(2,1)S(1)} collective-permute-done((bf16[384,512]{1,0:T(8,128)(2,1)}, bf16[384,512]{1,0:T(8,128)(2,1)S(1)}, u32[]{:S(2)}, u32[]{:S(2)}) %collective-permute-start.24) | collective-permute-done | bytes 393248 | tf_op jit(solution)/shard_map/ppermute | solution.py:198
  169.4 1.1 add_convert_fusion.1
  170.6 2.2 %collective-permute-start.26 = (bf16[384,512]{1,0:T(8,128)(2,1)S(1)}, bf16[384,512]{1,0:T(8,128)(2,1)S(1)}, u32[]{:S(2)}, u32[]{:S(2)}) collective-permute-start(bf16[384,512]{1,0:T(8,128)(2,1)S(1)} %add_convert_fusion.1), channel_id=1, source_target_pairs={{0,12},{4,0},{8,4},{12,8},{1,13},{5,1},{9,5},{13,9},{2,14},{6,2},{... | collective-permute-start | bytes 1179656 | tf_op jit(solution)/shard_map/ppermute | solution.py:198
  172.7 4.6 %collective-permute-done.19 = bf16[384,512]{1,0:T(8,128)(2,1)S(1)} collective-permute-done((bf16[384,512]{1,0:T(8,128)(2,1)}, bf16[384,512]{1,0:T(8,128)(2,1)S(1)}, u32[]{:S(2)}, u32[]{:S(2)}) %collective-permute-start.19) | collective-permute-done | bytes 393248 | tf_op jit(solution)/shard_map/ppermute | solution.py:198
  177.3 2.6 %collective-permute-done.23 = bf16[384,512]{1,0:T(8,128)(2,1)S(1)} collective-permute-done((bf16[384,512]{1,0:T(8,128)(2,1)S(1)}, bf16[384,512]{1,0:T(8,128)(2,1)S(1)}, u32[]{:S(2)}, u32[]{:S(2)}) %collective-permute-start.23) | collective-permute-done | bytes 393248 | tf_op jit(solution)/shard_map/ppermute | solution.py:198
  179.9 1.1 convert_add_fusion
  181.1 5.3 %collective-permute-done.26 = bf16[384,512]{1,0:T(8,128)(2,1)S(1)} collective-permute-done((bf16[384,512]{1,0:T(8,128)(2,1)S(1)}, bf16[384,512]{1,0:T(8,128)(2,1)S(1)}, u32[]{:S(2)}, u32[]{:S(2)}) %collective-permute-start.26) | collective-permute-done | bytes 393248 | tf_op jit(solution)/shard_map/ppermute | solution.py:198
  186.4 0.9 add_convert_fusion
  (70 shorter events, 2.1 us)
Async XLA Ops:
  0.0 6.9 %copy-start = (bf16[1,8192,64]{1,2,0:T(8,128)(2,1)S(1)}, bf16[1,8192,64]{1,2,0:T(8,128)(2,1)}, u32[]{:S(2)}) copy-start(bf16[1,8192,64]{1,2,0:T(8,128)(2,1)} %param.18) | copy-start | bytes 3145732
  0.0 30.4 %collective-permute-start.6 = (bf16[8192,512]{1,0:T(8,128)(2,1)}, bf16[8192,512]{1,0:T(8,128)(2,1)}, u32[]{:S(2)}, u32[]{:S(2)}) collective-permute-start(bf16[8192,512]{1,0:T(8,128)(2,1)} %refs_7_.4), channel_id=1, source_target_pairs={{0,1},{1,0},{2,3},{3,2},{4,5},{5,4},{6,7},{7,6},{8,9},{9,8},{10,11... | collective-permute-start | bytes 25165832 | tf_op jit(solution)/shard_map/ppermute | solution.py:198
  0.5 25.8 %collective-permute-start = (bf16[384,512]{1,0:T(8,128)(2,1)}, bf16[384,512]{1,0:T(8,128)(2,1)S(1)}, u32[]{:S(2)}, u32[]{:S(2)}) collective-permute-start(bf16[384,512]{1,0:T(8,128)(2,1)} %refs_0_.1), channel_id=1, source_target_pairs={{0,4},{4,8},{8,12},{12,0},{1,5},{5,9},{9,13},{13,1},{2,6},{6,10},{... | collective-permute-start | bytes 1179656 | tf_op jit(solution)/shard_map/ppermute | solution.py:198
  3.1 23.2 %collective-permute-start.1 = (bf16[384,512]{1,0:T(8,128)(2,1)}, bf16[384,512]{1,0:T(8,128)(2,1)S(1)}, u32[]{:S(2)}, u32[]{:S(2)}) collective-permute-start(bf16[384,512]{1,0:T(8,128)(2,1)} %refs_0_.1), channel_id=1, source_target_pairs={{0,2},{2,0},{1,3},{3,1},{4,6},{6,4},{5,7},{7,5},{8,10},{10,8},{9,1... | collective-permute-start | bytes 1179656 | tf_op jit(solution)/shard_map/ppermute | solution.py:198
  4.6 20.4 %collective-permute-start.4 = (bf16[384,512]{1,0:T(8,128)(2,1)}, bf16[384,512]{1,0:T(8,128)(2,1)S(1)}, u32[]{:S(2)}, u32[]{:S(2)}) collective-permute-start(bf16[384,512]{1,0:T(8,128)(2,1)} %refs_0_.1), channel_id=1, source_target_pairs={{0,12},{4,0},{8,4},{12,8},{1,13},{5,1},{9,5},{13,9},{2,14},{6,2},{... | collective-permute-start | bytes 1179656 | tf_op jit(solution)/shard_map/ppermute | solution.py:198
  6.9 19.4 %collective-permute-start.2 = (bf16[1,64,8192]{2,1,0:T(8,128)(2,1)}, bf16[1,64,8192]{2,1,0:T(8,128)(2,1)S(1)}, u32[]{:S(2)}, u32[]{:S(2)}) collective-permute-start(bf16[1,64,8192]{2,1,0:T(8,128)(2,1)} %bitcast.37), channel_id=1, source_target_pairs={{0,1},{1,0},{2,3},{3,2},{4,5},{5,4},{6,7},{7,6},{8,9},{9,8},{10,11... | collective-permute-start | bytes 3145736 | tf_op jit(solution)/shard_map/ppermute | solution.py:198
  8.2 34.0 %all-to-all-start = ((bf16[32,16,512]{2,0,1:T(8,128)(2,1)}), bf16[32,16,512]{2,0,1:T(8,128)(2,1)S(1)}, u32[]{:S(2)}, u32[]{:S(2)}) async-start(bf16[32,16,512]{2,0,1:T(8,128)(2,1)} %copy.36), calls=%async_computation | async-start | bytes 1048576 | tf_op jit(solution)/shard_map/all_to_all | solution.py:297
  25.0 5.4 %copy-start.10 = (bf16[384,512]{1,0:T(8,128)(2,1)}, bf16[384,512]{1,0:T(8,128)(2,1)S(1)}, u32[]{:S(2)}) copy-start(bf16[384,512]{1,0:T(8,128)(2,1)S(1)} %collective-permute-done.4.refs_3_) | copy-start | bytes 1179652
  25.0 15.4 %collective-permute-start.5 = (bf16[384,512]{1,0:T(8,128)(2,1)S(1)}, bf16[384,512]{1,0:T(8,128)(2,1)S(1)}, u32[]{:S(2)}, u32[]{:S(2)}) collective-permute-start(bf16[384,512]{1,0:T(8,128)(2,1)S(1)} %collective-permute-done.4.refs_3_), channel_id=1, source_target_pairs={{8,4},{4,0},{9,5},{5,1},{10,6},{6,2},{11,7},{7,3},{24,20},{20,16},... | collective-permute-start | bytes 1179656 | tf_op jit(solution)/shard_map/ppermute | solution.py:228
  26.3 4.1 %copy-start.9 = (bf16[384,512]{1,0:T(8,128)(2,1)}, bf16[384,512]{1,0:T(8,128)(2,1)S(1)}, u32[]{:S(2)}) copy-start(bf16[384,512]{1,0:T(8,128)(2,1)S(1)} %collective-permute-done.refs_2_) | copy-start | bytes 1179652
  26.3 4.1 %copy-start.11 = (bf16[384,512]{1,0:T(8,128)(2,1)}, bf16[384,512]{1,0:T(8,128)(2,1)S(1)}, u32[]{:S(2)}) copy-start(bf16[384,512]{1,0:T(8,128)(2,1)S(1)} %collective-permute-done.1.refs_1_) | copy-start | bytes 1179652
  26.3 4.1 %copy-start.2 = (bf16[1,64,8192]{2,1,0:T(8,128)(2,1)}, bf16[1,64,8192]{2,1,0:T(8,128)(2,1)S(1)}, u32[]{:S(2)}) copy-start(bf16[1,64,8192]{2,1,0:T(8,128)(2,1)S(1)} %collective-permute-done.2.refs_16_.refs_17_.refs_18_.refs_19_) | copy-start | bytes 3145732
  26.3 14.0 %collective-permute-start.3 = (bf16[384,512]{1,0:T(8,128)(2,1)S(1)}, bf16[384,512]{1,0:T(8,128)(2,1)}, u32[]{:S(2)}, u32[]{:S(2)}) collective-permute-start(bf16[384,512]{1,0:T(8,128)(2,1)S(1)} %collective-permute-done.refs_2_), channel_id=1, source_target_pairs={{4,8},{8,12},{5,9},{9,13},{6,10},{10,14},{7,11},{11,15},{20,24},{2... | collective-permute-start | bytes 1179656 | tf_op jit(solution)/shard_map/ppermute | solution.py:226
  28.4 22.2 %copy-start.16 = (s32[384,1]{0,1:T(1,128)S(1)}, s32[384,1]{0,1:T(1,128)}, u32[]{:S(2)}) copy-start(s32[384,1]{0,1:T(1,128)} %param.13) | copy-start | bytes 4612
  28.4 22.2 %copy-start.17 = (s32[16]{0:T(128)S(1)}, s32[16]{0:T(128)}, u32[]{:S(2)}) copy-start(s32[16]{0:T(128)} %param.14) | copy-start | bytes 196
  28.4 13.8 %collective-permute-start.8 = (bf16[384,512]{1,0:T(8,128)(2,1)S(1)}, bf16[384,512]{1,0:T(8,128)(2,1)}, u32[]{:S(2)}, u32[]{:S(2)}) collective-permute-start(bf16[384,512]{1,0:T(8,128)(2,1)S(1)} %collective-permute-done.4.refs_3_), channel_id=1, source_target_pairs={{0,2},{2,0},{1,3},{3,1},{4,6},{6,4},{5,7},{7,5},{8,10},{10,8},{9,1... | collective-permute-start | bytes 1179656 | tf_op jit(solution)/shard_map/ppermute | solution.py:198
  29.1 19.1 %collective-permute-start.7 = (bf16[384,512]{1,0:T(8,128)(2,1)S(1)}, bf16[384,512]{1,0:T(8,128)(2,1)}, u32[]{:S(2)}, u32[]{:S(2)}) collective-permute-start(bf16[384,512]{1,0:T(8,128)(2,1)S(1)} %collective-permute-done.refs_2_), channel_id=1, source_target_pairs={{0,2},{2,0},{1,3},{3,1},{4,6},{6,4},{5,7},{7,5},{8,10},{10,8},{9,1... | collective-permute-start | bytes 1179656 | tf_op jit(solution)/shard_map/ppermute | solution.py:198
  40.3 0.7 copy-start.13
  42.1 17.9 %copy-start.5 = (bf16[384,512]{1,0:T(8,128)(2,1)}, bf16[384,512]{1,0:T(8,128)(2,1)S(1)}, u32[]{:S(2)}) copy-start(bf16[384,512]{1,0:T(8,128)(2,1)S(1)} %broadcast_select_fusion.refs_2_) | copy-start | bytes 1179652
  42.2 25.9 %copy-start.4 = (bf16[32,16,512]{2,0,1:T(8,128)(2,1)}, bf16[32,16,512]{2,0,1:T(8,128)(2,1)S(1)}, u32[]{:S(2)}) copy-start(bf16[32,16,512]{2,0,1:T(8,128)(2,1)S(1)} %all-to-all-done) | copy-start | bytes 1572868
  48.2 11.8 %collective-permute-start.9 = (bf16[512,512]{1,0:T(8,128)(2,1)S(1)}, bf16[512,512]{1,0:T(8,128)(2,1)S(1)}, u32[]{:S(2)}, u32[]{:S(2)}) collective-permute-start(bf16[512,512]{1,0:T(8,128)(2,1)S(1)} %bitcast.51), channel_id=1, source_target_pairs={{0,16},{16,0},{1,17},{17,1},{2,18},{18,2},{3,19},{19,3},{4,20},{20... | collective-permute-start | bytes 1572872 | tf_op jit(solution)/shard_map/ppermute | solution.py:301
  49.8 10.3 %collective-permute-start.10 = (bf16[384,512]{1,0:T(8,128)(2,1)S(1)}, bf16[384,512]{1,0:T(8,128)(2,1)S(1)}, u32[]{:S(2)}, u32[]{:S(2)}) collective-permute-start(bf16[384,512]{1,0:T(8,128)(2,1)S(1)} %broadcast_select_fusion.refs_2_), channel_id=1, source_target_pairs={{0,2},{2,0},{1,3},{3,1},{4,6},{6,4},{5,7},{7,5},{8,10},{10,8},{9,1... | collective-permute-start | bytes 1179656 | tf_op jit(solution)/shard_map/ppermute | solution.py:198
  51.5 43.6 %copy-start.14 = (bf16[24,1024]{1,0:T(8,128)(2,1)S(1)}, bf16[24,1024]{1,0:T(8,128)(2,1)}, u32[]{:S(2)}) copy-start(bf16[24,1024]{1,0:T(8,128)(2,1)} %param.21) | copy-start | bytes 147460
  51.5 43.6 %copy-start.15 = (bf16[24,1024]{1,0:T(8,128)(2,1)S(1)}, bf16[24,1024]{1,0:T(8,128)(2,1)}, u32[]{:S(2)}) copy-start(bf16[24,1024]{1,0:T(8,128)(2,1)} %param.22) | copy-start | bytes 147460
  51.5 43.6 %copy-start.18 = (s32[24]{0:T(128)S(1)}, s32[24]{0:T(128)}, u32[]{:S(2)}) copy-start(s32[24]{0:T(128)} %param.15) | copy-start | bytes 292
  60.0 8.0 %copy-start.8 = (bf16[512,512]{1,0:T(8,128)(2,1)}, bf16[512,512]{1,0:T(8,128)(2,1)S(1)}, u32[]{:S(2)}) copy-start(bf16[512,512]{1,0:T(8,128)(2,1)S(1)} %collective-permute-done.9.up_other) | copy-start | bytes 1572868
  60.0 0.8 copy-start.12
  68.1 7.8 %collective-permute-start.13 = (f32[384,512]{1,0:T(8,128)}, f32[384,512]{1,0:T(8,128)S(1)}, u32[]{:S(2)}, u32[]{:S(2)}) collective-permute-start(f32[384,512]{1,0:T(8,128)} %get-tuple-element.52), channel_id=1, source_target_pairs={{0,1},{1,0},{2,3},{3,2},{4,5},{5,4},{6,7},{7,6},{8,9},{9,8},{10,11... | collective-permute-start | bytes 2359304 | tf_op jit(solution)/shard_map/ppermute | solution.py:198
  68.1 2.6 %collective-permute-start.11 = (f32[192,128]{1,0:T(8,128)}, f32[192,128]{1,0:T(8,128)S(1)}, u32[]{:S(2)}, u32[]{:S(2)}) collective-permute-start(f32[192,128]{1,0:T(8,128)} %get-tuple-element.51), channel_id=1, source_target_pairs={{0,1},{1,0},{2,3},{3,2},{4,5},{5,4},{6,7},{7,6},{8,9},{9,8},{10,11... | collective-permute-start | bytes 294920 | tf_op jit(solution)/shard_map/ppermute | solution.py:198
  71.7 4.2 %collective-permute-start.12 = (bf16[192,128]{1,0:T(8,128)(2,1)S(1)}, bf16[192,128]{1,0:T(8,128)(2,1)S(1)}, u32[]{:S(2)}, u32[]{:S(2)}) collective-permute-start(bf16[192,128]{1,0:T(8,128)(2,1)S(1)} %add_convert_fusion.4), channel_id=1, source_target_pairs={{0,2},{2,0},{1,3},{3,1},{4,6},{6,4},{5,7},{7,5},{8,10},{10,8},{9,1... | collective-permute-start | bytes 147464 | tf_op jit(solution)/shard_map/ppermute | solution.py:198
  75.9 9.8 %copy-start.7 = (f32[384,512]{1,0:T(8,128)}, f32[384,512]{1,0:T(8,128)S(1)}, u32[]{:S(2)}) copy-start(f32[384,512]{1,0:T(8,128)S(1)} %collective-permute-done.13.received) | copy-start | bytes 2359300
  75.9 6.9 %collective-permute-start.14 = (bf16[192,128]{1,0:T(8,128)(2,1)S(1)}, bf16[192,128]{1,0:T(8,128)(2,1)S(1)}, u32[]{:S(2)}, u32[]{:S(2)}) collective-permute-start(bf16[192,128]{1,0:T(8,128)(2,1)S(1)} %add.217), channel_id=1, source_target_pairs={{0,4},{4,8},{8,12},{12,0},{1,5},{5,9},{9,13},{13,1},{2,6},{6,10},{... | collective-permute-start | bytes 147464 | tf_op jit(solution)/shard_map/ppermute | solution.py:198
  79.5 5.5 %collective-permute-start.15 = (bf16[192,128]{1,0:T(8,128)(2,1)S(1)}, bf16[192,128]{1,0:T(8,128)(2,1)S(1)}, u32[]{:S(2)}, u32[]{:S(2)}) collective-permute-start(bf16[192,128]{1,0:T(8,128)(2,1)S(1)} %add.217), channel_id=1, source_target_pairs={{0,8},{4,12},{8,0},{12,4},{1,9},{5,13},{9,1},{13,5},{2,10},{6,14},... | collective-permute-start | bytes 147464 | tf_op jit(solution)/shard_map/ppermute | solution.py:198
  79.9 5.1 %collective-permute-start.16 = (bf16[192,128]{1,0:T(8,128)(2,1)S(1)}, bf16[192,128]{1,0:T(8,128)(2,1)S(1)}, u32[]{:S(2)}, u32[]{:S(2)}) collective-permute-start(bf16[192,128]{1,0:T(8,128)(2,1)S(1)} %add.217), channel_id=1, source_target_pairs={{0,12},{4,0},{8,4},{12,8},{1,13},{5,1},{9,5},{13,9},{2,14},{6,2},{... | collective-permute-start | bytes 147464 | tf_op jit(solution)/shard_map/ppermute | solution.py:198
  89.3 47.2 %collective-permute-start.18 = (bf16[512,8192]{1,0:T(8,128)(2,1)}, bf16[512,8192]{1,0:T(8,128)(2,1)}, u32[]{:S(2)}, u32[]{:S(2)}) collective-permute-start(bf16[512,8192]{1,0:T(8,128)(2,1)} %refs_2_.3), channel_id=1, source_target_pairs={{0,1},{1,0},{2,3},{3,2},{4,5},{5,4},{6,7},{7,6},{8,9},{9,8},{10,11... | collective-permute-start | bytes 25165832 | tf_op jit(solution)/shard_map/ppermute | solution.py:198
  89.3 18.0 %all-to-all-start.1 = ((bf16[16,24,512]{2,1,0:T(8,128)(2,1)}), bf16[16,24,512]{2,1,0:T(8,128)(2,1)S(1)}, u32[]{:S(2)}, u32[]{:S(2)}) async-start(bf16[16,24,512]{2,1,0:T(8,128)(2,1)} %bitcast.55), calls=%async_computation.1 | async-start | bytes 786432 | tf_op jit(solution)/shard_map/all_to_all | solution.py:316
  134.7 1.7 copy-start.3
  134.7 1.7 collective-permute-start.17
  136.4 0.8 copy-start.6
  140.7 11.6 %collective-permute-start.21 = (bf16[384,512]{1,0:T(8,128)(2,1)}, bf16[384,512]{1,0:T(8,128)(2,1)S(1)}, u32[]{:S(2)}, u32[]{:S(2)}) collective-permute-start(bf16[384,512]{1,0:T(8,128)(2,1)} %shard_map.122), channel_id=1, source_target_pairs={{0,2},{2,0},{1,3},{3,1},{4,6},{6,4},{5,7},{7,5},{8,10},{10,8},{9,1... | collective-permute-start | bytes 1179656 | tf_op jit(solution)/shard_map/ppermute | solution.py:198
  141.3 46.0 %copy-start.1 = (bf16[1,8192,64]{1,2,0:T(8,128)(2,1)S(1)}, bf16[1,8192,64]{1,2,0:T(8,128)(2,1)}, u32[]{:S(2)}) copy-start(bf16[1,8192,64]{1,2,0:T(8,128)(2,1)} %param.18) | copy-start | bytes 3145732
  148.7 12.2 %collective-permute-start.20 = (bf16[384,512]{1,0:T(8,128)(2,1)}, bf16[384,512]{1,0:T(8,128)(2,1)S(1)}, u32[]{:S(2)}, u32[]{:S(2)}) collective-permute-start(bf16[384,512]{1,0:T(8,128)(2,1)} %get-tuple-element.61), channel_id=1, source_target_pairs={{0,2},{2,0},{1,3},{3,1},{4,6},{6,4},{5,7},{7,5},{8,10},{10,8},{9,1... | collective-permute-start | bytes 1179656 | tf_op jit(solution)/shard_map/ppermute | solution.py:198
  153.4 10.9 %collective-permute-start.22 = (bf16[384,512]{1,0:T(8,128)(2,1)S(1)}, bf16[384,512]{1,0:T(8,128)(2,1)S(1)}, u32[]{:S(2)}, u32[]{:S(2)}) collective-permute-start(bf16[384,512]{1,0:T(8,128)(2,1)S(1)} %add_convert_fusion.3), channel_id=1, source_target_pairs={{0,4},{4,8},{1,5},{5,9},{2,6},{6,10},{3,7},{7,11},{16,20},{20,24},... | collective-permute-start | bytes 1179656 | tf_op jit(solution)/shard_map/ppermute | solution.py:243
  156.5 12.9 %collective-permute-start.24 = (bf16[384,512]{1,0:T(8,128)(2,1)}, bf16[384,512]{1,0:T(8,128)(2,1)S(1)}, u32[]{:S(2)}, u32[]{:S(2)}) collective-permute-start(bf16[384,512]{1,0:T(8,128)(2,1)} %get-tuple-element.66), channel_id=1, source_target_pairs={{0,2},{2,0},{1,3},{3,1},{4,6},{6,4},{5,7},{7,5},{8,10},{10,8},{9,1... | collective-permute-start | bytes 1179656 | tf_op jit(solution)/shard_map/ppermute | solution.py:198
  157.1 20.2 %collective-permute-start.19 = (bf16[384,512]{1,0:T(8,128)(2,1)}, bf16[384,512]{1,0:T(8,128)(2,1)S(1)}, u32[]{:S(2)}, u32[]{:S(2)}) collective-permute-start(bf16[384,512]{1,0:T(8,128)(2,1)} %get-tuple-element.58), channel_id=1, source_target_pairs={{0,2},{2,0},{1,3},{3,1},{4,6},{6,4},{5,7},{7,5},{8,10},{10,8},{9,1... | collective-permute-start | bytes 1179656 | tf_op jit(solution)/shard_map/ppermute | solution.py:198
  158.6 10.8 %collective-permute-start.25 = (bf16[384,512]{1,0:T(8,128)(2,1)S(1)}, bf16[384,512]{1,0:T(8,128)(2,1)S(1)}, u32[]{:S(2)}, u32[]{:S(2)}) collective-permute-start(bf16[384,512]{1,0:T(8,128)(2,1)S(1)} %add_convert_fusion.3), channel_id=1, source_target_pairs={{12,8},{8,4},{13,9},{9,5},{14,10},{10,6},{15,11},{11,7},{28,24},{2... | collective-permute-start | bytes 1179656 | tf_op jit(solution)/shard_map/ppermute | solution.py:244
  164.4 15.5 %collective-permute-start.23 = (bf16[384,512]{1,0:T(8,128)(2,1)S(1)}, bf16[384,512]{1,0:T(8,128)(2,1)S(1)}, u32[]{:S(2)}, u32[]{:S(2)}) collective-permute-start(bf16[384,512]{1,0:T(8,128)(2,1)S(1)} %add_convert_fusion.2), channel_id=1, source_target_pairs={{0,4},{4,8},{8,12},{12,0},{1,5},{5,9},{9,13},{13,1},{2,6},{6,10},{... | collective-permute-start | bytes 1179656 | tf_op jit(solution)/shard_map/ppermute | solution.py:198
  170.6 15.8 %collective-permute-start.26 = (bf16[384,512]{1,0:T(8,128)(2,1)S(1)}, bf16[384,512]{1,0:T(8,128)(2,1)S(1)}, u32[]{:S(2)}, u32[]{:S(2)}) collective-permute-start(bf16[384,512]{1,0:T(8,128)(2,1)S(1)} %add_convert_fusion.1), channel_id=1, source_target_pairs={{0,12},{4,0},{8,4},{12,8},{1,13},{5,1},{9,5},{13,9},{2,14},{6,2},{... | collective-permute-start | bytes 1179656 | tf_op jit(solution)/shard_map/ppermute | solution.py:198
